TPU v7x, 128 devices: a whole 4x4x4 slice. The times are simulated.
128 devices in a mesh: gr: 8 (over y_hi, z), gc: 16 (over x, y_lo, core).
Axes of the slice: x: 4, y: 4 (y_hi: 2, y_lo: 2; y = y_hi * 2 + y_lo), z: 4, core: 2. Of those that a mesh axis runs over, the one named last changes fastest.
Arguments:
- items: bfloat16 [16384, 4096], P(('gr', 'gc'))
- position_of: int32 [16384], P(('gr', 'gc')), may hold values from 0 to 16383, as said below
Outputs:
- similarity: bfloat16 [16384, 16384], P('gr', 'gc')
- best_other: float32 [16384], P('gr')
Inputs may be any that keep to these rules, and one draw needn't show every extreme that they name: `position_of`: A permutation. Position p has home device p // 128 in the order gr+gc; the items of device s go to home devices s * 128, s * 128 + 1, ... taken modulo 128, so each device sends at most 1 items to each home device and each home device receives 128.
All inputs are finite; a program needn't handle non-finite values.
Results may differ from a plain program's by a relative error of at most 0.001.
Values may be sent and summed in bfloat16 or wider, within the bound.
No kernel may reach another device: no remote copies, remote signals or barrier semaphores. Data moves between devices by JAX's collectives and lax.ppermute only.
A program may use at most 128 MiB of HBM per device.

v0:
```python
import jax
import jax.numpy as jnp
from jax import lax
from jax.sharding import PartitionSpec as P


def inverse_norm(block):
    wide = block.astype(jnp.float32)
    return 1.0 / jnp.sqrt(jnp.sum(wide * wide, axis=1) + 1e-06)


def per_device(items, position_of):
    count = items.shape[0]
    width = items.shape[1]
    n_rows = lax.axis_size("gr")
    n_cols = lax.axis_size("gc")
    shards = n_rows * n_cols
    slots = (count + shards - 1) // shards
    dest = position_of // count
    earlier = (dest[None, :] == dest[:, None]) & (position_of[None, :] < position_of[:, None])
    rank = jnp.sum(earlier.astype(jnp.int32), axis=1)
    slot = dest * slots + rank
    send = jnp.zeros((shards * slots, width), items.dtype).at[slot].set(items)
    send_pos = jnp.full((shards * slots,), -1, jnp.int32).at[slot].set(position_of)
    arrived, arrived_pos = (
        lax.all_to_all(send, ("gr", "gc"), split_axis=0, concat_axis=0, tiled=True),
        lax.all_to_all(send_pos, ("gr", "gc"), split_axis=0, concat_axis=0, tiled=True),
    )
    target = jnp.where(arrived_pos >= 0, arrived_pos % count, count)
    local = jnp.zeros_like(items).at[target].set(arrived, mode="drop")
    rows = lax.all_gather(local, "gc", axis=0, tiled=True)
    row_inv = inverse_norm(rows)
    piece = lax.all_gather(local, "gr", axis=0, tiled=True)
    product = lax.dot_general(
        rows, piece, (((1,), (1,)), ((), ())), preferred_element_type=jnp.float32
    )
    scaled = product * row_inv[:, None] * inverse_norm(piece)[None, :]
    row_here = lax.axis_index("gr")
    col_here = lax.axis_index("gc")
    row_local = jnp.arange(count * n_cols, dtype=jnp.int32)[:, None]
    col_local = jnp.arange(count * n_rows, dtype=jnp.int32)[None, :]
    itself = (row_local == col_here * count + col_local % count) & (col_local // count == row_here)
    masked = jnp.where(itself, jnp.float32(-2.0), scaled)
    best = lax.pmax(jnp.max(masked, axis=1), "gc")
    return (scaled.astype(jnp.bfloat16), best)


def solution(mesh):
    return jax.shard_map(
        per_device,
        mesh=mesh,
        in_specs=(P(("gr", "gc"), None), P(("gr", "gc"))),
        out_specs=(P("gr", "gc"), P("gr")),
        check_vma=False,
    )
```

profile of v0, /device:TPU:0, one launch (start us, length us, event | category | flops | bytes accessed | tf_op | source)
XLA Modules:
  0.0 335.4 jit_solution(11335868931634280589)
XLA Ops:
  7.2 0.7 and_select_fusion.1
  7.8 0.9 convert_reduce_fusion
  8.7 0.7 compare_select_fusion.1
  9.4 1.1 scatter_custom_fusion
  10.5 0.7 copy.12
  11.3 11.1 %all-to-all-start = ((s32[128,1,1]{2,1,0:T(1,128)}), s32[128,1,1]{2,1,0:T(1,128)S(1)}, u32[]{:S(2)}, u32[]{:S(2)}) async-start(s32[128,1,1]{2,1,0:T(1,128)} %copy.12), calls=%async_computation | async-start | bytes 131072 | tf_op jit(solution)/shard_map/all_to_all | solution.py:27
  22.4 3.0 scatter_custom_fusion.1
  25.4 0.5 broadcast.174
  25.9 1.4 reduce.1
  27.3 1.6 reshape.182
  28.9 2.7 all-to-all-done
  31.6 7.1 %all-to-all-start.1 = ((bf16[128,2,2048]{2,1,0:T(2,128)(2,1)}), bf16[128,2,2048]{2,1,0:T(2,128)(2,1)S(1)}, u32[]{:S(2)}, u32[]{:S(2)}) async-start(bf16[128,2,2048]{2,1,0:T(2,128)(2,1)} %reshape.182), calls=%async_computation.1 | async-start | bytes 2097152 | tf_op jit(solution)/shard_map/all_to_all | solution.py:26
  38.7 0.0 all-gather.5.cloned.1.call-start
  38.7 2.4 reduce
  41.1 16.5 %all-to-all-done.1 = bf16[128,2,2048]{2,1,0:T(2,128)(2,1)S(1)} async-done(((bf16[128,2,2048]{2,1,0:T(2,128)(2,1)}), bf16[128,2,2048]{2,1,0:T(2,128)(2,1)S(1)}, u32[]{:S(2)}, u32[]{:S(2)}) %all-to-all-start.1) | async-done | bytes 1048608 | tf_op jit(solution)/shard_map/all_to_all | solution.py:26
  57.6 1.0 reshape.183
  58.7 4.1 %scatter_custom_fusion.2 = bf16[128,4096]{1,0:T(8,128)(2,1)} fusion(s32[128]{0:T(128)S(1)} %fusion.16, bf16[128,1,4096]{2,1,0:T(2,128)(2,1)S(1)} %reshape.183, bf16[]{:T(256)} %constant.60.clone.1), kind=kCustom, calls=%fused_computation.10 | custom fusion | bytes 3145730 | tf_op jit(solution)/shard_map/scatter | solution.py:30
  62.8 0.0 all-gather.5.cloned.1.call-update
  62.8 0.2 all-gather.3.cloned.1.call-start
  63.0 0.5 all-gather.3.cloned.1.call-update
  63.6 103.0 %all-gather.5.cloned.1.call-done = bf16[1024,4096]{1,0:T(8,128)(2,1)} async-done(((bf16[128,4096]{1,0:T(8,128)(2,1)}), bf16[1024,4096]{1,0:T(8,128)(2,1)}) %all-gather.5.cloned.1.call-update) | async-done | bytes 8388624 | tf_op jit(solution)/shard_map/all_gather | solution.py:33
  166.6 5.1 %multiply_reduce_fusion.1 = f32[1024]{0:T(1024)S(1)} fusion(bf16[1024,4096]{1,0:T(8,128)(2,1)} %all-gather.5.cloned.1.call-done), kind=kLoop, calls=%fused_computation.4 | loop fusion | flops 12581888 | bytes 8392704 | tf_op jit(solution)/shard_map/reduce_sum | solution.py:9
  171.7 86.5 %all-gather.3.cloned.1.call-done = bf16[2048,4096]{1,0:T(8,128)(2,1)} async-done(((bf16[128,4096]{1,0:T(8,128)(2,1)}), bf16[2048,4096]{1,0:T(8,128)(2,1)}) %all-gather.3.cloned.1.call-update) | async-done | bytes 16777232 | tf_op jit(solution)/shard_map/all_gather | solution.py:31
  258.2 0.0 copy-start
  258.2 7.5 %multiply_reduce_fusion = f32[2048]{0:T(1024)S(1)} fusion(bf16[2048,4096]{1,0:T(8,128)(2,1)} %all-gather.3.cloned.1.call-done), kind=kLoop, calls=%fused_computation.3 | loop fusion | flops 25163776 | bytes 16785408 | tf_op jit(solution)/shard_map/reduce_sum | solution.py:9
  265.7 3.1 copy-done
  268.8 22.5 %select_reduce_fusion = (f32[2048]{0:T(1024)S(1)}, bf16[2048,1024]{0,1:T(8,128)(2,1)}) fusion(s32[1024]{0:T(1024)S(1)} %fusion.8, f32[1024]{0:T(1024)S(1)} %add_rsqrt_fusion.1, f32[2048]{0:T(1024)S(1)} %add_rsqrt_fusion, pred[1024]{0:T(1024)(128)(4,1)S(1)} %fusion.10, bf16[2048,4096]{1,0:T(8,128)(2,1)S(1)} %copy-done, ...), kind=kOutput, calls=%fused_computation.5 | convolution fusion | flops 17194547200 | bytes 29385728 | tf_op jit(solution)/shard_map/dot_general | solution.py:34
  291.3 30.9 %pmax.7 = f32[2048]{0:T(1024)} all-reduce(f32[2048]{0:T(1024)S(1)} %get-tuple-element.12), channel_id=1, replica_groups=mesh['gr'=8,'gc'=16] {'gc'}, use_global_device_ids=true, to_apply=%region_7.8 | all-reduce | flops 2048 | bytes 16384 | tf_op jit(solution)/shard_map/pmax | solution.py:44
  322.2 6.4 %copy.14 = bf16[2048,1024]{1,0:T(8,128)(2,1)} copy(bf16[2048,1024]{0,1:T(8,128)(2,1)} %get-tuple-element.13) | data formatting | bytes 8388608
  (5 shorter events, 0.0 us)
Async XLA Ops:
  11.3 20.3 %all-to-all-start = ((s32[128,1,1]{2,1,0:T(1,128)}), s32[128,1,1]{2,1,0:T(1,128)S(1)}, u32[]{:S(2)}, u32[]{:S(2)}) async-start(s32[128,1,1]{2,1,0:T(1,128)} %copy.12), calls=%async_computation | async-start | bytes 131072 | tf_op jit(solution)/shard_map/all_to_all | solution.py:27
  31.6 26.0 %all-to-all-start.1 = ((bf16[128,2,2048]{2,1,0:T(2,128)(2,1)}), bf16[128,2,2048]{2,1,0:T(2,128)(2,1)S(1)}, u32[]{:S(2)}, u32[]{:S(2)}) async-start(bf16[128,2,2048]{2,1,0:T(2,128)(2,1)} %reshape.182), calls=%async_computation.1 | async-start | bytes 2097152 | tf_op jit(solution)/shard_map/all_to_all | solution.py:26
  38.7 127.9 %all-gather.5.cloned.1.call-start = ((), (), s32[]{:S(2)}) async-start(), calls=%async_computation.3 | async-start | bytes 9437184 | tf_op jit(solution)/shard_map/all_gather | solution.py:33
  62.8 195.4 %all-gather.3.cloned.1.call-start = ((), (), s32[]{:S(2)}) async-start(), calls=%async_computation.2 | async-start | bytes 17825792 | tf_op jit(solution)/shard_map/all_gather | solution.py:31
  258.2 10.7 %copy-start = (bf16[2048,4096]{1,0:T(8,128)(2,1)S(1)}, bf16[2048,4096]{1,0:T(8,128)(2,1)}, u32[]{:S(2)}) copy-start(bf16[2048,4096]{1,0:T(8,128)(2,1)} %all-gather.3.cloned.1.call-done) | copy-start | bytes 50331652
Sparse Core Ops, SparseCore 0:
  62.9 103.5 all-gather.4
  168.8 89.2 all-gather.2
where the time goes:
time: 336 us; the launch traced here: 335 us
  waiting for transfers between devices  209 us (62%)
  blocking collectives  30.9 us (9%)
  matrix products  22.5 us (7%)
  local copies, waits for them, and re-layouts  21.6 us (6%)
  other arithmetic  18.6 us (6%)
  starting transfers between devices  18.5 us (6%)
  between operations  14.1 us (4%)
    all_gather x1, waiting for transfers between devices, per_device(): piece = lax.all_gather(local, 'gr', axis=0, tiled=True)  103 us
    all_gather x1, waiting for transfers between devices, per_device(): rows = lax.all_gather(local, 'gc', axis=0, tiled=True)  86.5 us
    pmax x1, blocking collectives, per_device(): best = lax.pmax(jnp.max(masked, axis=1), 'gc')  30.9 us
    dot_general x1, matrix products, per_device(): lax.dot_general(rows, piece, (((1,), (1,)), ((), ())), preferred_element_...  22.5 us
    all_to_all x1, waiting for transfers between devices, per_device(): lax.all_to_all(send, ('gr', 'gc'), split_axis=0, concat_axis=0, tiled=True)  16.5 us
    reduce_sum x2, other arithmetic, inverse_norm(): return 1.0 / jnp.sqrt(jnp.sum(wide * wide, axis=1) + 1e-06)  12.6 us
    unnamed x5, local copies, waits for them, and re-layouts  12.1 us
    all_to_all x1, starting transfers between devices, per_device(): lax.all_to_all(send_pos, ('gr', 'gc'), split_axis=0, concat_axis=0, tiled...  11.1 us
  transfers between devices with their start and end apart: 4, of which 4 were waited for; matrix products, arithmetic and copies ran while one was open for 4% of the time, Pallas kernels for 0%

commit v1 on v0

v1 whole, which is shorter than its diff:
```python
import jax
import jax.numpy as jnp
from jax import lax
from jax.experimental import pallas as pl
from jax.experimental.pallas import tpu as pltpu
from jax.sharding import PartitionSpec as P

AXES = ("gr", "gc")
SIZES = {"yh": 2, "z": 4, "x": 4, "yl": 2, "c": 2}
F32 = jnp.float32
BF16 = jnp.bfloat16
MIB = 1024 * 1024


def coords(d):
    gr, gc = divmod(d, 16)
    return {"yh": gr // 4, "z": gr % 4, "x": gc // 4, "yl": (gc // 2) % 2, "c": gc % 2}


def flat(c):
    return (c["yh"] * 4 + c["z"]) * 16 + c["x"] * 4 + c["yl"] * 2 + c["c"]


def send(value, route):
    pairs = []
    for d in range(128):
        c = coords(d)
        for k, v in route.items():
            step = (1 if c["c"] == 0 else -1) if v == "ring" else v
            c[k] = (c[k] + step) % SIZES[k]
        pairs.append((d, flat(c)))
    return lax.ppermute(value, AXES, pairs)


def pack_kernel(pos_ref, items_ref, out_ref):
    count, width = items_ref.shape
    pos = pos_ref[...]
    dest = lax.broadcasted_iota(jnp.int32, (count, count), 0)
    hit = (pos // count) == dest
    pick = jnp.where(hit, 1.0, 0.0).astype(BF16)
    step = 1024
    for s in range(0, width, step):
        out_ref[:, s : s + step] = jnp.dot(
            pick, items_ref[:, s : s + step], preferred_element_type=F32
        ).astype(BF16)
    slot = jnp.sum(jnp.where(hit, (pos % count).astype(F32), 0.0), axis=1, keepdims=True)
    out_ref[:, width:] = jnp.broadcast_to(slot, (count, 128)).astype(BF16)


def place_kernel(in_ref, out_ref, low_ref, high_ref):
    count, width = out_ref.shape
    slot = in_ref[:, width:].astype(F32)
    lane = lax.broadcasted_iota(jnp.int32, (count, count), 1).astype(F32)
    pick = jnp.where(slot == lane, 1.0, 0.0).astype(BF16)
    step = 1024
    for s in range(0, width, step):
        out_ref[:, s : s + step] = lax.dot_general(
            pick, in_ref[:, s : s + step], (((0,), (0,)), ((), ())), preferred_element_type=F32
        ).astype(BF16)
    low_ref[...] = out_ref[: count // 2, :]
    high_ref[...] = out_ref[count // 2 :, :]


def join_kernel(low_ref, high_ref, out_ref, sems):
    half = low_ref.shape[0]
    copies = [
        pltpu.make_async_copy(src, out_ref.at[pl.ds(half * n, half)], sems.at[n])
        for n, src in enumerate((low_ref, high_ref))
    ]
    for c in copies:
        c.start()
    for c in copies:
        c.wait()


def join(low, high):
    any_spec = pl.BlockSpec(memory_space=pl.ANY)
    return pl.pallas_call(
        join_kernel,
        out_shape=jax.ShapeDtypeStruct((2 * low.shape[0], low.shape[1]), BF16),
        in_specs=[any_spec, any_spec],
        out_specs=pl.BlockSpec(memory_space=pltpu.VMEM),
        scratch_shapes=[pltpu.SemaphoreType.DMA((2,))],
        compiler_params=pltpu.CompilerParams(vmem_limit_bytes=2 * MIB),
    )(low, high)


def inverse_norm(ref, start, rows):
    total = jnp.zeros((rows, 128), F32)
    for s in range(0, ref.shape[1], 128):
        part = ref[start : start + rows, s : s + 128].astype(F32)
        total = total + part * part
    return 1.0 / jnp.sqrt(jnp.sum(total, axis=1, keepdims=True) + 1e-06)


def across(column):
    return jnp.transpose(jnp.broadcast_to(column, (128, 128)))[:1, :]


def make_block_kernel(n_rb, n_cb, fresh_rows, fresh_cols, diagonal, last):
    tile = 512 if fresh_rows else 1024
    per_tile = tile // 128

    def kernel(*refs):
        refs = list(refs)
        where = refs.pop(0)
        n_rows = [refs.pop(0) for _ in range(n_rb if fresh_rows else 2)]
        n_cols = [refs.pop(0) for _ in range(n_cb if fresh_cols else 1)]
        row_inv = None if fresh_rows else [refs.pop(0), refs.pop(0)]
        col_inv = None if fresh_cols else refs.pop(0)
        best_in = None if fresh_rows else [refs.pop(0), refs.pop(0)]
        if not diagonal:
            refs.pop(0)
        out_ref = refs.pop(0)
        final_ref = refs.pop(0) if last else None
        best_out = [refs.pop(0)] if fresh_rows or last else [refs.pop(0), refs.pop(0)]
        rows_v = refs.pop(0) if fresh_rows else None
        row_inv_out = refs.pop(0) if fresh_rows else None
        cols_v = refs.pop(0) if fresh_cols else n_cols[0]
        if fresh_cols:
            col_inv = refs.pop(0)
        row_sem, col_sem, out_sem = refs

        col_loads, row_loads = [], []
        if fresh_cols:
            for n, src in enumerate(n_cols):
                c = pltpu.make_async_copy(src, cols_v.at[pl.ds(128 * n, 128)], col_sem.at[n])
                c.start()
                col_loads.append(c)
        if fresh_rows:
            for n, src in enumerate(n_rows):
                c = pltpu.make_async_copy(src, rows_v.at[pl.ds(128 * n, 128)], row_sem.at[n])
                c.start()
                row_loads.append(c)
        for n, c in enumerate(col_loads):
            c.wait()
            col_inv[:, 128 * n : 128 * n + 128] = jnp.broadcast_to(
                across(inverse_norm(cols_v, 128 * n, 128)), (8, 128)
            )
        stores = []
        n_tiles = n_rb // per_tile
        for t in range(n_tiles):
            if fresh_rows:
                for c in row_loads[t * per_tile : (t + 1) * per_tile]:
                    c.wait()
                source, at = rows_v, t * tile
                part, at_r = None, t * tile
            else:
                part, at_r = divmod(t * tile, 1024)
                source, at = n_rows[part], at_r
            product = lax.dot_general(
                source[at : at + tile, :],
                cols_v[...],
                (((1,), (1,)), ((), ())),
                preferred_element_type=F32,
            )
            for k in range(per_tile):
                r = t * per_tile + k
                span = slice(at_r + 128 * k, at_r + 128 * k + 128)
                if fresh_rows:
                    inv = jnp.broadcast_to(
                        inverse_norm(rows_v, at_r + 128 * k, 128), (128, 128)
                    )
                    row_inv_out[span, :] = inv
                    top = None
                else:
                    inv = row_inv[part][span, :]
                    top = best_in[part][span, :]
                a = where[r]
                here = pl.ds(pl.multiple_of(a * 128, 128), 128)
                for b in range(n_cb):
                    lanes = slice(128 * b, 128 * b + 128)
                    scaled = product[128 * k : 128 * k + 128, lanes] * inv * col_inv[:1, lanes]
                    out_ref[
                        here, pl.ds(pl.multiple_of(where[n_rb + b] * 128, 128), 128)
                    ] = scaled.astype(BF16)
                    if diagonal and r == 0 and b == 0:
                        lane = lax.broadcasted_iota(jnp.int32, scaled.shape, 1)
                        sub = lax.broadcasted_iota(jnp.int32, scaled.shape, 0)
                        scaled = jnp.where(lane == sub, -2.0, scaled)
                    top = scaled if top is None else jnp.maximum(top, scaled)
                if last:
                    best_out[0][pl.ds(a, 1), :] = across(jnp.max(top, axis=1, keepdims=True))
                    c = pltpu.make_async_copy(
                        out_ref.at[here, :], final_ref.at[here, :], out_sem.at[r]
                    )
                    c.start()
                    stores.append(c)
                elif fresh_rows:
                    best_out[0][span, :] = top
                else:
                    best_out[part][span, :] = top
        for c in stores:
            c.wait()

    return kernel


def block_call(where, rows, cols, out, row_inv=None, col_inv=None, best=None, last=False):
    fresh_rows, fresh_cols = row_inv is None, col_inv is None
    n_rb = len(rows) if fresh_rows else 16
    n_cb = len(cols) if fresh_cols else cols[0].shape[0] // 128
    width = rows[0].shape[1]
    any_spec = pl.BlockSpec(memory_space=pl.ANY)
    vmem_spec = pl.BlockSpec(memory_space=pltpu.VMEM)
    args = [where, *rows, *cols]
    in_specs = [pl.BlockSpec(memory_space=pltpu.SMEM)]
    in_specs += [any_spec if fresh_rows else vmem_spec] * len(rows)
    in_specs += [any_spec if fresh_cols else vmem_spec] * len(cols)
    for extra in (row_inv, col_inv, best):
        if extra is not None:
            extra = extra if isinstance(extra, (list, tuple)) else [extra]
            args += extra
            in_specs += [vmem_spec] * len(extra)
    aliases = {}
    if out is not None:
        args.append(out)
        in_specs.append(vmem_spec)
        aliases = {len(args) - 1: 0}
    out_shape = [jax.ShapeDtypeStruct((2048, 1024), BF16)]
    if last:
        out_shape.append(jax.ShapeDtypeStruct((2048, 1024), BF16))
        out_shape.append(jax.ShapeDtypeStruct((16, 128), F32))
    else:
        out_shape += [jax.ShapeDtypeStruct((1024, 128), F32)] * (1 if fresh_rows else 2)
    if fresh_rows:
        out_shape.append(jax.ShapeDtypeStruct((128 * n_rb, width), BF16))
        out_shape.append(jax.ShapeDtypeStruct((128 * n_rb, 128), F32))
    if fresh_cols:
        out_shape.append(jax.ShapeDtypeStruct((128 * n_cb, width), BF16))
        out_shape.append(jax.ShapeDtypeStruct((8, 128 * n_cb), F32))
    return pl.pallas_call(
        make_block_kernel(n_rb, n_cb, fresh_rows, fresh_cols, out is None, last),
        out_shape=out_shape,
        in_specs=in_specs,
        out_specs=[any_spec if last and n == 1 else vmem_spec for n in range(len(out_shape))],
        input_output_aliases=aliases,
        scratch_shapes=[
            pltpu.SemaphoreType.DMA((n_rb,)),
            pltpu.SemaphoreType.DMA((n_cb,)),
            pltpu.SemaphoreType.DMA((n_rb,)),
        ],
        compiler_params=pltpu.CompilerParams(vmem_limit_bytes=VMEM_LIMIT),
        cost_estimate=pl.CostEstimate(
            flops=2 * n_rb * n_cb * 128 * 128 * width,
            bytes_accessed=2 * n_rb * n_cb * 128 * 128,
            transcendentals=0,
        ),
    )(*args)


VMEM_LIMIT = 12 * MIB


def tied(value, *others):
    return lax.optimization_barrier((value,) + others)[0]


def per_device(items, position_of):
    count, width = items.shape
    vmem_spec = pl.BlockSpec(memory_space=pltpu.VMEM)
    packed = pl.pallas_call(
        pack_kernel,
        out_shape=jax.ShapeDtypeStruct((count, width + 128), BF16),
        in_specs=[vmem_spec, vmem_spec],
        out_specs=vmem_spec,
    )(position_of.reshape(1, count), items)
    gr, gc = lax.axis_index("gr"), lax.axis_index("gc")
    yh, z = gr // 4, gr % 4
    x, yl, core = gc // 4, (gc // 2) % 2, gc % 2
    ring = 1 - 2 * core

    def row_at(dx=0, dy=0, dc=0):
        return ((x + dx + 4) % 4) * 4 + ((yl + dy) % 2) * 2 + (core + dc) % 2

    def col_at(dy=0, dz=0):
        return ((yh + dy) % 2) * 4 + (z + dz + 4) % 4

    rows_at_1 = [
        row_at(), row_at(dc=1), row_at(-ring), row_at(-ring, dc=1),
        row_at(ring, dc=1), row_at(ring), row_at(dy=1), row_at(dy=1, dc=1),
    ]
    rows_at_2 = [
        row_at(-ring, 1), row_at(-ring, 1, 1), row_at(ring, 1, 1), row_at(ring, 1),
        row_at(2), row_at(2, dc=1), row_at(2, 1), row_at(2, 1, 1),
    ]
    cols_at_1 = [col_at(), col_at(dz=-ring), col_at(dz=ring), col_at(dz=2)]
    cols_at_2 = [col_at(1, -ring), col_at(1, ring)]
    cols_at_3 = [col_at(1), col_at(1, 2)]
    places = jnp.stack(
        rows_at_1 + cols_at_1 + rows_at_2 + cols_at_1
        + rows_at_1 + rows_at_2 + cols_at_2
        + rows_at_1 + rows_at_2 + cols_at_3
    ).astype(jnp.int32)
    where_1, where_2, where_3, where_4 = (
        places[:12], places[12:24], places[24:42], places[42:60]
    )
    packed, where_1, where_2, where_3, where_4 = lax.optimization_barrier(
        (packed, where_1, where_2, where_3, where_4)
    )
    arrived = lax.all_to_all(packed, AXES, split_axis=0, concat_axis=0, tiled=True)
    own, own_low, own_high = pl.pallas_call(
        place_kernel,
        out_shape=[
            jax.ShapeDtypeStruct((count, width), BF16),
            jax.ShapeDtypeStruct((count // 2, width), BF16),
            jax.ShapeDtypeStruct((count // 2, width), BF16),
        ],
        in_specs=[vmem_spec],
        out_specs=[vmem_spec] * 3,
    )(arrived)

    cross, up_x, up_z = {"c": 1}, {"x": "ring"}, {"z": "ring"}
    pair_low = send(own_low, {"yl": 1})
    pair_high = send(tied(own_high, pair_low), {"yl": 1})
    far_low = send(pair_low, {"yh": 1, "yl": 1})
    far_high = send(pair_high, {"yh": 1, "yl": 1})
    pair, far = join(pair_low, pair_high), join(far_low, far_high)
    own_c = send(own, cross)
    x_a, z_a = send(own, up_x), send(own, up_z)
    x_b, z_b = send(own_c, up_x), send(own_c, up_z)
    x_2, z_2 = send(x_a, up_x), send(z_a, up_z)
    pair_c, x_a_c, x_b_c, z_b_c = (send(v, cross) for v in (pair, x_a, x_b, z_b))
    p_a, p_b = send(pair, up_x), send(pair_c, up_x)
    out, best_1, rows_1, inv_1, cols_1, col_inv_1 = block_call(
        tied(where_1, far),
        [own, own_c, x_a, x_b, x_a_c, x_b_c, pair, pair_c],
        [own, z_a, z_b_c, z_2],
        None,
    )
    far_c = send(far, cross)
    f_a, f_b = send(far, up_z), send(tied(far_c, best_1), up_z)
    p_2 = send(x_2, {"yl": 1})
    p_a_c, p_b_c, x_2_c, p_2_c = (send(v, cross) for v in (p_a, p_b, x_2, p_2))
    out, best_2, rows_2, inv_2 = block_call(
        where_2,
        [p_a, p_b, p_a_c, p_b_c, x_2, x_2_c, p_2, p_2_c],
        [cols_1],
        out,
        col_inv=col_inv_1,
    )
    f_b_c = send(f_b, cross)
    f_2 = send(f_a, up_z)
    out, best_1, best_2, _, _ = block_call(
        where_3, [rows_1, rows_2], [f_a, f_b_c], out, row_inv=[inv_1, inv_2], best=[best_1, best_2]
    )
    _, out, best, _, _ = block_call(
        where_4,
        [rows_1, rows_2],
        [far, f_2],
        out,
        row_inv=[inv_1, inv_2],
        best=[best_1, best_2],
        last=True,
    )

    best = jnp.maximum(best, send(best, cross))
    best = jnp.maximum(best, send(best, {"yl": 1}))
    best = jnp.maximum(
        jnp.maximum(best, send(best, {"x": 2})),
        jnp.maximum(send(best, {"x": 1}), send(best, {"x": -1})),
    )
    return out, best.reshape(-1)


def solution(mesh):
    return jax.shard_map(
        per_device,
        mesh=mesh,
        in_specs=(P(("gr", "gc"), None), P(("gr", "gc"))),
        out_specs=(P("gr", "gc"), P("gr")),
        check_vma=False,
    )
```

time: 336 us -> 171 us (0.51)
  waiting for transfers between devices: 209 us -> 71.5 us
  Pallas kernels: 0 us -> 39.1 us
  matrix products: 22.5 us -> 0 us
  local copies, waits for them, and re-layouts: 21.6 us -> 3.98 us
  other arithmetic: 18.6 us -> 3.24 us
  between operations: 14.1 us -> 1.09 us
    all_gather x2 -> x0, waiting for transfers between devices: 190 us -> none  [the longest x1 103 us: per_device(): piece = lax.all_gather(local, 'gr', axis=0, tiled=True)]
    ppermute x0 -> x32, waiting for transfers between devices: none -> 71.5 us  [send(): return lax.ppermute(value, AXES, pairs)]
    pallas_call x0 -> x8, Pallas kernels: none -> 39.1 us  [the longest x4 33.3 us: block_call(): pl.pallas_call(make_block_kernel(n_rb, n_cb, fresh_rows, fresh_cols, out...]
    pmax x1 -> x0, blocking collectives: 30.9 us -> none  [per_device(): best = lax.pmax(jnp.max(masked, axis=1), 'gc')]
    all_to_all x0 -> x1, blocking collectives: none -> 30.6 us  [per_device(): lax.all_to_all(packed, AXES, split_axis=0, concat_axis=0, tiled=True)]
    dot_general x1 -> x0, matrix products: 22.5 us -> none  [per_device(): lax.dot_general(rows, piece, (((1,), (1,)), ((), ())), preferred_element_...]
    ppermute x0 -> x32, starting transfers between devices: none -> 20.4 us  [send(): return lax.ppermute(value, AXES, pairs)]
    all_to_all x2 -> x0, waiting for transfers between devices: 19.2 us -> none  [the longest x1 16.5 us: per_device(): lax.all_to_all(send, ('gr', 'gc'), split_axis=0, concat_axis=0, tiled=True)]
  transfers between devices with their start and end apart: 4 -> 32, of which waited for: 4 -> 16; matrix products, arithmetic and copies ran while one was open for 4% -> 0% of each run, Pallas kernels for 0% -> 14%
where the time goes in v1:
time: 171 us; the launch traced here: 170 us
  waiting for transfers between devices  71.5 us (42%)
  Pallas kernels  39.1 us (23%)
  blocking collectives  30.6 us (18%)
  starting transfers between devices  20.4 us (12%)
  local copies, waits for them, and re-layouts  3.98 us (2%)
  other arithmetic  3.24 us (2%)
    ppermute x32, waiting for transfers between devices, send(): return lax.ppermute(value, AXES, pairs)  71.5 us
    pallas_call x4, Pallas kernels, block_call(): pl.pallas_call(make_block_kernel(n_rb, n_cb, fresh_rows, fresh_cols, out...  33.3 us
    all_to_all x1, blocking collectives, per_device(): lax.all_to_all(packed, AXES, split_axis=0, concat_axis=0, tiled=True)  30.6 us
    ppermute x32, starting transfers between devices, send(): return lax.ppermute(value, AXES, pairs)  20.4 us
  transfers between devices with their start and end apart: 32, of which 16 were waited for; matrix products, arithmetic and copies ran while one was open for 0% of the time, Pallas kernels for 14%

profile of v1, /device:TPU:0, one launch (start us, length us, event | category | flops | bytes accessed | tf_op | source)
XLA Modules:
  0.0 170.0 jit_solution(5934101054027794897)
XLA Ops:
  1.3 2.6 %shard_map.41 = bf16[128,4224]{1,0:T(8,128)(2,1)} custom-call(s32[1,128]{1,0:T(1,128)} %bitcast.33, bf16[128,4096]{1,0:T(8,128)(2,1)} %items_ref.1), custom_call_target="tpu_custom_call" | custom-call | tf_op jit(solution)/shard_map/pallas_call | solution.py:262
  4.5 2.6 %reduce = bf16[128,4224]{1,0:T(8,128)(2,1)S(1)} reduce(bf16[128,1,4224]{2,0,1:T(8,128)(2,1)} %bitcast.31, bf16[]{:T(256)} %broadcast.20), dimensions={1}, to_apply=%copy.8.reduce_sub_computation | reduce | bytes 2162690 | tf_op jit(solution)/shard_map/all_to_all | solution.py:301
  7.9 30.6 %all_to_all.11 = bf16[128,2,2112]{2,1,0:T(2,128)(2,1)S(1)} all-to-all(bf16[128,2,2112]{2,1,0:T(2,128)(2,1)S(1)} %reshape.14), channel_id=1, replica_groups=mesh['gr'=8,'gc'=16] {'gr','gc'}, dimensions={0} | all-to-all | bytes 2162688 | tf_op jit(solution)/shard_map/all_to_all | solution.py:301
  38.5 1.2 reshape.15
  39.7 1.1 copy.11
  40.8 3.0 %shard_map.42 = (bf16[128,4096]{1,0:T(8,128)(2,1)}, bf16[64,4096]{1,0:T(8,128)(2,1)}, bf16[64,4096]{1,0:T(8,128)(2,1)}) custom-call(bf16[128,4224]{1,0:T(8,128)(2,1)} %bitcast.32), custom_call_target="tpu_custom_call" | custom-call | tf_op jit(solution)/shard_map/pallas_call | solution.py:302
  44.8 12.2 %collective-permute-done.low_ref = bf16[64,4096]{1,0:T(8,128)(2,1)S(1)} collective-permute-done((bf16[64,4096]{1,0:T(8,128)(2,1)}, bf16[64,4096]{1,0:T(8,128)(2,1)S(1)}, u32[]{:S(2)}, u32[]{:S(2)}) %collective-permute-start) | collective-permute-done | bytes 524320 | tf_op jit(solution)/shard_map/ppermute | solution.py:32
  57.5 1.6 collective-permute-start.1
  59.1 10.3 %collective-permute-done.2.high_ref = bf16[64,4096]{1,0:T(8,128)(2,1)S(1)} collective-permute-done((bf16[64,4096]{1,0:T(8,128)(2,1)}, bf16[64,4096]{1,0:T(8,128)(2,1)S(1)}, u32[]{:S(2)}, u32[]{:S(2)}) %collective-permute-start.2) | collective-permute-done | bytes 524320 | tf_op jit(solution)/shard_map/ppermute | solution.py:32
  69.5 2.1 %collective-permute-start.11 = (bf16[128,4096]{1,0:T(8,128)(2,1)S(1)}, bf16[128,4096]{1,0:T(8,128)(2,1)S(1)}, u32[]{:S(2)}, u32[]{:S(2)}) collective-permute-start(bf16[128,4096]{1,0:T(8,128)(2,1)S(1)} %collective-permute-done.4.refs_2_), channel_id=1, source_target_pairs={{0,16},{1,49},{2,18},{3,51},{4,20},{5,53},{6,22},{7,55},{8,24},{9,... | collective-permute-start | bytes 3145736 | tf_op jit(solution)/shard_map/ppermute | solution.py:32
  73.0 1.1 collective-permute-start.13
  74.1 13.8 %collective-permute-done.3.high_ref = bf16[64,4096]{1,0:T(8,128)(2,1)S(1)} collective-permute-done((bf16[64,4096]{1,0:T(8,128)(2,1)S(1)}, bf16[64,4096]{1,0:T(8,128)(2,1)S(1)}, u32[]{:S(2)}, u32[]{:S(2)}) %collective-permute-start.3) | collective-permute-done | bytes 524320 | tf_op jit(solution)/shard_map/ppermute | solution.py:32
  88.5 1.0 collective-permute-start.12
  89.7 7.2 %collective-permute-done.13.refs_12_ = bf16[128,4096]{1,0:T(8,128)(2,1)S(1)} collective-permute-done((bf16[128,4096]{1,0:T(8,128)(2,1)S(1)}, bf16[128,4096]{1,0:T(8,128)(2,1)S(1)}, u32[]{:S(2)}, u32[]{:S(2)}) %collective-permute-start.13) | collective-permute-done | bytes 1048608 | tf_op jit(solution)/shard_map/ppermute | solution.py:32
  96.9 1.9 %collective-permute-start.14 = (bf16[128,4096]{1,0:T(8,128)(2,1)S(1)}, bf16[128,4096]{1,0:T(8,128)(2,1)S(1)}, u32[]{:S(2)}, u32[]{:S(2)}) collective-permute-start(bf16[128,4096]{1,0:T(8,128)(2,1)S(1)} %shard_map.44.refs_7_), channel_id=1, source_target_pairs={{0,4},{1,13},{2,6},{3,15},{4,8},{5,1},{6,10},{7,3},{8,12},{9,5},{1... | collective-permute-start | bytes 3145736 | tf_op jit(solution)/shard_map/ppermute | solution.py:32
  98.8 5.7 %collective-permute-done.18.refs_5_ = bf16[128,4096]{1,0:T(8,128)(2,1)S(1)} collective-permute-done((bf16[128,4096]{1,0:T(8,128)(2,1)S(1)}, bf16[128,4096]{1,0:T(8,128)(2,1)S(1)}, u32[]{:S(2)}, u32[]{:S(2)}) %collective-permute-start.18) | collective-permute-done | bytes 1048608 | tf_op jit(solution)/shard_map/ppermute | solution.py:32
  104.5 1.6 collective-permute-start.22
  106.4 9.2 %shard_map.45 = (bf16[2048,1024]{1,0:T(8,128)(2,1)S(1)}, f32[1024,128]{1,0:T(8,128)S(1)}, bf16[1024,4096]{1,0:T(8,128)(2,1)S(1)}, f32[1024,128]{1,0:T(8,128)S(1)...) custom-call(s32[12]{0:T(128)S(1)} %stack.130.refs_0_, bf16[128,4096]{1,0:T(8,128)(2,1)S(1)} %copy-done, ...), custom_call_target="tpu_custom_call" | custom-call | flops 4294967296 | bytes 1048576 | tf_op jit(solution)/shard_map/pallas_call | solution.py:232
  115.8 4.7 %collective-permute-done.22.refs_3_ = bf16[128,4096]{1,0:T(8,128)(2,1)S(1)} collective-permute-done((bf16[128,4096]{1,0:T(8,128)(2,1)S(1)}, bf16[128,4096]{1,0:T(8,128)(2,1)S(1)}, u32[]{:S(2)}, u32[]{:S(2)}) %collective-permute-start.22) | collective-permute-done | bytes 1048608 | tf_op jit(solution)/shard_map/ppermute | solution.py:32
  120.5 6.5 %collective-permute-done.15.refs_2_ = bf16[128,4096]{1,0:T(8,128)(2,1)S(1)} collective-permute-done((bf16[128,4096]{1,0:T(8,128)(2,1)S(1)}, bf16[128,4096]{1,0:T(8,128)(2,1)S(1)}, u32[]{:S(2)}, u32[]{:S(2)}) %collective-permute-start.15) | collective-permute-done | bytes 1048608 | tf_op jit(solution)/shard_map/ppermute | solution.py:32
  127.0 2.5 %collective-permute-done.20.refs_7_ = bf16[128,4096]{1,0:T(8,128)(2,1)S(1)} collective-permute-done((bf16[128,4096]{1,0:T(8,128)(2,1)S(1)}, bf16[128,4096]{1,0:T(8,128)(2,1)S(1)}, u32[]{:S(2)}, u32[]{:S(2)}) %collective-permute-start.20) | collective-permute-done | bytes 1048608 | tf_op jit(solution)/shard_map/ppermute | solution.py:32
  129.5 2.2 %collective-permute-done.25 = bf16[128,4096]{1,0:T(8,128)(2,1)S(1)} collective-permute-done((bf16[128,4096]{1,0:T(8,128)(2,1)S(1)}, bf16[128,4096]{1,0:T(8,128)(2,1)S(1)}, u32[]{:S(2)}, u32[]{:S(2)}) %collective-permute-start.25) | collective-permute-done | bytes 1048608 | tf_op jit(solution)/shard_map/ppermute | solution.py:32
  132.2 7.5 %shard_map.46 = (bf16[2048,1024]{1,0:T(8,128)(2,1)S(1)}, f32[1024,128]{1,0:T(8,128)S(1)}, bf16[1024,4096]{1,0:T(8,128)(2,1)S(1)}, f32[1024,128]{1,0:T(8,128)S(1)}) custom-call(s32[12]{0:T(128)S(1)} %stack.139.refs_0_, bf16[128,4096]{1,0:T(8,128)(2,1)S(1)} %collective-permute-done.14.refs_1_, ...), custom_call_target="tpu_custom_call", output_to_operand_aliasing={{0}: (11, {})} | custom-call | flops 4294967296 | bytes 1048576 | tf_op jit(solution)/shard_map/pallas_call | solution.py:232
  139.7 7.3 %shard_map.47 = (bf16[2048,1024]{1,0:T(8,128)(2,1)S(1)}, f32[1024,128]{1,0:T(8,128)S(1)}, f32[1024,128]{1,0:T(8,128)S(1)}, bf16[256,4096]{1,0:T(8,128)(2,1)}, f32[8,256]{1,0:T(8,128)}) custom-call(s32[18]{0:T(128)S(1)} %stack.142.refs_0_, bf16[1024,4096]{1,0:T(8,128)(2,1)S(1)} %get-tuple-element.36.refs_1_, ...), custom_call_target="tpu_custom_call", output_to_operand_aliasing={{0}: (9, {})} | custom-call | flops 4294967296 | bytes 1048576 | tf_op jit(solution)/shard_map/pallas_call | solution.py:232
  147.8 9.3 %shard_map.48 = (bf16[2048,1024]{1,0:T(8,128)(2,1)S(1)}, bf16[2048,1024]{1,0:T(8,128)(2,1)}, f32[16,128]{1,0:T(8,128)S(1)}, bf16[256,4096]{1,0:T(8,128)(2,1)}, f32[8,256]{1,0:T(8,128)}) custom-call(s32[18]{0:T(128)S(1)} %stack.145.refs_0_, bf16[1024,4096]{1,0:T(8,128)(2,1)S(1)} %get-tuple-element.36.refs_1_, ...), custom_call_target="tpu_custom_call", output_to_operand_aliasing={{0}: (9, {})} | custom-call | flops 4294967296 | bytes 1048576 | tf_op jit(solution)/shard_map/pallas_call | solution.py:232
  157.2 1.2 collective-permute-done.27
  158.3 1.9 %collective-permute-start.28 = (f32[16,128]{1,0:T(8,128)S(1)}, f32[16,128]{1,0:T(8,128)S(1)}, u32[]{:S(2)}, u32[]{:S(2)}) collective-permute-start(f32[16,128]{1,0:T(8,128)S(1)} %max.15), channel_id=1, source_target_pairs={{0,2},{1,3},{2,0},{3,1},{4,6},{5,7},{6,4},{7,5},{8,10},{9,11},{10,... | collective-permute-start | bytes 24584 | tf_op jit(solution)/shard_map/ppermute | solution.py:32
  160.2 1.8 %collective-permute-done.28 = f32[16,128]{1,0:T(8,128)S(1)} collective-permute-done((f32[16,128]{1,0:T(8,128)S(1)}, f32[16,128]{1,0:T(8,128)S(1)}, u32[]{:S(2)}, u32[]{:S(2)}) %collective-permute-start.28) | collective-permute-done | bytes 8224 | tf_op jit(solution)/shard_map/ppermute | solution.py:32
  162.0 1.6 collective-permute-start.29
  163.5 2.2 %collective-permute-start.30 = (f32[16,128]{1,0:T(8,128)S(1)}, f32[16,128]{1,0:T(8,128)S(1)}, u32[]{:S(2)}, u32[]{:S(2)}) collective-permute-start(f32[16,128]{1,0:T(8,128)S(1)} %max.16), channel_id=1, source_target_pairs={{0,4},{1,5},{2,6},{3,7},{4,8},{5,9},{6,10},{7,11},{8,12},{9,13},{1... | collective-permute-start | bytes 24584 | tf_op jit(solution)/shard_map/ppermute | solution.py:32
  165.7 1.1 collective-permute-start.31
  167.1 1.3 collective-permute-done.30
  (55 shorter events, 9.2 us)
Async XLA Ops:
  43.8 13.2 %collective-permute-start = (bf16[64,4096]{1,0:T(8,128)(2,1)}, bf16[64,4096]{1,0:T(8,128)(2,1)S(1)}, u32[]{:S(2)}, u32[]{:S(2)}) collective-permute-start(bf16[64,4096]{1,0:T(8,128)(2,1)} %get-tuple-element.31), channel_id=1, source_target_pairs={{0,2},{1,3},{2,0},{3,1},{4,6},{5,7},{6,4},{7,5},{8,10},{9,11},{10,... | collective-permute-start | bytes 1572872 | tf_op jit(solution)/shard_map/ppermute | solution.py:32
  44.3 25.2 %collective-permute-start.4 = (bf16[128,4096]{1,0:T(8,128)(2,1)}, bf16[128,4096]{1,0:T(8,128)(2,1)S(1)}, u32[]{:S(2)}, u32[]{:S(2)}) collective-permute-start(bf16[128,4096]{1,0:T(8,128)(2,1)} %get-tuple-element.35.refs_1_.refs_9_), channel_id=1, source_target_pairs={{0,1},{1,0},{2,3},{3,2},{4,5},{5,4},{6,7},{7,6},{8,9},{9,8},{10,11... | collective-permute-start | bytes 3145736 | tf_op jit(solution)/shard_map/ppermute | solution.py:32
  44.3 27.4 %collective-permute-start.10 = (bf16[128,4096]{1,0:T(8,128)(2,1)}, bf16[128,4096]{1,0:T(8,128)(2,1)S(1)}, u32[]{:S(2)}, u32[]{:S(2)}) collective-permute-start(bf16[128,4096]{1,0:T(8,128)(2,1)} %get-tuple-element.35.refs_1_.refs_9_), channel_id=1, source_target_pairs={{0,16},{1,49},{2,18},{3,51},{4,20},{5,53},{6,22},{7,55},{8,24},{9,... | collective-permute-start | bytes 3145736 | tf_op jit(solution)/shard_map/ppermute | solution.py:32
  44.3 28.0 %collective-permute-start.5 = (bf16[128,4096]{1,0:T(8,128)(2,1)}, bf16[128,4096]{1,0:T(8,128)(2,1)S(1)}, u32[]{:S(2)}, u32[]{:S(2)}) collective-permute-start(bf16[128,4096]{1,0:T(8,128)(2,1)} %get-tuple-element.35.refs_1_.refs_9_), channel_id=1, source_target_pairs={{0,4},{1,13},{2,6},{3,15},{4,8},{5,1},{6,10},{7,3},{8,12},{9,5},{1... | collective-permute-start | bytes 3145736 | tf_op jit(solution)/shard_map/ppermute | solution.py:32
  57.0 12.3 %collective-permute-start.2 = (bf16[64,4096]{1,0:T(8,128)(2,1)}, bf16[64,4096]{1,0:T(8,128)(2,1)S(1)}, u32[]{:S(2)}, u32[]{:S(2)}) collective-permute-start(bf16[64,4096]{1,0:T(8,128)(2,1)} %get-tuple-element.33), channel_id=1, source_target_pairs={{0,2},{1,3},{2,0},{3,1},{4,6},{5,7},{6,4},{7,5},{8,10},{9,11},{10,... | collective-permute-start | bytes 1572872 | tf_op jit(solution)/shard_map/ppermute | solution.py:32
  57.5 15.6 %collective-permute-start.1 = (bf16[64,4096]{1,0:T(8,128)(2,1)S(1)}, bf16[64,4096]{1,0:T(8,128)(2,1)S(1)}, u32[]{:S(2)}, u32[]{:S(2)}) collective-permute-start(bf16[64,4096]{1,0:T(8,128)(2,1)S(1)} %collective-permute-done.low_ref), channel_id=1, source_target_pairs={{0,66},{1,67},{2,64},{3,65},{4,70},{5,71},{6,68},{7,69},{8,74},{9,... | collective-permute-start | bytes 1572872 | tf_op jit(solution)/shard_map/ppermute | solution.py:32
  69.4 19.0 %collective-permute-start.9 = (bf16[128,4096]{1,0:T(8,128)(2,1)S(1)}, bf16[128,4096]{1,0:T(8,128)(2,1)S(1)}, u32[]{:S(2)}, u32[]{:S(2)}) collective-permute-start(bf16[128,4096]{1,0:T(8,128)(2,1)S(1)} %shard_map.44.refs_7_), channel_id=1, source_target_pairs={{0,1},{1,0},{2,3},{3,2},{4,5},{5,4},{6,7},{7,6},{8,9},{9,8},{10,11... | collective-permute-start | bytes 3145736 | tf_op jit(solution)/shard_map/ppermute | solution.py:32
  69.5 19.0 %collective-permute-start.11 = (bf16[128,4096]{1,0:T(8,128)(2,1)S(1)}, bf16[128,4096]{1,0:T(8,128)(2,1)S(1)}, u32[]{:S(2)}, u32[]{:S(2)}) collective-permute-start(bf16[128,4096]{1,0:T(8,128)(2,1)S(1)} %collective-permute-done.4.refs_2_), channel_id=1, source_target_pairs={{0,16},{1,49},{2,18},{3,51},{4,20},{5,53},{6,22},{7,55},{8,24},{9,... | collective-permute-start | bytes 3145736 | tf_op jit(solution)/shard_map/ppermute | solution.py:32
  71.7 17.8 %collective-permute-start.6 = (bf16[128,4096]{1,0:T(8,128)(2,1)S(1)}, bf16[128,4096]{1,0:T(8,128)(2,1)S(1)}, u32[]{:S(2)}, u32[]{:S(2)}) collective-permute-start(bf16[128,4096]{1,0:T(8,128)(2,1)S(1)} %collective-permute-done.4.refs_2_), channel_id=1, source_target_pairs={{0,4},{1,13},{2,6},{3,15},{4,8},{5,1},{6,10},{7,3},{8,12},{9,5},{1... | collective-permute-start | bytes 3145736 | tf_op jit(solution)/shard_map/ppermute | solution.py:32
  72.4 15.6 %collective-permute-start.3 = (bf16[64,4096]{1,0:T(8,128)(2,1)S(1)}, bf16[64,4096]{1,0:T(8,128)(2,1)S(1)}, u32[]{:S(2)}, u32[]{:S(2)}) collective-permute-start(bf16[64,4096]{1,0:T(8,128)(2,1)S(1)} %collective-permute-done.2.high_ref), channel_id=1, source_target_pairs={{0,66},{1,67},{2,64},{3,65},{4,70},{5,71},{6,68},{7,69},{8,74},{9,... | collective-permute-start | bytes 1572872 | tf_op jit(solution)/shard_map/ppermute | solution.py:32
  73.0 23.8 %collective-permute-start.13 = (bf16[128,4096]{1,0:T(8,128)(2,1)S(1)}, bf16[128,4096]{1,0:T(8,128)(2,1)S(1)}, u32[]{:S(2)}, u32[]{:S(2)}) collective-permute-start(bf16[128,4096]{1,0:T(8,128)(2,1)S(1)} %collective-permute-done.10.refs_10_), channel_id=1, source_target_pairs={{0,16},{1,49},{2,18},{3,51},{4,20},{5,53},{6,22},{7,55},{8,24},{9,... | collective-permute-start | bytes 3145736 | tf_op jit(solution)/shard_map/ppermute | solution.py:32
  87.9 8.9 %collective-permute-start.7 = (bf16[128,4096]{1,0:T(8,128)(2,1)S(1)}, bf16[128,4096]{1,0:T(8,128)(2,1)S(1)}, u32[]{:S(2)}, u32[]{:S(2)}) collective-permute-start(bf16[128,4096]{1,0:T(8,128)(2,1)S(1)} %collective-permute-done.5.refs_3_), channel_id=1, source_target_pairs={{0,1},{1,0},{2,3},{3,2},{4,5},{5,4},{6,7},{7,6},{8,9},{9,8},{10,11... | collective-permute-start | bytes 3145736 | tf_op jit(solution)/shard_map/ppermute | solution.py:32
  88.5 16.0 %collective-permute-start.18 = (bf16[128,4096]{1,0:T(8,128)(2,1)S(1)}, bf16[128,4096]{1,0:T(8,128)(2,1)S(1)}, u32[]{:S(2)}, u32[]{:S(2)}) collective-permute-start(bf16[128,4096]{1,0:T(8,128)(2,1)S(1)} %collective-permute-done.5.refs_3_), channel_id=1, source_target_pairs={{0,4},{1,13},{2,6},{3,15},{4,8},{5,1},{6,10},{7,3},{8,12},{9,5},{1... | collective-permute-start | bytes 3145736 | tf_op jit(solution)/shard_map/ppermute | solution.py:32
  88.5 17.6 %collective-permute-start.12 = (bf16[128,4096]{1,0:T(8,128)(2,1)S(1)}, bf16[128,4096]{1,0:T(8,128)(2,1)S(1)}, u32[]{:S(2)}, u32[]{:S(2)}) collective-permute-start(bf16[128,4096]{1,0:T(8,128)(2,1)S(1)} %collective-permute-done.11), channel_id=1, source_target_pairs={{0,1},{1,0},{2,3},{3,2},{4,5},{5,4},{6,7},{7,6},{8,9},{9,8},{10,11... | collective-permute-start | bytes 3145736 | tf_op jit(solution)/shard_map/ppermute | solution.py:32
  89.5 16.6 %collective-permute-start.8 = (bf16[128,4096]{1,0:T(8,128)(2,1)S(1)}, bf16[128,4096]{1,0:T(8,128)(2,1)S(1)}, u32[]{:S(2)}, u32[]{:S(2)}) collective-permute-start(bf16[128,4096]{1,0:T(8,128)(2,1)S(1)} %collective-permute-done.6.refs_4_), channel_id=1, source_target_pairs={{0,1},{1,0},{2,3},{3,2},{4,5},{5,4},{6,7},{7,6},{8,9},{9,8},{10,11... | collective-permute-start | bytes 3145736 | tf_op jit(solution)/shard_map/ppermute | solution.py:32
  96.9 18.7 %collective-permute-start.24 = (bf16[128,4096]{1,0:T(8,128)(2,1)S(1)}, bf16[128,4096]{1,0:T(8,128)(2,1)S(1)}, u32[]{:S(2)}, u32[]{:S(2)}) collective-permute-start(bf16[128,4096]{1,0:T(8,128)(2,1)S(1)} %shard_map.43.refs_3_), channel_id=1, source_target_pairs={{0,1},{1,0},{2,3},{3,2},{4,5},{5,4},{6,7},{7,6},{8,9},{9,8},{10,11... | collective-permute-start | bytes 3145736 | tf_op jit(solution)/shard_map/ppermute | solution.py:32
  96.9 18.9 %collective-permute-start.14 = (bf16[128,4096]{1,0:T(8,128)(2,1)S(1)}, bf16[128,4096]{1,0:T(8,128)(2,1)S(1)}, u32[]{:S(2)}, u32[]{:S(2)}) collective-permute-start(bf16[128,4096]{1,0:T(8,128)(2,1)S(1)} %shard_map.44.refs_7_), channel_id=1, source_target_pairs={{0,4},{1,13},{2,6},{3,15},{4,8},{5,1},{6,10},{7,3},{8,12},{9,5},{1... | collective-permute-start | bytes 3145736 | tf_op jit(solution)/shard_map/ppermute | solution.py:32
  104.5 16.0 %collective-permute-start.22 = (bf16[128,4096]{1,0:T(8,128)(2,1)S(1)}, bf16[128,4096]{1,0:T(8,128)(2,1)S(1)}, u32[]{:S(2)}, u32[]{:S(2)}) collective-permute-start(bf16[128,4096]{1,0:T(8,128)(2,1)S(1)} %shard_map.43.refs_3_), channel_id=1, source_target_pairs={{0,16},{1,49},{2,18},{3,51},{4,20},{5,53},{6,22},{7,55},{8,24},{9,... | collective-permute-start | bytes 3145736 | tf_op jit(solution)/shard_map/ppermute | solution.py:32
  106.1 20.9 %collective-permute-start.15 = (bf16[128,4096]{1,0:T(8,128)(2,1)S(1)}, bf16[128,4096]{1,0:T(8,128)(2,1)S(1)}, u32[]{:S(2)}, u32[]{:S(2)}) collective-permute-start(bf16[128,4096]{1,0:T(8,128)(2,1)S(1)} %collective-permute-done.9.refs_8_), channel_id=1, source_target_pairs={{0,4},{1,13},{2,6},{3,15},{4,8},{5,1},{6,10},{7,3},{8,12},{9,5},{1... | collective-permute-start | bytes 3145736 | tf_op jit(solution)/shard_map/ppermute | solution.py:32
  106.1 23.4 %collective-permute-start.20 = (bf16[128,4096]{1,0:T(8,128)(2,1)S(1)}, bf16[128,4096]{1,0:T(8,128)(2,1)S(1)}, u32[]{:S(2)}, u32[]{:S(2)}) collective-permute-start(bf16[128,4096]{1,0:T(8,128)(2,1)S(1)} %collective-permute-done.18.refs_5_), channel_id=1, source_target_pairs={{0,2},{1,3},{2,0},{3,1},{4,6},{5,7},{6,4},{7,5},{8,10},{9,11},{10,... | collective-permute-start | bytes 3145736 | tf_op jit(solution)/shard_map/ppermute | solution.py:32
  115.6 16.2 %collective-permute-start.25 = (bf16[128,4096]{1,0:T(8,128)(2,1)S(1)}, bf16[128,4096]{1,0:T(8,128)(2,1)S(1)}, u32[]{:S(2)}, u32[]{:S(2)}) collective-permute-start(bf16[128,4096]{1,0:T(8,128)(2,1)S(1)} %collective-permute-done.24), channel_id=1, source_target_pairs={{0,16},{1,49},{2,18},{3,51},{4,20},{5,53},{6,22},{7,55},{8,24},{9,... | collective-permute-start | bytes 3145736 | tf_op jit(solution)/shard_map/ppermute | solution.py:32
  115.7 16.0 %collective-permute-start.16 = (bf16[128,4096]{1,0:T(8,128)(2,1)S(1)}, bf16[128,4096]{1,0:T(8,128)(2,1)S(1)}, u32[]{:S(2)}, u32[]{:S(2)}) collective-permute-start(bf16[128,4096]{1,0:T(8,128)(2,1)S(1)} %collective-permute-done.14.refs_1_), channel_id=1, source_target_pairs={{0,1},{1,0},{2,3},{3,2},{4,5},{5,4},{6,7},{7,6},{8,9},{9,8},{10,11... | collective-permute-start | bytes 3145736 | tf_op jit(solution)/shard_map/ppermute | solution.py:32
  120.5 11.6 %collective-permute-start.19 = (bf16[128,4096]{1,0:T(8,128)(2,1)S(1)}, bf16[128,4096]{1,0:T(8,128)(2,1)S(1)}, u32[]{:S(2)}, u32[]{:S(2)}) collective-permute-start(bf16[128,4096]{1,0:T(8,128)(2,1)S(1)} %collective-permute-done.18.refs_5_), channel_id=1, source_target_pairs={{0,1},{1,0},{2,3},{3,2},{4,5},{5,4},{6,7},{7,6},{8,9},{9,8},{10,11... | collective-permute-start | bytes 3145736 | tf_op jit(solution)/shard_map/ppermute | solution.py:32
  127.0 5.2 %collective-permute-start.17 = (bf16[128,4096]{1,0:T(8,128)(2,1)S(1)}, bf16[128,4096]{1,0:T(8,128)(2,1)S(1)}, u32[]{:S(2)}, u32[]{:S(2)}) collective-permute-start(bf16[128,4096]{1,0:T(8,128)(2,1)S(1)} %collective-permute-done.15.refs_2_), channel_id=1, source_target_pairs={{0,1},{1,0},{2,3},{3,2},{4,5},{5,4},{6,7},{7,6},{8,9},{9,8},{10,11... | collective-permute-start | bytes 3145736 | tf_op jit(solution)/shard_map/ppermute | solution.py:32
  129.5 2.7 %collective-permute-start.21 = (bf16[128,4096]{1,0:T(8,128)(2,1)S(1)}, bf16[128,4096]{1,0:T(8,128)(2,1)S(1)}, u32[]{:S(2)}, u32[]{:S(2)}) collective-permute-start(bf16[128,4096]{1,0:T(8,128)(2,1)S(1)} %collective-permute-done.20.refs_7_), channel_id=1, source_target_pairs={{0,1},{1,0},{2,3},{3,2},{4,5},{5,4},{6,7},{7,6},{8,9},{9,8},{10,11... | collective-permute-start | bytes 3145736 | tf_op jit(solution)/shard_map/ppermute | solution.py:32
  131.7 8.0 %collective-permute-start.26 = (bf16[128,4096]{1,0:T(8,128)(2,1)S(1)}, bf16[128,4096]{1,0:T(8,128)(2,1)S(1)}, u32[]{:S(2)}, u32[]{:S(2)}) collective-permute-start(bf16[128,4096]{1,0:T(8,128)(2,1)S(1)} %collective-permute-done.25), channel_id=1, source_target_pairs={{0,1},{1,0},{2,3},{3,2},{4,5},{5,4},{6,7},{7,6},{8,9},{9,8},{10,11... | collective-permute-start | bytes 3145736 | tf_op jit(solution)/shard_map/ppermute | solution.py:32
  131.7 16.0 %collective-permute-start.23 = (bf16[128,4096]{1,0:T(8,128)(2,1)S(1)}, bf16[128,4096]{1,0:T(8,128)(2,1)S(1)}, u32[]{:S(2)}, u32[]{:S(2)}) collective-permute-start(bf16[128,4096]{1,0:T(8,128)(2,1)S(1)} %collective-permute-done.22.refs_3_), channel_id=1, source_target_pairs={{0,16},{1,49},{2,18},{3,51},{4,20},{5,53},{6,22},{7,55},{8,24},{9,... | collective-permute-start | bytes 3145736 | tf_op jit(solution)/shard_map/ppermute | solution.py:32
  157.1 1.3 collective-permute-start.27
  158.3 3.7 %collective-permute-start.28 = (f32[16,128]{1,0:T(8,128)S(1)}, f32[16,128]{1,0:T(8,128)S(1)}, u32[]{:S(2)}, u32[]{:S(2)}) collective-permute-start(f32[16,128]{1,0:T(8,128)S(1)} %max.15), channel_id=1, source_target_pairs={{0,2},{1,3},{2,0},{3,1},{4,6},{5,7},{6,4},{7,5},{8,10},{9,11},{10,... | collective-permute-start | bytes 24584 | tf_op jit(solution)/shard_map/ppermute | solution.py:32
  162.0 5.2 %collective-permute-start.29 = (f32[16,128]{1,0:T(8,128)S(1)}, f32[16,128]{1,0:T(8,128)S(1)}, u32[]{:S(2)}, u32[]{:S(2)}) collective-permute-start(f32[16,128]{1,0:T(8,128)S(1)} %max.16), channel_id=1, source_target_pairs={{0,8},{1,9},{2,10},{3,11},{4,12},{5,13},{6,14},{7,15},{8,0},{9,1},... | collective-permute-start | bytes 24584 | tf_op jit(solution)/shard_map/ppermute | solution.py:32
  163.5 4.9 %collective-permute-start.30 = (f32[16,128]{1,0:T(8,128)S(1)}, f32[16,128]{1,0:T(8,128)S(1)}, u32[]{:S(2)}, u32[]{:S(2)}) collective-permute-start(f32[16,128]{1,0:T(8,128)S(1)} %max.16), channel_id=1, source_target_pairs={{0,4},{1,5},{2,6},{3,7},{4,8},{5,9},{6,10},{7,11},{8,12},{9,13},{1... | collective-permute-start | bytes 24584 | tf_op jit(solution)/shard_map/ppermute | solution.py:32
  165.7 3.7 %collective-permute-start.31 = (f32[16,128]{1,0:T(8,128)S(1)}, f32[16,128]{1,0:T(8,128)S(1)}, u32[]{:S(2)}, u32[]{:S(2)}) collective-permute-start(f32[16,128]{1,0:T(8,128)S(1)} %max.16), channel_id=1, source_target_pairs={{0,12},{1,13},{2,14},{3,15},{4,0},{5,1},{6,2},{7,3},{8,4},{9,5},{1... | collective-permute-start | bytes 24584 | tf_op jit(solution)/shard_map/ppermute | solution.py:32
  (1 other events, 62.6 us)

commit v2 on v1

v2 whole, which is shorter than its diff:
```python
import jax
import jax.numpy as jnp
from jax import lax
from jax.experimental import pallas as pl
from jax.experimental.pallas import tpu as pltpu
from jax.sharding import PartitionSpec as P

AXES = ("gr", "gc")
SIZES = {"yh": 2, "z": 4, "x": 4, "yl": 2, "c": 2}
F32 = jnp.float32
BF16 = jnp.bfloat16
MIB = 1024 * 1024


def coords(d):
    gr, gc = divmod(d, 16)
    return {"yh": gr // 4, "z": gr % 4, "x": gc // 4, "yl": (gc // 2) % 2, "c": gc % 2}


def flat(c):
    return (c["yh"] * 4 + c["z"]) * 16 + c["x"] * 4 + c["yl"] * 2 + c["c"]


def send(value, route):
    pairs = []
    for d in range(128):
        c = coords(d)
        for k, v in route.items():
            if v == "ring":
                v = 1 if c["c"] == 0 else -1
            elif v == "even":
                v = 1 if c[k] % 2 == 0 else -1
            elif v == "odd":
                v = 1 if c[k] % 2 == 1 else -1
            c[k] = (c[k] + v) % SIZES[k]
        pairs.append((d, flat(c)))
    return lax.ppermute(value, AXES, pairs)


def pack_kernel(pos_ref, items_ref, out_ref):
    count, width = items_ref.shape
    pos = pos_ref[...]
    dest = lax.broadcasted_iota(jnp.int32, (count, count), 0)
    hit = (pos // count) == dest
    pick = jnp.where(hit, 1.0, 0.0).astype(BF16)
    step = 1024
    for s in range(0, width, step):
        out_ref[:, s : s + step] = jnp.dot(
            pick, items_ref[:, s : s + step], preferred_element_type=F32
        ).astype(BF16)
    slot = jnp.sum(jnp.where(hit, (pos % count).astype(F32), 0.0), axis=1, keepdims=True)
    out_ref[:, width:] = jnp.broadcast_to(slot, (count, out_ref.shape[1] - width)).astype(BF16)


def place_kernel(in_ref, out_ref):
    count, width = out_ref.shape
    slot = in_ref[:, width : width + 128].astype(F32)
    lane = lax.broadcasted_iota(jnp.int32, (count, count), 1).astype(F32)
    pick = jnp.where(slot == lane, 1.0, 0.0).astype(BF16)
    step = 1024
    for s in range(0, width, step):
        out_ref[:, s : s + step] = lax.dot_general(
            pick, in_ref[:, s : s + step], (((0,), (0,)), ((), ())), preferred_element_type=F32
        ).astype(BF16)


def moved(sources, sizes):
    width = sources[0].shape[1]
    ins, at = [], 0
    for n, s in enumerate(sources):
        ins.append((n, at, at + s.shape[0]))
        at += s.shape[0]
    pieces, at = [], 0
    for m, size in enumerate(sizes):
        for n, lo, hi in ins:
            start, end = max(lo, at), min(hi, at + size)
            if start < end:
                pieces.append((n, start - lo, m, start - at, end - start))
        at += size

    def kernel(*refs):
        src, dst, sems = refs[: len(sources)], refs[len(sources) : -1], refs[-1]
        copies = [
            pltpu.make_async_copy(
                src[n].at[pl.ds(i, rows)], dst[m].at[pl.ds(o, rows)], sems.at[k]
            )
            for k, (n, i, m, o, rows) in enumerate(pieces)
        ]
        for c in copies:
            c.start()
        for c in copies:
            c.wait()

    return pl.pallas_call(
        kernel,
        out_shape=[jax.ShapeDtypeStruct((size, width), BF16) for size in sizes],
        in_specs=[pl.BlockSpec(memory_space=pl.ANY)] * len(sources),
        out_specs=[pl.BlockSpec(memory_space=pltpu.VMEM)] * len(sizes),
        scratch_shapes=[pltpu.SemaphoreType.DMA((len(pieces),))],
        compiler_params=pltpu.CompilerParams(vmem_limit_bytes=2 * MIB),
    )(*sources)


def pick_kernel(core_ref, up_ref, down_ref, out_ref, sem):
    def take(src):
        c = pltpu.make_async_copy(src, out_ref, sem)
        c.start()
        c.wait()

    @pl.when(core_ref[0] == 0)
    def _():
        take(up_ref)

    @pl.when(core_ref[0] != 0)
    def _():
        take(down_ref)


def pick(core, up, down):
    any_spec = pl.BlockSpec(memory_space=pl.ANY)
    return pl.pallas_call(
        pick_kernel,
        out_shape=jax.ShapeDtypeStruct(up.shape, BF16),
        in_specs=[pl.BlockSpec(memory_space=pltpu.SMEM), any_spec, any_spec],
        out_specs=pl.BlockSpec(memory_space=pltpu.VMEM),
        scratch_shapes=[pltpu.SemaphoreType.DMA],
        compiler_params=pltpu.CompilerParams(vmem_limit_bytes=2 * MIB),
    )(core, up, down)


def inverse_norm(ref, start, rows):
    total = jnp.zeros((rows, 128), F32)
    for s in range(0, ref.shape[1], 128):
        part = ref[start : start + rows, s : s + 128].astype(F32)
        total = total + part * part
    return 1.0 / jnp.sqrt(jnp.sum(total, axis=1, keepdims=True) + 1e-06)


def across(column):
    return jnp.transpose(jnp.broadcast_to(column, (128, 128)))[:1, :]


def make_block_kernel(row_sizes, col_sizes, fresh_rows, fresh_cols, diagonal, last):
    n_rb, n_cb = sum(row_sizes) // 128, sum(col_sizes) // 128
    tile = 512
    per_tile = tile // 128

    def kernel(*refs):
        refs = list(refs)

        def grab(count):
            return [refs.pop(0) for _ in range(count)]

        (where,) = grab(1)
        row_refs, col_refs = grab(len(row_sizes)), grab(len(col_sizes))
        row_inv = [] if fresh_rows else grab(len(row_sizes))
        col_inv = [] if fresh_cols else grab(len(col_sizes))
        best_in = [] if fresh_rows else grab(len(row_sizes))
        if not diagonal:
            grab(1)
        (out_ref,) = grab(1)
        best_out = grab(1 if fresh_rows or last else len(row_sizes))
        if fresh_rows:
            rows_v, row_inv_out = grab(2)
        if fresh_cols:
            cols_v, col_inv_out = grab(2)
        row_sem, col_sem = refs

        def loads(sources, sizes, target, sems):
            made, at = [], 0
            for n, (ref, size) in enumerate(zip(sources, sizes)):
                c = pltpu.make_async_copy(
                    ref.at[pl.ds(0, size)], target.at[pl.ds(at, size)], sems.at[n]
                )
                c.start()
                made.append((at, c))
                at += size
            return made

        col_loads = loads(col_refs, col_sizes, cols_v, col_sem) if fresh_cols else []
        row_loads = loads(row_refs, row_sizes, rows_v, row_sem) if fresh_rows else []
        for _, c in col_loads:
            c.wait()
        if fresh_cols:
            for lane in range(0, sum(col_sizes), 128):
                col_inv_out[:, lane : lane + 128] = jnp.broadcast_to(
                    across(inverse_norm(cols_v, lane, 128)), (8, 128)
                )
        if fresh_cols:
            groups = [(0, cols_v, col_inv_out)]
        else:
            starts = [sum(col_sizes[:n]) for n in range(len(col_sizes))]
            groups = list(zip(starts, col_refs, col_inv))
        for t in range(n_rb // per_tile):
            if fresh_rows:
                while row_loads and row_loads[0][0] < (t + 1) * tile:
                    row_loads.pop(0)[1].wait()
                source, part, base = rows_v, None, t * tile
            else:
                part, base = t, 0
                source = row_refs[part]
            products = [
                lax.dot_general(
                    source[base : base + tile, :],
                    ref[...],
                    (((1,), (1,)), ((), ())),
                    preferred_element_type=F32,
                )
                for _, ref, _ in groups
            ]
            for k in range(per_tile):
                r = t * per_tile + k
                span = slice(base + 128 * k, base + 128 * k + 128)
                if fresh_rows:
                    inv = jnp.broadcast_to(inverse_norm(rows_v, span.start, 128), (128, 128))
                    row_inv_out[span, :] = inv
                    top = None
                else:
                    inv = row_inv[part][span, :]
                    top = best_in[part][span, :]
                a = where[r]
                here = pl.ds(pl.multiple_of(a * 128, 128), 128)
                for (first, ref, inv_ref), product in zip(groups, products):
                    for lane in range(0, ref.shape[0], 128):
                        lanes = slice(lane, lane + 128)
                        scaled = product[128 * k : 128 * k + 128, lanes] * inv * inv_ref[:1, lanes]
                        there = where[n_rb + (first + lane) // 128]
                        out_ref[here, pl.ds(pl.multiple_of(there * 128, 128), 128)] = scaled.astype(
                            BF16
                        )
                        if diagonal and r == 0 and first + lane == 0:
                            across_i = lax.broadcasted_iota(jnp.int32, scaled.shape, 1)
                            down_i = lax.broadcasted_iota(jnp.int32, scaled.shape, 0)
                            scaled = jnp.where(across_i == down_i, -2.0, scaled)
                        top = scaled if top is None else jnp.maximum(top, scaled)
                if last:
                    best_out[0][pl.ds(a, 1), :] = across(jnp.max(top, axis=1, keepdims=True))
                elif fresh_rows:
                    best_out[0][span, :] = top
                else:
                    best_out[part][span, :] = top

    return kernel


def block_call(where, rows, cols, out, row_inv=None, col_inv=None, best=None, last=False):
    fresh_rows, fresh_cols = row_inv is None, col_inv is None
    row_sizes, col_sizes = [r.shape[0] for r in rows], [c.shape[0] for c in cols]
    n_rows, n_cols = sum(row_sizes), sum(col_sizes)
    width = rows[0].shape[1]
    any_spec = pl.BlockSpec(memory_space=pl.ANY)
    vmem_spec = pl.BlockSpec(memory_space=pltpu.VMEM)
    args = [where, *rows, *cols]
    in_specs = [pl.BlockSpec(memory_space=pltpu.SMEM)]
    in_specs += [any_spec if fresh_rows else vmem_spec] * len(rows)
    in_specs += [any_spec if fresh_cols else vmem_spec] * len(cols)
    for extra in (row_inv, col_inv, best):
        if extra is not None:
            args += extra
            in_specs += [vmem_spec] * len(extra)
    aliases = {}
    if out is not None:
        args.append(out)
        in_specs.append(vmem_spec)
        aliases = {len(args) - 1: 0}
    out_shape = [jax.ShapeDtypeStruct((2048, 1024), BF16)]
    if last:
        out_shape.append(jax.ShapeDtypeStruct((16, 128), F32))
    else:
        out_shape += [jax.ShapeDtypeStruct((512, 128), F32)] * (1 if fresh_rows else len(rows))
    if fresh_rows:
        out_shape.append(jax.ShapeDtypeStruct((n_rows, width), BF16))
        out_shape.append(jax.ShapeDtypeStruct((n_rows, 128), F32))
    if fresh_cols:
        out_shape.append(jax.ShapeDtypeStruct((n_cols, width), BF16))
        out_shape.append(jax.ShapeDtypeStruct((8, n_cols), F32))
    return pl.pallas_call(
        make_block_kernel(row_sizes, col_sizes, fresh_rows, fresh_cols, out is None, last),
        out_shape=out_shape,
        in_specs=in_specs,
        out_specs=[vmem_spec] * len(out_shape),
        input_output_aliases=aliases,
        scratch_shapes=[
            pltpu.SemaphoreType.DMA((len(rows),)),
            pltpu.SemaphoreType.DMA((len(cols),)),
        ],
        compiler_params=pltpu.CompilerParams(vmem_limit_bytes=VMEM_LIMIT),
        cost_estimate=pl.CostEstimate(
            flops=n_rows * n_cols * width // 4,
            bytes_accessed=2 * n_rows * n_cols,
            transcendentals=0,
        ),
    )(*args)


def store_kernel(held_ref, out_ref, sems):
    rows = held_ref.shape[0] // sems.shape[0]
    copies = [
        pltpu.make_async_copy(
            held_ref.at[pl.ds(rows * n, rows)], out_ref.at[pl.ds(rows * n, rows)], sems.at[n]
        )
        for n in range(sems.shape[0])
    ]
    for c in copies:
        c.start()
    for c in copies:
        c.wait()


def store(held):
    return pl.pallas_call(
        store_kernel,
        out_shape=jax.ShapeDtypeStruct(held.shape, held.dtype),
        in_specs=[pl.BlockSpec(memory_space=pltpu.VMEM)],
        out_specs=pl.BlockSpec(memory_space=pl.ANY),
        scratch_shapes=[pltpu.SemaphoreType.DMA((4,))],
        compiler_params=pltpu.CompilerParams(vmem_limit_bytes=2 * MIB),
        cost_estimate=pl.CostEstimate(
            flops=0, bytes_accessed=2 * held.size * 2, transcendentals=0
        ),
    )(held)


VMEM_LIMIT = 12 * MIB


def fence(*values):
    return lax.optimization_barrier(values)


def per_device(items, position_of):
    count, width = items.shape
    vmem_spec = pl.BlockSpec(memory_space=pltpu.VMEM)
    packed = pl.pallas_call(
        pack_kernel,
        out_shape=jax.ShapeDtypeStruct((count, width + 1024), BF16),
        in_specs=[vmem_spec, vmem_spec],
        out_specs=vmem_spec,
    )(position_of.reshape(1, count), items)
    gr, gc = lax.axis_index("gr"), lax.axis_index("gc")
    yh, z = gr // 4, gr % 4
    x, yl, core = gc // 4, (gc // 2) % 2, gc % 2

    def row_at(dx=0, dy=0, dc=0):
        return ((x + dx + 4) % 4) * 4 + ((yl + dy) % 2) * 2 + (core + dc) % 2

    def col_at(dy=0, dz=0):
        return ((yh + dy) % 2) * 4 + (z + dz + 4) % 4

    ring = 1 - 2 * core
    rows_at = [
        [row_at(), row_at(dc=1), row_at(-ring), row_at(-ring, dc=1)],
        [row_at(dy=1), row_at(dy=1, dc=1), row_at(ring, dc=1), row_at(ring)],
        [row_at(2), row_at(-ring, 1, 1), row_at(2, dc=1), row_at(ring, 1)],
        [row_at(-ring, 1), row_at(ring, 1, 1), row_at(2, 1), row_at(2, 1, 1)],
    ]
    cols_at = [
        [col_at(), col_at(dz=-ring)],
        [col_at(dz=ring), col_at(dz=2)],
        [col_at(1), col_at(1, -ring)],
        [col_at(1, ring), col_at(1, 2)],
    ]

    def places(rows, cols):
        flat_list = sum([rows_at[r] for r in rows], []) + sum([cols_at[c] for c in cols], [])
        return jnp.stack(flat_list).astype(jnp.int32)

    packed, *where = fence(
        packed,
        places([0], [0]),
        places([1], [0]),
        places([0, 1], [1]),
        places([2], [0, 1]),
        places([0, 1, 2], [2]),
        places([3], [0, 1, 2]),
        places([0, 1, 2, 3], [3]),
    )
    arrived = lax.all_to_all(
        packed.reshape(count, -1, 128), AXES, split_axis=0, concat_axis=0, tiled=True
    ).reshape(count, -1)
    own = pl.pallas_call(
        place_kernel,
        out_shape=jax.ShapeDtypeStruct((count, width), BF16),
        in_specs=[vmem_spec],
        out_specs=vmem_spec,
    )(arrived)

    cross, near, over = {"c": 1}, {"yl": 1}, {"yh": 1, "yl": 1}
    up_x, up_z = {"x": "ring"}, {"z": "ring"}
    def swap(value):
        return [send(v, cross) for v in moved([value], [count // 2] * 2)]

    own_c = send(own, cross)
    x_a, z_a, pair = send(own, up_x), send(own, up_z), send(own, near)
    x_b, z_b = send(own_c, up_x), send(own_c, up_z)
    pair_c = swap(pair)
    own_c, x_a, x_b, z_a, z_b, pair, *pair_c = fence(own_c, x_a, x_b, z_a, z_b, pair, *pair_c)

    (x_ring,) = moved([x_a, *pair_c], [256])
    x_2 = send(x_ring, up_x)
    p_a, far = send(x_a, near), send(pair, over)
    x_a_c, x_b_c = send(x_a, cross), send(x_b, cross)
    out, best_1, rows_1, inv_1, cols_1, col_inv_1 = block_call(
        where[0], [own, own_c, x_a, x_b], [own, z_a], None
    )
    out, best_2, rows_2, inv_2 = block_call(
        where[1], [pair, *pair_c, x_a_c, x_b_c], [cols_1], out, col_inv=[col_inv_1]
    )
    z_a, z_b, best_2 = fence(z_a, z_b, best_2)
    z_2, z_b_c = send(z_a, up_z), send(z_b, cross)
    far, p_a, z_b_c, x_2 = fence(far, p_a, z_b_c, x_2)
    far_c, p_a_c = swap(far), swap(p_a)
    (far_c,) = moved(far_c, [count])
    x_2, p_a, far, z_2, far_c, z_b_c, best_2, *p_a_c = fence(
        x_2, p_a, far, z_2, far_c, z_b_c, best_2, *p_a_c
    )

    f_a, f_2, p_2 = send(far, up_z), send(z_2, {"yh": 1}), send(p_a, up_x)
    x_2_c = send(x_2, cross)
    out, best_1, best_2, cols_2, col_inv_2 = block_call(
        where[2], [rows_1, rows_2], [z_b_c, z_2], out, row_inv=[inv_1, inv_2], best=[best_1, best_2]
    )
    out, best_3, rows_3, inv_3 = block_call(
        where[3], [x_2, x_2_c], [cols_1, cols_2], out, col_inv=[col_inv_1, col_inv_2]
    )
    far_c, best_3 = fence(far_c, best_3)
    f_b = send(far_c, up_z)
    p_2, best_3 = fence(p_2, best_3)
    p_2_c = swap(p_2)
    out, best_1, best_2, best_3, cols_3, col_inv_3 = block_call(
        where[4],
        [rows_1, rows_2, rows_3],
        [far, f_a],
        out,
        row_inv=[inv_1, inv_2, inv_3],
        best=[best_1, best_2, best_3],
    )
    out, best_4, rows_4, inv_4 = block_call(
        where[5],
        [p_a, *p_a_c, p_2, *p_2_c],
        [cols_1, cols_2, cols_3],
        out,
        col_inv=[col_inv_1, col_inv_2, col_inv_3],
    )
    f_b, f_2, best_4 = fence(f_b, f_2, best_4)
    f_b_c = swap(f_b)
    out, best, _, _ = block_call(
        where[6],
        [rows_1, rows_2, rows_3, rows_4],
        [*f_b_c, f_2],
        out,
        row_inv=[inv_1, inv_2, inv_3, inv_4],
        best=[best_1, best_2, best_3, best_4],
        last=True,
    )

    best = jnp.maximum(best, send(best, cross))
    best = jnp.maximum(best, send(best, near))
    best = jnp.maximum(best, send(best, {"x": "even"}))
    best, out = fence(best, store(out))
    best = jnp.maximum(best, send(best, {"x": "odd"}))
    return out, best.reshape(-1)


def solution(mesh):
    return jax.shard_map(
        per_device,
        mesh=mesh,
        in_specs=(P(("gr", "gc"), None), P(("gr", "gc"))),
        out_specs=(P("gr", "gc"), P("gr")),
        check_vma=False,
    )
```

time: 171 us -> 158 us (0.924)
  starting transfers between devices: 20.4 us -> 12.6 us
  waiting for transfers between devices: 71.5 us -> 67.8 us
  other arithmetic: 3.24 us -> 0.61 us
  blocking collectives: 30.6 us -> 32.6 us
    ppermute x32, starting transfers between devices: 20.4 us -> 12.6 us  [send(): return lax.ppermute(value, AXES, pairs)]
    ppermute x32, waiting for transfers between devices: 71.5 us -> 67.8 us  [send(): return lax.ppermute(value, AXES, pairs)]
    all_to_all x1 -> x0, other arithmetic: 2.63 us -> none  [per_device(): lax.all_to_all(packed, AXES, split_axis=0, concat_axis=0, tiled=True)]
    all_to_all x1, blocking collectives: 30.6 us -> 32.6 us  [per_device(): lax.all_to_all(packed.reshape(count, -1, 128), AXES, split_axis=0, concat...]
    pallas_call x7 -> x16, Pallas kernels: 36.5 us -> 36.4 us  [the longest x7 30.9 us: block_call(): pl.pallas_call(make_block_kernel(row_sizes, col_sizes, fresh_rows, fresh_...]
  transfers between devices with their start and end apart: 32 -> 32, of which waited for: 16 -> 18; matrix products, arithmetic and copies ran while one was open for 0% -> 0% of each run, Pallas kernels for 14% -> 17%
where the time goes in v2:
time: 158 us; the launch traced here: 157 us
  waiting for transfers between devices  67.8 us (43%)
  Pallas kernels  39.1 us (25%)
  blocking collectives  32.6 us (21%)
  starting transfers between devices  12.6 us (8%)
  local copies, waits for them, and re-layouts  3.5 us (2%)
    ppermute x32, waiting for transfers between devices, send(): return lax.ppermute(value, AXES, pairs)  67.8 us
    all_to_all x1, blocking collectives, per_device(): lax.all_to_all(packed.reshape(count, -1, 128), AXES, split_axis=0, concat...  32.6 us
    pallas_call x7, Pallas kernels, block_call(): pl.pallas_call(make_block_kernel(row_sizes, col_sizes, fresh_rows, fresh_...  30.9 us
    ppermute x32, starting transfers between devices, send(): return lax.ppermute(value, AXES, pairs)  12.6 us
  transfers between devices with their start and end apart: 32, of which 18 were waited for; matrix products, arithmetic and copies ran while one was open for 0% of the time, Pallas kernels for 17%

profile of v2, /device:TPU:0, one launch (start us, length us, event | category | flops | bytes accessed | tf_op | source)
XLA Modules:
  0.0 157.5 jit_solution(7548279069651464720)
XLA Ops:
  1.6 2.7 %shard_map.41 = bf16[128,5120]{1,0:T(8,128)(2,1)} custom-call(s32[1,128]{1,0:T(1,128)} %bitcast.37, bf16[128,4096]{1,0:T(8,128)(2,1)} %items_ref.1), custom_call_target="tpu_custom_call" | custom-call | tf_op jit(solution)/shard_map/pallas_call | solution.py:334
  4.3 1.6 copy.10
  5.8 32.6 %all_to_all.5 = bf16[128,40,128]{2,1,0:T(8,128)(2,1)S(1)} all-to-all(bf16[128,40,128]{2,1,0:T(8,128)(2,1)S(1)} %bitcast.33), channel_id=1, replica_groups=mesh['gr'=8,'gc'=16] {'gr','gc'}, dimensions={0} | all-to-all | bytes 2621440 | tf_op jit(solution)/shard_map/all_to_all | solution.py:378
  38.5 1.3 copy.13
  39.8 2.8 %shard_map.42.refs_1_.refs_5_ = bf16[128,4096]{1,0:T(8,128)(2,1)} custom-call(bf16[128,5120]{1,0:T(8,128)(2,1)} %bitcast.35), custom_call_target="tpu_custom_call" | custom-call | tf_op jit(solution)/shard_map/pallas_call | solution.py:381
  43.7 1.8 %collective-permute-done.refs_2_ = bf16[128,4096]{1,0:T(8,128)(2,1)S(1)} collective-permute-done((bf16[128,4096]{1,0:T(8,128)(2,1)}, bf16[128,4096]{1,0:T(8,128)(2,1)S(1)}, u32[]{:S(2)}, u32[]{:S(2)}) %collective-permute-start) | collective-permute-done | bytes 1048608 | tf_op jit(solution)/shard_map/ppermute | solution.py:37
  45.6 22.8 %collective-permute-done.5.refs_0_.refs_1_ = bf16[128,4096]{1,0:T(8,128)(2,1)S(1)} collective-permute-done((bf16[128,4096]{1,0:T(8,128)(2,1)}, bf16[128,4096]{1,0:T(8,128)(2,1)S(1)}, u32[]{:S(2)}, u32[]{:S(2)}) %collective-permute-start.5) | collective-permute-done | bytes 1048608 | tf_op jit(solution)/shard_map/ppermute | solution.py:37
  69.0 1.4 collective-permute-done.6.refs_2_.refs_1_
  72.0 0.9 collective-permute-start.11
  72.9 1.0 collective-permute-start.10
  73.9 3.6 %shard_map.44 = (bf16[2048,1024]{1,0:T(8,128)(2,1)S(1)}, f32[512,128]{1,0:T(8,128)S(1)}, bf16[512,4096]{1,0:T(8,128)(2,1)S(1)}, f32[512,128]{1,0:T(8,128)S(1)}, ...) custom-call(s32[6]{0:T(128)S(1)} %stack.68.refs_0_, bf16[128,4096]{1,0:T(8,128)(2,1)S(1)} %copy-done, ...), custom_call_target="tpu_custom_call" | custom-call | flops 134217728 | bytes 262144 | tf_op jit(solution)/shard_map/pallas_call | solution.py:277
  77.5 2.9 %shard_map.45 = (bf16[2048,1024]{1,0:T(8,128)(2,1)S(1)}, f32[512,128]{1,0:T(8,128)S(1)}, bf16[512,4096]{1,0:T(8,128)(2,1)S(1)}, f32[512,128]{1,0:T(8,128)S(1)}) custom-call(s32[6]{0:T(128)S(1)} %stack.73.refs_0_, bf16[128,4096]{1,0:T(8,128)(2,1)S(1)} %collective-permute-done.5.refs_0_.refs_1_, ...), custom_call_target="tpu_custom_call", output_to_operand_aliasing={{0}: (8, {})} | custom-call | flops 134217728 | bytes 262144 | tf_op jit(solution)/shard_map/pallas_call | solution.py:277
  80.5 1.1 collective-permute-start.14
  81.6 18.1 %collective-permute-done.10.refs_0_.refs_4_ = bf16[128,4096]{1,0:T(8,128)(2,1)S(1)} collective-permute-done((bf16[128,4096]{1,0:T(8,128)(2,1)S(1)}, bf16[128,4096]{1,0:T(8,128)(2,1)S(1)}, u32[]{:S(2)}, u32[]{:S(2)}) %collective-permute-start.10) | collective-permute-done | bytes 1048608 | tf_op jit(solution)/shard_map/ppermute | solution.py:37
  100.9 0.9 collective-permute-done.15.refs_0_
  104.2 0.9 collective-permute-start.20
  105.2 1.1 collective-permute-start.23
  106.3 3.5 %shard_map.50 = (bf16[2048,1024]{1,0:T(8,128)(2,1)S(1)}, f32[512,128]{1,0:T(8,128)S(1)}, f32[512,128]{1,0:T(8,128)S(1)}, bf16[256,4096]{1,0:T(8,128)(2,1)S(1)}, f32[8,256]{1,0:T(8,128)S(1)}) custom-call(s32[10]{0:T(128)S(1)} %stack.76.refs_0_, bf16[512,4096]{1,0:T(8,128)(2,1)S(1)} %get-tuple-element.93.refs_1_, ...), custom_call_target="tpu_custom_call", output_to_operand_aliasing={{0}: (9, {})} | custom-call | flops 268435456 | bytes 524288 | tf_op jit(solution)/shard_map/pallas_call | solution.py:277
  109.8 4.0 %shard_map.51 = (bf16[2048,1024]{1,0:T(8,128)(2,1)S(1)}, f32[512,128]{1,0:T(8,128)S(1)}, bf16[512,4096]{1,0:T(8,128)(2,1)S(1)}, f32[512,128]{1,0:T(8,128)S(1)}) custom-call(s32[8]{0:T(128)S(1)} %stack.160.refs_0_, bf16[256,4096]{1,0:T(8,128)(2,1)S(1)} %collective-permute-done.13.refs_1_, ...), custom_call_target="tpu_custom_call", output_to_operand_aliasing={{0}: (7, {})} | custom-call | flops 268435456 | bytes 524288 | tf_op jit(solution)/shard_map/pallas_call | solution.py:277
  113.8 1.2 collective-permute-start.24
  115.0 5.2 %collective-permute-done.20.refs_0_.refs_4_ = bf16[128,4096]{1,0:T(8,128)(2,1)S(1)} collective-permute-done((bf16[128,4096]{1,0:T(8,128)(2,1)S(1)}, bf16[128,4096]{1,0:T(8,128)(2,1)S(1)}, u32[]{:S(2)}, u32[]{:S(2)}) %collective-permute-start.20) | collective-permute-done | bytes 1048608 | tf_op jit(solution)/shard_map/ppermute | solution.py:37
  121.2 4.6 %shard_map.53 = (bf16[2048,1024]{1,0:T(8,128)(2,1)S(1)}, f32[512,128]{1,0:T(8,128)S(1)}, f32[512,128]{1,0:T(8,128)S(1)}, f32[512,128]{1,0:T(8,128)S(1)}, bf16[25...) custom-call(s32[14]{0:T(128)S(1)} %stack.163.refs_0_, ...), custom_call_target="tpu_custom_call", output_to_operand_aliasing={{0}: (12, {})} | custom-call | flops 402653184 | bytes 786432 | tf_op jit(solution)/shard_map/pallas_call | solution.py:277
  125.8 5.2 %shard_map.54 = (bf16[2048,1024]{1,0:T(8,128)(2,1)S(1)}, f32[512,128]{1,0:T(8,128)S(1)}, bf16[512,4096]{1,0:T(8,128)(2,1)S(1)}, f32[512,128]{1,0:T(8,128)S(1)}) custom-call(s32[10]{0:T(128)S(1)} %stack.168.refs_0_, bf16[128,4096]{1,0:T(8,128)(2,1)S(1)} %collective-permute-done.11.refs_0_.refs_1_, ...), custom_call_target="tpu_custom_call", output_to_operand_aliasing={{0}: (13, {})} | custom-call | flops 402653184 | bytes 786432 | tf_op jit(solution)/shard_map/pallas_call | solution.py:277
  131.1 2.4 %collective-permute-done.25.refs_7_ = bf16[128,4096]{1,0:T(8,128)(2,1)S(1)} collective-permute-done((bf16[128,4096]{1,0:T(8,128)(2,1)S(1)}, bf16[128,4096]{1,0:T(8,128)(2,1)S(1)}, u32[]{:S(2)}, u32[]{:S(2)}) %collective-permute-start.25) | collective-permute-done | bytes 1048608 | tf_op jit(solution)/shard_map/ppermute | solution.py:37
  134.2 1.4 collective-permute-done.26.refs_5_
  136.4 7.1 %shard_map.56 = (bf16[2048,1024]{1,0:T(8,128)(2,1)S(1)}, f32[16,128]{1,0:T(8,128)S(1)}, bf16[256,4096]{1,0:T(8,128)(2,1)}, f32[8,256]{1,0:T(8,128)}) custom-call(s32[18]{0:T(128)S(1)} %stack.171.refs_0_, bf16[512,4096]{1,0:T(8,128)(2,1)S(1)} %get-tuple-element.93.refs_1_, ...), custom_call_target="tpu_custom_call", output_to_operand_aliasing={{0}: (16, {})} | custom-call | flops 536870912 | bytes 1048576 | tf_op jit(solution)/shard_map/pallas_call | solution.py:277
  143.7 1.0 collective-permute-done.28
  144.7 3.6 %collective-permute-done.29 = f32[16,128]{1,0:T(8,128)S(1)} collective-permute-done((f32[16,128]{1,0:T(8,128)S(1)}, f32[16,128]{1,0:T(8,128)S(1)}, u32[]{:S(2)}, u32[]{:S(2)}) %collective-permute-start.29) | collective-permute-done | bytes 8224 | tf_op jit(solution)/shard_map/ppermute | solution.py:37
  148.4 2.0 %shard_map.57 = bf16[2048,1024]{1,0:T(8,128)(2,1)} custom-call(bf16[2048,1024]{1,0:T(8,128)(2,1)S(1)} %get-tuple-element.163.held_ref), custom_call_target="tpu_custom_call" | custom-call | bytes 8388608 | tf_op jit(solution)/shard_map/pallas_call | solution.py:311
  150.4 1.6 %collective-permute-done.30 = f32[16,128]{1,0:T(8,128)S(1)} collective-permute-done((f32[16,128]{1,0:T(8,128)S(1)}, f32[16,128]{1,0:T(8,128)S(1)}, u32[]{:S(2)}, u32[]{:S(2)}) %collective-permute-start.30) | collective-permute-done | bytes 8224 | tf_op jit(solution)/shard_map/ppermute | solution.py:37
  152.0 1.2 collective-permute-start.31
  153.2 3.7 %collective-permute-done.31 = f32[16,128]{1,0:T(8,128)S(1)} collective-permute-done((f32[16,128]{1,0:T(8,128)S(1)}, f32[16,128]{1,0:T(8,128)S(1)}, u32[]{:S(2)}, u32[]{:S(2)}) %collective-permute-start.31) | collective-permute-done | bytes 8224 | tf_op jit(solution)/shard_map/ppermute | solution.py:37
  (65 shorter events, 11.0 us)
Async XLA Ops:
  42.6 2.9 %collective-permute-start = (bf16[128,4096]{1,0:T(8,128)(2,1)}, bf16[128,4096]{1,0:T(8,128)(2,1)S(1)}, u32[]{:S(2)}, u32[]{:S(2)}) collective-permute-start(bf16[128,4096]{1,0:T(8,128)(2,1)} %shard_map.42.refs_1_.refs_5_), channel_id=1, source_target_pairs={{0,1},{1,0},{2,3},{3,2},{4,5},{5,4},{6,7},{7,6},{8,9},{9,8},{10,11... | collective-permute-start | bytes 3145736 | tf_op jit(solution)/shard_map/ppermute | solution.py:37
  42.6 25.8 %collective-permute-start.5 = (bf16[128,4096]{1,0:T(8,128)(2,1)}, bf16[128,4096]{1,0:T(8,128)(2,1)S(1)}, u32[]{:S(2)}, u32[]{:S(2)}) collective-permute-start(bf16[128,4096]{1,0:T(8,128)(2,1)} %shard_map.42.refs_1_.refs_5_), channel_id=1, source_target_pairs={{0,2},{1,3},{2,0},{3,1},{4,6},{5,7},{6,4},{7,5},{8,10},{9,11},{10,... | collective-permute-start | bytes 3145736 | tf_op jit(solution)/shard_map/ppermute | solution.py:37
  43.1 25.4 %collective-permute-start.3 = (bf16[128,4096]{1,0:T(8,128)(2,1)}, bf16[128,4096]{1,0:T(8,128)(2,1)S(1)}, u32[]{:S(2)}, u32[]{:S(2)}) collective-permute-start(bf16[128,4096]{1,0:T(8,128)(2,1)} %shard_map.42.refs_1_.refs_5_), channel_id=1, source_target_pairs={{0,16},{1,49},{2,18},{3,51},{4,20},{5,53},{6,22},{7,55},{8,24},{9,... | collective-permute-start | bytes 3145736 | tf_op jit(solution)/shard_map/ppermute | solution.py:37
  43.1 25.9 %collective-permute-start.1 = (bf16[128,4096]{1,0:T(8,128)(2,1)}, bf16[128,4096]{1,0:T(8,128)(2,1)S(1)}, u32[]{:S(2)}, u32[]{:S(2)}) collective-permute-start(bf16[128,4096]{1,0:T(8,128)(2,1)} %shard_map.42.refs_1_.refs_5_), channel_id=1, source_target_pairs={{0,4},{1,13},{2,6},{3,15},{4,8},{5,1},{6,10},{7,3},{8,12},{9,5},{1... | collective-permute-start | bytes 3145736 | tf_op jit(solution)/shard_map/ppermute | solution.py:37
  45.4 25.8 %collective-permute-start.4 = (bf16[128,4096]{1,0:T(8,128)(2,1)S(1)}, bf16[128,4096]{1,0:T(8,128)(2,1)S(1)}, u32[]{:S(2)}, u32[]{:S(2)}) collective-permute-start(bf16[128,4096]{1,0:T(8,128)(2,1)S(1)} %collective-permute-done.refs_2_), channel_id=1, source_target_pairs={{0,16},{1,49},{2,18},{3,51},{4,20},{5,53},{6,22},{7,55},{8,24},{9,... | collective-permute-start | bytes 3145736 | tf_op jit(solution)/shard_map/ppermute | solution.py:37
  45.4 25.8 %collective-permute-start.2 = (bf16[128,4096]{1,0:T(8,128)(2,1)S(1)}, bf16[128,4096]{1,0:T(8,128)(2,1)S(1)}, u32[]{:S(2)}, u32[]{:S(2)}) collective-permute-start(bf16[128,4096]{1,0:T(8,128)(2,1)S(1)} %collective-permute-done.refs_2_), channel_id=1, source_target_pairs={{0,4},{1,13},{2,6},{3,15},{4,8},{5,1},{6,10},{7,3},{8,12},{9,5},{1... | collective-permute-start | bytes 3145736 | tf_op jit(solution)/shard_map/ppermute | solution.py:37
  68.4 2.0 %collective-permute-start.6 = (bf16[64,4096]{1,0:T(8,128)(2,1)S(1)}, bf16[64,4096]{1,0:T(8,128)(2,1)S(1)}, u32[]{:S(2)}, u32[]{:S(2)}) collective-permute-start(bf16[64,4096]{1,0:T(8,128)(2,1)S(1)} %get-tuple-element.87), channel_id=1, source_target_pairs={{0,1},{1,0},{2,3},{3,2},{4,5},{5,4},{6,7},{7,6},{8,9},{9,8},{10,11... | collective-permute-start | bytes 1572872 | tf_op jit(solution)/shard_map/ppermute | solution.py:37
  68.6 2.6 %collective-permute-start.7 = (bf16[64,4096]{1,0:T(8,128)(2,1)S(1)}, bf16[64,4096]{1,0:T(8,128)(2,1)S(1)}, u32[]{:S(2)}, u32[]{:S(2)}) collective-permute-start(bf16[64,4096]{1,0:T(8,128)(2,1)S(1)} %get-tuple-element.88), channel_id=1, source_target_pairs={{0,1},{1,0},{2,3},{3,2},{4,5},{5,4},{6,7},{7,6},{8,9},{9,8},{10,11... | collective-permute-start | bytes 1572872 | tf_op jit(solution)/shard_map/ppermute | solution.py:37
  71.2 6.3 %collective-permute-start.9 = (bf16[128,4096]{1,0:T(8,128)(2,1)S(1)}, bf16[128,4096]{1,0:T(8,128)(2,1)S(1)}, u32[]{:S(2)}, u32[]{:S(2)}) collective-permute-start(bf16[128,4096]{1,0:T(8,128)(2,1)S(1)} %collective-permute-done.2.refs_4_), channel_id=1, source_target_pairs={{0,1},{1,0},{2,3},{3,2},{4,5},{5,4},{6,7},{7,6},{8,9},{9,8},{10,11... | collective-permute-start | bytes 3145736 | tf_op jit(solution)/shard_map/ppermute | solution.py:37
  71.3 6.2 %collective-permute-start.8 = (bf16[128,4096]{1,0:T(8,128)(2,1)S(1)}, bf16[128,4096]{1,0:T(8,128)(2,1)S(1)}, u32[]{:S(2)}, u32[]{:S(2)}) collective-permute-start(bf16[128,4096]{1,0:T(8,128)(2,1)S(1)} %collective-permute-done.1.refs_3_.refs_0_), channel_id=1, source_target_pairs={{0,1},{1,0},{2,3},{3,2},{4,5},{5,4},{6,7},{7,6},{8,9},{9,8},{10,11... | collective-permute-start | bytes 3145736 | tf_op jit(solution)/shard_map/ppermute | solution.py:37
  71.9 27.7 %collective-permute-start.13 = (bf16[256,4096]{1,0:T(8,128)(2,1)S(1)}, bf16[256,4096]{1,0:T(8,128)(2,1)S(1)}, u32[]{:S(2)}, u32[]{:S(2)}) collective-permute-start(bf16[256,4096]{1,0:T(8,128)(2,1)S(1)} %shard_map.46), channel_id=1, source_target_pairs={{0,4},{1,13},{2,6},{3,15},{4,8},{5,1},{6,10},{7,3},{8,12},{9,5},{1... | collective-permute-start | bytes 6291464 | tf_op jit(solution)/shard_map/ppermute | solution.py:37
  72.0 27.6 %collective-permute-start.11 = (bf16[128,4096]{1,0:T(8,128)(2,1)S(1)}, bf16[128,4096]{1,0:T(8,128)(2,1)S(1)}, u32[]{:S(2)}, u32[]{:S(2)}) collective-permute-start(bf16[128,4096]{1,0:T(8,128)(2,1)S(1)} %collective-permute-done.1.refs_3_.refs_0_), channel_id=1, source_target_pairs={{0,2},{1,3},{2,0},{3,1},{4,6},{5,7},{6,4},{7,5},{8,10},{9,11},{10,... | collective-permute-start | bytes 3145736 | tf_op jit(solution)/shard_map/ppermute | solution.py:37
  72.9 26.7 %collective-permute-start.10 = (bf16[128,4096]{1,0:T(8,128)(2,1)S(1)}, bf16[128,4096]{1,0:T(8,128)(2,1)S(1)}, u32[]{:S(2)}, u32[]{:S(2)}) collective-permute-start(bf16[128,4096]{1,0:T(8,128)(2,1)S(1)} %collective-permute-done.5.refs_0_.refs_1_), channel_id=1, source_target_pairs={{0,66},{1,67},{2,64},{3,65},{4,70},{5,71},{6,68},{7,69},{8,74},{9,... | collective-permute-start | bytes 3145736 | tf_op jit(solution)/shard_map/ppermute | solution.py:37
  80.4 19.3 %collective-permute-start.12 = (bf16[128,4096]{1,0:T(8,128)(2,1)S(1)}, bf16[128,4096]{1,0:T(8,128)(2,1)S(1)}, u32[]{:S(2)}, u32[]{:S(2)}) collective-permute-start(bf16[128,4096]{1,0:T(8,128)(2,1)S(1)} %collective-permute-done.4), channel_id=1, source_target_pairs={{0,1},{1,0},{2,3},{3,2},{4,5},{5,4},{6,7},{7,6},{8,9},{9,8},{10,11... | collective-permute-start | bytes 3145736 | tf_op jit(solution)/shard_map/ppermute | solution.py:37
  80.5 22.2 %collective-permute-start.14 = (bf16[128,4096]{1,0:T(8,128)(2,1)S(1)}, bf16[128,4096]{1,0:T(8,128)(2,1)S(1)}, u32[]{:S(2)}, u32[]{:S(2)}) collective-permute-start(bf16[128,4096]{1,0:T(8,128)(2,1)S(1)} %collective-permute-done.3.refs_6_), channel_id=1, source_target_pairs={{0,16},{1,49},{2,18},{3,51},{4,20},{5,53},{6,22},{7,55},{8,24},{9,... | collective-permute-start | bytes 3145736 | tf_op jit(solution)/shard_map/ppermute | solution.py:37
  99.8 2.0 %collective-permute-start.15 = (bf16[64,4096]{1,0:T(8,128)(2,1)S(1)}, bf16[64,4096]{1,0:T(8,128)(2,1)S(1)}, u32[]{:S(2)}, u32[]{:S(2)}) collective-permute-start(bf16[64,4096]{1,0:T(8,128)(2,1)S(1)} %get-tuple-element.110), channel_id=1, source_target_pairs={{0,1},{1,0},{2,3},{3,2},{4,5},{5,4},{6,7},{7,6},{8,9},{9,8},{10,11... | collective-permute-start | bytes 1572872 | tf_op jit(solution)/shard_map/ppermute | solution.py:37
  99.9 2.6 %collective-permute-start.16 = (bf16[64,4096]{1,0:T(8,128)(2,1)S(1)}, bf16[64,4096]{1,0:T(8,128)(2,1)S(1)}, u32[]{:S(2)}, u32[]{:S(2)}) collective-permute-start(bf16[64,4096]{1,0:T(8,128)(2,1)S(1)} %get-tuple-element.111), channel_id=1, source_target_pairs={{0,1},{1,0},{2,3},{3,2},{4,5},{5,4},{6,7},{7,6},{8,9},{9,8},{10,11... | collective-permute-start | bytes 1572872 | tf_op jit(solution)/shard_map/ppermute | solution.py:37
  100.4 2.9 %collective-permute-start.17 = (bf16[64,4096]{1,0:T(8,128)(2,1)S(1)}, bf16[64,4096]{1,0:T(8,128)(2,1)S(1)}, u32[]{:S(2)}, u32[]{:S(2)}) collective-permute-start(bf16[64,4096]{1,0:T(8,128)(2,1)S(1)} %get-tuple-element.114), channel_id=1, source_target_pairs={{0,1},{1,0},{2,3},{3,2},{4,5},{5,4},{6,7},{7,6},{8,9},{9,8},{10,11... | collective-permute-start | bytes 1572872 | tf_op jit(solution)/shard_map/ppermute | solution.py:37
  100.7 3.4 %collective-permute-start.18 = (bf16[64,4096]{1,0:T(8,128)(2,1)S(1)}, bf16[64,4096]{1,0:T(8,128)(2,1)S(1)}, u32[]{:S(2)}, u32[]{:S(2)}) collective-permute-start(bf16[64,4096]{1,0:T(8,128)(2,1)S(1)} %get-tuple-element.115), channel_id=1, source_target_pairs={{0,1},{1,0},{2,3},{3,2},{4,5},{5,4},{6,7},{7,6},{8,9},{9,8},{10,11... | collective-permute-start | bytes 1572872 | tf_op jit(solution)/shard_map/ppermute | solution.py:37
  104.1 5.7 %collective-permute-start.19 = (bf16[256,4096]{1,0:T(8,128)(2,1)S(1)}, bf16[256,4096]{1,0:T(8,128)(2,1)S(1)}, u32[]{:S(2)}, u32[]{:S(2)}) collective-permute-start(bf16[256,4096]{1,0:T(8,128)(2,1)S(1)} %collective-permute-done.13.refs_1_), channel_id=1, source_target_pairs={{0,1},{1,0},{2,3},{3,2},{4,5},{5,4},{6,7},{7,6},{8,9},{9,8},{10,11... | collective-permute-start | bytes 6291464 | tf_op jit(solution)/shard_map/ppermute | solution.py:37
  104.2 16.0 %collective-permute-start.20 = (bf16[128,4096]{1,0:T(8,128)(2,1)S(1)}, bf16[128,4096]{1,0:T(8,128)(2,1)S(1)}, u32[]{:S(2)}, u32[]{:S(2)}) collective-permute-start(bf16[128,4096]{1,0:T(8,128)(2,1)S(1)} %collective-permute-done.11.refs_0_.refs_1_), channel_id=1, source_target_pairs={{0,4},{1,13},{2,6},{3,15},{4,8},{5,1},{6,10},{7,3},{8,12},{9,5},{1... | collective-permute-start | bytes 3145736 | tf_op jit(solution)/shard_map/ppermute | solution.py:37
  105.2 16.0 %collective-permute-start.23 = (bf16[128,4096]{1,0:T(8,128)(2,1)S(1)}, bf16[128,4096]{1,0:T(8,128)(2,1)S(1)}, u32[]{:S(2)}, u32[]{:S(2)}) collective-permute-start(bf16[128,4096]{1,0:T(8,128)(2,1)S(1)} %collective-permute-done.10.refs_0_.refs_4_), channel_id=1, source_target_pairs={{0,16},{1,49},{2,18},{3,51},{4,20},{5,53},{6,22},{7,55},{8,24},{9,... | collective-permute-start | bytes 3145736 | tf_op jit(solution)/shard_map/ppermute | solution.py:37
  106.3 27.2 %collective-permute-start.25 = (bf16[128,4096]{1,0:T(8,128)(2,1)S(1)}, bf16[128,4096]{1,0:T(8,128)(2,1)S(1)}, u32[]{:S(2)}, u32[]{:S(2)}) collective-permute-start(bf16[128,4096]{1,0:T(8,128)(2,1)S(1)} %collective-permute-done.14.refs_4_), channel_id=1, source_target_pairs={{0,64},{1,65},{2,66},{3,67},{4,68},{5,69},{6,70},{7,71},{8,72},{9,... | collective-permute-start | bytes 3145736 | tf_op jit(solution)/shard_map/ppermute | solution.py:37
  113.8 19.7 %collective-permute-start.24 = (bf16[128,4096]{1,0:T(8,128)(2,1)S(1)}, bf16[128,4096]{1,0:T(8,128)(2,1)S(1)}, u32[]{:S(2)}, u32[]{:S(2)}) collective-permute-start(bf16[128,4096]{1,0:T(8,128)(2,1)S(1)} %shard_map.48), channel_id=1, source_target_pairs={{0,16},{1,49},{2,18},{3,51},{4,20},{5,53},{6,22},{7,55},{8,24},{9,... | collective-permute-start | bytes 3145736 | tf_op jit(solution)/shard_map/ppermute | solution.py:37
  120.3 5.5 %collective-permute-start.21 = (bf16[64,4096]{1,0:T(8,128)(2,1)S(1)}, bf16[64,4096]{1,0:T(8,128)(2,1)S(1)}, u32[]{:S(2)}, u32[]{:S(2)}) collective-permute-start(bf16[64,4096]{1,0:T(8,128)(2,1)S(1)} %get-tuple-element.137), channel_id=1, source_target_pairs={{0,1},{1,0},{2,3},{3,2},{4,5},{5,4},{6,7},{7,6},{8,9},{9,8},{10,11... | collective-permute-start | bytes 1572872 | tf_op jit(solution)/shard_map/ppermute | solution.py:37
  120.4 5.4 %collective-permute-start.22 = (bf16[64,4096]{1,0:T(8,128)(2,1)S(1)}, bf16[64,4096]{1,0:T(8,128)(2,1)S(1)}, u32[]{:S(2)}, u32[]{:S(2)}) collective-permute-start(bf16[64,4096]{1,0:T(8,128)(2,1)S(1)} %get-tuple-element.138), channel_id=1, source_target_pairs={{0,1},{1,0},{2,3},{3,2},{4,5},{5,4},{6,7},{7,6},{8,9},{9,8},{10,11... | collective-permute-start | bytes 1572872 | tf_op jit(solution)/shard_map/ppermute | solution.py:37
  133.6 2.0 %collective-permute-start.26 = (bf16[64,4096]{1,0:T(8,128)(2,1)S(1)}, bf16[64,4096]{1,0:T(8,128)(2,1)S(1)}, u32[]{:S(2)}, u32[]{:S(2)}) collective-permute-start(bf16[64,4096]{1,0:T(8,128)(2,1)S(1)} %get-tuple-element.153), channel_id=1, source_target_pairs={{0,1},{1,0},{2,3},{3,2},{4,5},{5,4},{6,7},{7,6},{8,9},{9,8},{10,11... | collective-permute-start | bytes 1572872 | tf_op jit(solution)/shard_map/ppermute | solution.py:37
  133.7 2.6 %collective-permute-start.27 = (bf16[64,4096]{1,0:T(8,128)(2,1)S(1)}, bf16[64,4096]{1,0:T(8,128)(2,1)S(1)}, u32[]{:S(2)}, u32[]{:S(2)}) collective-permute-start(bf16[64,4096]{1,0:T(8,128)(2,1)S(1)} %get-tuple-element.154), channel_id=1, source_target_pairs={{0,1},{1,0},{2,3},{3,2},{4,5},{5,4},{6,7},{7,6},{8,9},{9,8},{10,11... | collective-permute-start | bytes 1572872 | tf_op jit(solution)/shard_map/ppermute | solution.py:37
  143.5 1.3 collective-permute-start.28
  144.7 3.7 %collective-permute-start.29 = (f32[16,128]{1,0:T(8,128)S(1)}, f32[16,128]{1,0:T(8,128)S(1)}, u32[]{:S(2)}, u32[]{:S(2)}) collective-permute-start(f32[16,128]{1,0:T(8,128)S(1)} %max.12), channel_id=1, source_target_pairs={{0,2},{1,3},{2,0},{3,1},{4,6},{5,7},{6,4},{7,5},{8,10},{9,11},{10,... | collective-permute-start | bytes 24584 | tf_op jit(solution)/shard_map/ppermute | solution.py:37
  148.4 3.7 %collective-permute-start.30 = (f32[16,128]{1,0:T(8,128)S(1)}, f32[16,128]{1,0:T(8,128)S(1)}, u32[]{:S(2)}, u32[]{:S(2)}) collective-permute-start(f32[16,128]{1,0:T(8,128)S(1)} %max.13), channel_id=1, source_target_pairs={{0,4},{1,5},{2,6},{3,7},{4,0},{5,1},{6,2},{7,3},{8,12},{9,13},{10,... | collective-permute-start | bytes 24584 | tf_op jit(solution)/shard_map/ppermute | solution.py:37
  152.0 4.9 %collective-permute-start.31 = (f32[16,128]{1,0:T(8,128)S(1)}, f32[16,128]{1,0:T(8,128)S(1)}, u32[]{:S(2)}, u32[]{:S(2)}) collective-permute-start(f32[16,128]{1,0:T(8,128)S(1)} %max.14), channel_id=1, source_target_pairs={{0,12},{1,13},{2,14},{3,15},{4,8},{5,9},{6,10},{7,11},{8,4},{9,5},... | collective-permute-start | bytes 24584 | tf_op jit(solution)/shard_map/ppermute | solution.py:37
  (1 other events, 31.4 us)

commit v3 on v2

--- a/solution.py
+++ b/solution.py
@@ -45,22 +45,22 @@
     pick = jnp.where(hit, 1.0, 0.0).astype(BF16)
     step = 1024
     for s in range(0, width, step):
-        out_ref[:, s : s + step] = jnp.dot(
-            pick, items_ref[:, s : s + step], preferred_element_type=F32
-        ).astype(BF16)
+        part = jnp.dot(pick, items_ref[:, s : s + step], preferred_element_type=F32)
+        out_ref[:, s // 128 : (s + step) // 128, :] = part.reshape(count, 8, 128).astype(BF16)
     slot = jnp.sum(jnp.where(hit, (pos % count).astype(F32), 0.0), axis=1, keepdims=True)
-    out_ref[:, width:] = jnp.broadcast_to(slot, (count, out_ref.shape[1] - width)).astype(BF16)
+    out_ref[:, width // 128 :, :] = jnp.broadcast_to(slot[:, :, None], (count, 8, 128)).astype(BF16)
 
 
 def place_kernel(in_ref, out_ref):
     count, width = out_ref.shape
-    slot = in_ref[:, width : width + 128].astype(F32)
+    slot = in_ref[:, width // 128, :].astype(F32)
     lane = lax.broadcasted_iota(jnp.int32, (count, count), 1).astype(F32)
     pick = jnp.where(slot == lane, 1.0, 0.0).astype(BF16)
     step = 1024
     for s in range(0, width, step):
+        part = in_ref[:, s // 128 : (s + step) // 128, :].astype(F32).reshape(count, step)
         out_ref[:, s : s + step] = lax.dot_general(
-            pick, in_ref[:, s : s + step], (((0,), (0,)), ((), ())), preferred_element_type=F32
+            pick, part.astype(BF16), (((0,), (0,)), ((), ())), preferred_element_type=F32
         ).astype(BF16)
 
 
@@ -140,7 +140,7 @@
     return jnp.transpose(jnp.broadcast_to(column, (128, 128)))[:1, :]
 
 
-def make_block_kernel(row_sizes, col_sizes, fresh_rows, fresh_cols, diagonal, last):
+def make_block_kernel(line, row_sizes, col_sizes, fresh_rows, fresh_cols, diagonal, last):
     n_rb, n_cb = sum(row_sizes) // 128, sum(col_sizes) // 128
     tile = 512
     per_tile = tile // 128
@@ -218,13 +218,13 @@
                 else:
                     inv = row_inv[part][span, :]
                     top = best_in[part][span, :]
-                a = where[r]
+                a = where[line, r]
                 here = pl.ds(pl.multiple_of(a * 128, 128), 128)
                 for (first, ref, inv_ref), product in zip(groups, products):
                     for lane in range(0, ref.shape[0], 128):
                         lanes = slice(lane, lane + 128)
                         scaled = product[128 * k : 128 * k + 128, lanes] * inv * inv_ref[:1, lanes]
-                        there = where[n_rb + (first + lane) // 128]
+                        there = where[line, n_rb + (first + lane) // 128]
                         out_ref[here, pl.ds(pl.multiple_of(there * 128, 128), 128)] = scaled.astype(
                             BF16
                         )
@@ -244,6 +244,7 @@
 
 
 def block_call(where, rows, cols, out, row_inv=None, col_inv=None, best=None, last=False):
+    where, line = where
     fresh_rows, fresh_cols = row_inv is None, col_inv is None
     row_sizes, col_sizes = [r.shape[0] for r in rows], [c.shape[0] for c in cols]
     n_rows, n_cols = sum(row_sizes), sum(col_sizes)
@@ -275,7 +276,7 @@
         out_shape.append(jax.ShapeDtypeStruct((n_cols, width), BF16))
         out_shape.append(jax.ShapeDtypeStruct((8, n_cols), F32))
     return pl.pallas_call(
-        make_block_kernel(row_sizes, col_sizes, fresh_rows, fresh_cols, out is None, last),
+        make_block_kernel(line, row_sizes, col_sizes, fresh_rows, fresh_cols, out is None, last),
         out_shape=out_shape,
         in_specs=in_specs,
         out_specs=[vmem_spec] * len(out_shape),
@@ -333,7 +334,7 @@
     vmem_spec = pl.BlockSpec(memory_space=pltpu.VMEM)
     packed = pl.pallas_call(
         pack_kernel,
-        out_shape=jax.ShapeDtypeStruct((count, width + 1024), BF16),
+        out_shape=jax.ShapeDtypeStruct((count, width // 128 + 8, 128), BF16),
         in_specs=[vmem_spec, vmem_spec],
         out_specs=vmem_spec,
     )(position_of.reshape(1, count), items)
@@ -363,10 +364,9 @@
 
     def places(rows, cols):
         flat_list = sum([rows_at[r] for r in rows], []) + sum([cols_at[c] for c in cols], [])
-        return jnp.stack(flat_list).astype(jnp.int32)
-
-    packed, *where = fence(
-        packed,
+        return flat_list
+
+    lists = [
         places([0], [0]),
         places([1], [0]),
         places([0, 1], [1]),
@@ -374,10 +374,13 @@
         places([0, 1, 2], [2]),
         places([3], [0, 1, 2]),
         places([0, 1, 2, 3], [3]),
-    )
+    ]
+    table = jnp.stack([jnp.stack(p + [p[0]] * (18 - len(p))) for p in lists]).astype(jnp.int32)
+    packed, table = fence(packed, table)
+    where = [(table, n) for n in range(len(lists))]
     arrived = lax.all_to_all(
-        packed.reshape(count, -1, 128), AXES, split_axis=0, concat_axis=0, tiled=True
-    ).reshape(count, -1)
+        packed, AXES, split_axis=0, concat_axis=0, tiled=True
+    )
     own = pl.pallas_call(
         place_kernel,
         out_shape=jax.ShapeDtypeStruct((count, width), BF16),
@@ -409,14 +412,12 @@
     z_a, z_b, best_2 = fence(z_a, z_b, best_2)
     z_2, z_b_c = send(z_a, up_z), send(z_b, cross)
     far, p_a, z_b_c, x_2 = fence(far, p_a, z_b_c, x_2)
-    far_c, p_a_c = swap(far), swap(p_a)
+    far_c = swap(far)
     (far_c,) = moved(far_c, [count])
-    x_2, p_a, far, z_2, far_c, z_b_c, best_2, *p_a_c = fence(
-        x_2, p_a, far, z_2, far_c, z_b_c, best_2, *p_a_c
-    )
+    x_2, p_a, far, z_2, far_c, z_b_c, best_2 = fence(x_2, p_a, far, z_2, far_c, z_b_c, best_2)
 
     f_a, f_2, p_2 = send(far, up_z), send(z_2, {"yh": 1}), send(p_a, up_x)
-    x_2_c = send(x_2, cross)
+    x_2_c, p_a_c = fence(send(x_2, cross), send(p_a, cross))
     out, best_1, best_2, cols_2, col_inv_2 = block_call(
         where[2], [rows_1, rows_2], [z_b_c, z_2], out, row_inv=[inv_1, inv_2], best=[best_1, best_2]
     )
@@ -437,7 +438,7 @@
     )
     out, best_4, rows_4, inv_4 = block_call(
         where[5],
-        [p_a, *p_a_c, p_2, *p_2_c],
+        [p_a, p_a_c, p_2, *p_2_c],
         [cols_1, cols_2, cols_3],
         out,
         col_inv=[col_inv_1, col_inv_2, col_inv_3],
@@ -455,8 +456,8 @@
     )
 
     best = jnp.maximum(best, send(best, cross))
-    best = jnp.maximum(best, send(best, near))
-    best = jnp.maximum(best, send(best, {"x": "even"}))
+    others = [send(best, way) for way in (near, {"x": "even"}, {"yl": 1, "x": "even"})]
+    best = jnp.maximum(jnp.maximum(best, others[0]), jnp.maximum(others[1], others[2]))
     best, out = fence(best, store(out))
     best = jnp.maximum(best, send(best, {"x": "odd"}))
     return out, best.reshape(-1)

time: 158 us -> 153 us (0.968)
  waiting for transfers between devices: 67.8 us -> 60.6 us
  starting transfers between devices: 12.6 us -> 16.6 us
  local copies, waits for them, and re-layouts: 3.5 us -> 0.72 us
    ppermute x32, waiting for transfers between devices: 67.8 us -> 60.6 us  [send(): return lax.ppermute(value, AXES, pairs)]
    ppermute x32, starting transfers between devices: 12.6 us -> 16.6 us  [send(): return lax.ppermute(value, AXES, pairs)]
    unnamed x4 -> x2, local copies, waits for them, and re-layouts: 2.88 us -> 0.01 us
  transfers between devices with their start and end apart: 32 -> 32, of which waited for: 18 -> 14; matrix products, arithmetic and copies ran while one was open for 0% -> 0% of each run, Pallas kernels for 17% -> 17%
where the time goes in v3:
time: 153 us
  waiting for transfers between devices  60.6 us (40%)
  Pallas kernels  40.2 us (26%)
  blocking collectives  32.9 us (22%)
  starting transfers between devices  16.6 us (11%)
    ppermute x32, waiting for transfers between devices, send(): return lax.ppermute(value, AXES, pairs)  60.6 us
    all_to_all x1, blocking collectives, per_device(): lax.all_to_all(packed, AXES, split_axis=0, concat_axis=0, tiled=True)  32.9 us
    pallas_call x7, Pallas kernels, block_call(): pl.pallas_call(make_block_kernel(line, row_sizes, col_sizes, fresh_rows,...  31.3 us
    ppermute x32, starting transfers between devices, send(): return lax.ppermute(value, AXES, pairs)  16.6 us
    pallas_call x1, Pallas kernels, per_device(): pl.pallas_call(place_kernel, out_shape=jax.ShapeDtypeStruct((count, width...  3.17 us
  transfers between devices with their start and end apart: 32, of which 14 were waited for; matrix products, arithmetic and copies ran while one was open for 0% of the time, Pallas kernels for 17%

profile of v3, /device:TPU:0, one launch (start us, length us, event | category | flops | bytes accessed | tf_op | source)
XLA Modules:
  0.0 152.9 jit_solution(9366990602591509732)
XLA Ops:
  1.6 3.0 %shard_map.41 = bf16[128,40,128]{2,1,0:T(8,128)(2,1)} custom-call(s32[1,128]{1,0:T(1,128)} %bitcast.41, bf16[128,4096]{1,0:T(8,128)(2,1)} %items_ref.1), custom_call_target="tpu_custom_call" | custom-call | tf_op jit(solution)/shard_map/pallas_call | solution.py:335
  4.7 32.9 %all_to_all.5.in_ref = bf16[128,40,128]{2,1,0:T(8,128)(2,1)} all-to-all(bf16[128,40,128]{2,1,0:T(8,128)(2,1)} %shard_map.41), channel_id=1, replica_groups=mesh['gr'=8,'gc'=16] {'gr','gc'}, dimensions={0} | all-to-all | bytes 2621440 | tf_op jit(solution)/shard_map/all_to_all | solution.py:381
  37.6 3.2 %shard_map.42.refs_1_.refs_5_ = bf16[128,4096]{1,0:T(8,128)(2,1)} custom-call(bf16[128,40,128]{2,1,0:T(8,128)(2,1)} %all_to_all.5.in_ref), custom_call_target="tpu_custom_call" | custom-call | tf_op jit(solution)/shard_map/pallas_call | solution.py:384
  41.9 1.8 %collective-permute-done.refs_2_ = bf16[128,4096]{1,0:T(8,128)(2,1)S(1)} collective-permute-done((bf16[128,4096]{1,0:T(8,128)(2,1)}, bf16[128,4096]{1,0:T(8,128)(2,1)S(1)}, u32[]{:S(2)}, u32[]{:S(2)}) %collective-permute-start) | collective-permute-done | bytes 1048608 | tf_op jit(solution)/shard_map/ppermute | solution.py:37
  43.8 22.8 %collective-permute-done.5.refs_0_.refs_1_ = bf16[128,4096]{1,0:T(8,128)(2,1)S(1)} collective-permute-done((bf16[128,4096]{1,0:T(8,128)(2,1)}, bf16[128,4096]{1,0:T(8,128)(2,1)S(1)}, u32[]{:S(2)}, u32[]{:S(2)}) %collective-permute-start.5) | collective-permute-done | bytes 1048608 | tf_op jit(solution)/shard_map/ppermute | solution.py:37
  67.3 1.4 collective-permute-done.6.refs_2_.refs_1_
  68.7 0.7 collective-permute-done.7.refs_3_.refs_2_
  70.2 0.9 collective-permute-start.11
  71.2 1.0 collective-permute-start.10
  72.2 3.6 %shard_map.44 = (bf16[2048,1024]{1,0:T(8,128)(2,1)S(1)}, f32[512,128]{1,0:T(8,128)S(1)}, bf16[512,4096]{1,0:T(8,128)(2,1)S(1)}, f32[512,128]{1,0:T(8,128)S(1)}, ...) custom-call(s32[7,18]{1,0:T(8,128)S(1)} %stack.116.refs_0_, bf16[128,4096]{1,0:T(8,128)(2,1)S(1)} %copy-done, ...), custom_call_target="tpu_custom_call" | custom-call | flops 134217728 | bytes 262144 | tf_op jit(solution)/shard_map/pallas_call | solution.py:278
  75.8 2.9 %shard_map.45 = (bf16[2048,1024]{1,0:T(8,128)(2,1)S(1)}, f32[512,128]{1,0:T(8,128)S(1)}, bf16[512,4096]{1,0:T(8,128)(2,1)S(1)}, f32[512,128]{1,0:T(8,128)S(1)}) custom-call(s32[7,18]{1,0:T(8,128)S(1)} %stack.116.refs_0_, bf16[128,4096]{1,0:T(8,128)(2,1)S(1)} %collective-permute-done.5.refs_0_.refs_1_, ...), custom_call_target="tpu_custom_call", output_to_operand_aliasing={{0}: (8, {})} | custom-call | flops 134217728 | bytes 262144 | tf_op jit(solution)/shard_map/pallas_call | solution.py:278
  78.8 1.3 collective-permute-start.14
  80.1 17.8 %collective-permute-done.10.refs_0_.refs_4_ = bf16[128,4096]{1,0:T(8,128)(2,1)S(1)} collective-permute-done((bf16[128,4096]{1,0:T(8,128)(2,1)S(1)}, bf16[128,4096]{1,0:T(8,128)(2,1)S(1)}, u32[]{:S(2)}, u32[]{:S(2)}) %collective-permute-start.10) | collective-permute-done | bytes 1048608 | tf_op jit(solution)/shard_map/ppermute | solution.py:37
  98.6 1.4 collective-permute-done.15.refs_0_
  101.4 0.9 collective-permute-start.19
  102.4 1.1 collective-permute-start.22
  103.5 3.6 %shard_map.49 = (bf16[2048,1024]{1,0:T(8,128)(2,1)S(1)}, f32[512,128]{1,0:T(8,128)S(1)}, f32[512,128]{1,0:T(8,128)S(1)}, bf16[256,4096]{1,0:T(8,128)(2,1)S(1)}, f32[8,256]{1,0:T(8,128)S(1)}) custom-call(s32[7,18]{1,0:T(8,128)S(1)} %stack.116.refs_0_, bf16[512,4096]{1,0:T(8,128)(2,1)S(1)} %get-tuple-element.84.refs_1_, ...), custom_call_target="tpu_custom_call", output_to_operand_aliasing={{0}: (9, {})} | custom-call | flops 268435456 | bytes 524288 | tf_op jit(solution)/shard_map/pallas_call | solution.py:278
  107.1 4.1 %shard_map.50 = (bf16[2048,1024]{1,0:T(8,128)(2,1)S(1)}, f32[512,128]{1,0:T(8,128)S(1)}, bf16[512,4096]{1,0:T(8,128)(2,1)S(1)}, f32[512,128]{1,0:T(8,128)S(1)}) custom-call(s32[7,18]{1,0:T(8,128)S(1)} %stack.116.refs_0_, bf16[256,4096]{1,0:T(8,128)(2,1)S(1)} %collective-permute-done.13.refs_1_, ...), custom_call_target="tpu_custom_call", output_to_operand_aliasing={{0}: (7, {})} | custom-call | flops 268435456 | bytes 524288 | tf_op jit(solution)/shard_map/pallas_call | solution.py:278
  111.1 1.2 collective-permute-start.23
  112.4 5.0 %collective-permute-done.19.refs_0_.refs_3_ = bf16[128,4096]{1,0:T(8,128)(2,1)S(1)} collective-permute-done((bf16[128,4096]{1,0:T(8,128)(2,1)S(1)}, bf16[128,4096]{1,0:T(8,128)(2,1)S(1)}, u32[]{:S(2)}, u32[]{:S(2)}) %collective-permute-start.19) | collective-permute-done | bytes 1048608 | tf_op jit(solution)/shard_map/ppermute | solution.py:37
  118.4 4.7 %shard_map.52 = (bf16[2048,1024]{1,0:T(8,128)(2,1)S(1)}, f32[512,128]{1,0:T(8,128)S(1)}, f32[512,128]{1,0:T(8,128)S(1)}, f32[512,128]{1,0:T(8,128)S(1)}, bf16[25...) custom-call(s32[7,18]{1,0:T(8,128)S(1)} %stack.116.refs_0_, ...), custom_call_target="tpu_custom_call", output_to_operand_aliasing={{0}: (12, {})} | custom-call | flops 402653184 | bytes 786432 | tf_op jit(solution)/shard_map/pallas_call | solution.py:278
  123.1 5.3 %shard_map.53 = (bf16[2048,1024]{1,0:T(8,128)(2,1)S(1)}, f32[512,128]{1,0:T(8,128)S(1)}, bf16[512,4096]{1,0:T(8,128)(2,1)S(1)}, f32[512,128]{1,0:T(8,128)S(1)}) custom-call(s32[7,18]{1,0:T(8,128)S(1)} %stack.116.refs_0_, bf16[128,4096]{1,0:T(8,128)(2,1)S(1)} %collective-permute-done.11.refs_1_, ...), custom_call_target="tpu_custom_call", output_to_operand_aliasing={{0}: (12, {})} | custom-call | flops 402653184 | bytes 786432 | tf_op jit(solution)/shard_map/pallas_call | solution.py:278
  128.4 2.1 %collective-permute-done.24.refs_7_ = bf16[128,4096]{1,0:T(8,128)(2,1)S(1)} collective-permute-done((bf16[128,4096]{1,0:T(8,128)(2,1)S(1)}, bf16[128,4096]{1,0:T(8,128)(2,1)S(1)}, u32[]{:S(2)}, u32[]{:S(2)}) %collective-permute-start.24) | collective-permute-done | bytes 1048608 | tf_op jit(solution)/shard_map/ppermute | solution.py:37
  131.2 1.4 collective-permute-done.25.refs_5_
  132.6 0.7 collective-permute-done.26.refs_6_
  133.3 7.2 %shard_map.55 = (bf16[2048,1024]{1,0:T(8,128)(2,1)S(1)}, f32[16,128]{1,0:T(8,128)S(1)}, bf16[256,4096]{1,0:T(8,128)(2,1)}, f32[8,256]{1,0:T(8,128)}) custom-call(s32[7,18]{1,0:T(8,128)S(1)} %stack.116.refs_0_, bf16[512,4096]{1,0:T(8,128)(2,1)S(1)} %get-tuple-element.84.refs_1_, ...), custom_call_target="tpu_custom_call", output_to_operand_aliasing={{0}: (16, {})} | custom-call | flops 536870912 | bytes 1048576 | tf_op jit(solution)/shard_map/pallas_call | solution.py:278
  140.7 1.0 collective-permute-done.27
  141.8 1.0 collective-permute-start.29
  142.7 2.5 %collective-permute-start.28 = (f32[16,128]{1,0:T(8,128)S(1)}, f32[16,128]{1,0:T(8,128)S(1)}, u32[]{:S(2)}, u32[]{:S(2)}) collective-permute-start(f32[16,128]{1,0:T(8,128)S(1)} %max.15), channel_id=1, source_target_pairs={{0,2},{1,3},{2,0},{3,1},{4,6},{5,7},{6,4},{7,5},{8,10},{9,11},{10,... | collective-permute-start | bytes 24584 | tf_op jit(solution)/shard_map/ppermute | solution.py:37
  145.2 2.0 %shard_map.56 = bf16[2048,1024]{1,0:T(8,128)(2,1)} custom-call(bf16[2048,1024]{1,0:T(8,128)(2,1)S(1)} %get-tuple-element.147.held_ref), custom_call_target="tpu_custom_call" | custom-call | bytes 8388608 | tf_op jit(solution)/shard_map/pallas_call | solution.py:312
  147.3 1.5 collective-permute-start.31
  148.9 3.4 %collective-permute-done.31 = f32[16,128]{1,0:T(8,128)S(1)} collective-permute-done((f32[16,128]{1,0:T(8,128)S(1)}, f32[16,128]{1,0:T(8,128)S(1)}, u32[]{:S(2)}, u32[]{:S(2)}) %collective-permute-start.31) | collective-permute-done | bytes 8224 | tf_op jit(solution)/shard_map/ppermute | solution.py:37
  (62 shorter events, 8.1 us)
Async XLA Ops:
  40.8 2.9 %collective-permute-start = (bf16[128,4096]{1,0:T(8,128)(2,1)}, bf16[128,4096]{1,0:T(8,128)(2,1)S(1)}, u32[]{:S(2)}, u32[]{:S(2)}) collective-permute-start(bf16[128,4096]{1,0:T(8,128)(2,1)} %shard_map.42.refs_1_.refs_5_), channel_id=1, source_target_pairs={{0,1},{1,0},{2,3},{3,2},{4,5},{5,4},{6,7},{7,6},{8,9},{9,8},{10,11... | collective-permute-start | bytes 3145736 | tf_op jit(solution)/shard_map/ppermute | solution.py:37
  40.8 25.8 %collective-permute-start.5 = (bf16[128,4096]{1,0:T(8,128)(2,1)}, bf16[128,4096]{1,0:T(8,128)(2,1)S(1)}, u32[]{:S(2)}, u32[]{:S(2)}) collective-permute-start(bf16[128,4096]{1,0:T(8,128)(2,1)} %shard_map.42.refs_1_.refs_5_), channel_id=1, source_target_pairs={{0,2},{1,3},{2,0},{3,1},{4,6},{5,7},{6,4},{7,5},{8,10},{9,11},{10,... | collective-permute-start | bytes 3145736 | tf_op jit(solution)/shard_map/ppermute | solution.py:37
  41.3 25.4 %collective-permute-start.3 = (bf16[128,4096]{1,0:T(8,128)(2,1)}, bf16[128,4096]{1,0:T(8,128)(2,1)S(1)}, u32[]{:S(2)}, u32[]{:S(2)}) collective-permute-start(bf16[128,4096]{1,0:T(8,128)(2,1)} %shard_map.42.refs_1_.refs_5_), channel_id=1, source_target_pairs={{0,16},{1,49},{2,18},{3,51},{4,20},{5,53},{6,22},{7,55},{8,24},{9,... | collective-permute-start | bytes 3145736 | tf_op jit(solution)/shard_map/ppermute | solution.py:37
  41.3 25.9 %collective-permute-start.1 = (bf16[128,4096]{1,0:T(8,128)(2,1)}, bf16[128,4096]{1,0:T(8,128)(2,1)S(1)}, u32[]{:S(2)}, u32[]{:S(2)}) collective-permute-start(bf16[128,4096]{1,0:T(8,128)(2,1)} %shard_map.42.refs_1_.refs_5_), channel_id=1, source_target_pairs={{0,4},{1,13},{2,6},{3,15},{4,8},{5,1},{6,10},{7,3},{8,12},{9,5},{1... | collective-permute-start | bytes 3145736 | tf_op jit(solution)/shard_map/ppermute | solution.py:37
  43.7 25.8 %collective-permute-start.4 = (bf16[128,4096]{1,0:T(8,128)(2,1)S(1)}, bf16[128,4096]{1,0:T(8,128)(2,1)S(1)}, u32[]{:S(2)}, u32[]{:S(2)}) collective-permute-start(bf16[128,4096]{1,0:T(8,128)(2,1)S(1)} %collective-permute-done.refs_2_), channel_id=1, source_target_pairs={{0,16},{1,49},{2,18},{3,51},{4,20},{5,53},{6,22},{7,55},{8,24},{9,... | collective-permute-start | bytes 3145736 | tf_op jit(solution)/shard_map/ppermute | solution.py:37
  43.7 25.8 %collective-permute-start.2 = (bf16[128,4096]{1,0:T(8,128)(2,1)S(1)}, bf16[128,4096]{1,0:T(8,128)(2,1)S(1)}, u32[]{:S(2)}, u32[]{:S(2)}) collective-permute-start(bf16[128,4096]{1,0:T(8,128)(2,1)S(1)} %collective-permute-done.refs_2_), channel_id=1, source_target_pairs={{0,4},{1,13},{2,6},{3,15},{4,8},{5,1},{6,10},{7,3},{8,12},{9,5},{1... | collective-permute-start | bytes 3145736 | tf_op jit(solution)/shard_map/ppermute | solution.py:37
  66.7 2.0 %collective-permute-start.6 = (bf16[64,4096]{1,0:T(8,128)(2,1)S(1)}, bf16[64,4096]{1,0:T(8,128)(2,1)S(1)}, u32[]{:S(2)}, u32[]{:S(2)}) collective-permute-start(bf16[64,4096]{1,0:T(8,128)(2,1)S(1)} %get-tuple-element.78), channel_id=1, source_target_pairs={{0,1},{1,0},{2,3},{3,2},{4,5},{5,4},{6,7},{7,6},{8,9},{9,8},{10,11... | collective-permute-start | bytes 1572872 | tf_op jit(solution)/shard_map/ppermute | solution.py:37
  66.8 2.6 %collective-permute-start.7 = (bf16[64,4096]{1,0:T(8,128)(2,1)S(1)}, bf16[64,4096]{1,0:T(8,128)(2,1)S(1)}, u32[]{:S(2)}, u32[]{:S(2)}) collective-permute-start(bf16[64,4096]{1,0:T(8,128)(2,1)S(1)} %get-tuple-element.79), channel_id=1, source_target_pairs={{0,1},{1,0},{2,3},{3,2},{4,5},{5,4},{6,7},{7,6},{8,9},{9,8},{10,11... | collective-permute-start | bytes 1572872 | tf_op jit(solution)/shard_map/ppermute | solution.py:37
  69.4 6.3 %collective-permute-start.9 = (bf16[128,4096]{1,0:T(8,128)(2,1)S(1)}, bf16[128,4096]{1,0:T(8,128)(2,1)S(1)}, u32[]{:S(2)}, u32[]{:S(2)}) collective-permute-start(bf16[128,4096]{1,0:T(8,128)(2,1)S(1)} %collective-permute-done.2.refs_4_), channel_id=1, source_target_pairs={{0,1},{1,0},{2,3},{3,2},{4,5},{5,4},{6,7},{7,6},{8,9},{9,8},{10,11... | collective-permute-start | bytes 3145736 | tf_op jit(solution)/shard_map/ppermute | solution.py:37
  69.6 6.2 %collective-permute-start.8 = (bf16[128,4096]{1,0:T(8,128)(2,1)S(1)}, bf16[128,4096]{1,0:T(8,128)(2,1)S(1)}, u32[]{:S(2)}, u32[]{:S(2)}) collective-permute-start(bf16[128,4096]{1,0:T(8,128)(2,1)S(1)} %collective-permute-done.1.refs_3_.refs_0_), channel_id=1, source_target_pairs={{0,1},{1,0},{2,3},{3,2},{4,5},{5,4},{6,7},{7,6},{8,9},{9,8},{10,11... | collective-permute-start | bytes 3145736 | tf_op jit(solution)/shard_map/ppermute | solution.py:37
  70.1 27.7 %collective-permute-start.13 = (bf16[256,4096]{1,0:T(8,128)(2,1)S(1)}, bf16[256,4096]{1,0:T(8,128)(2,1)S(1)}, u32[]{:S(2)}, u32[]{:S(2)}) collective-permute-start(bf16[256,4096]{1,0:T(8,128)(2,1)S(1)} %shard_map.46), channel_id=1, source_target_pairs={{0,4},{1,13},{2,6},{3,15},{4,8},{5,1},{6,10},{7,3},{8,12},{9,5},{1... | collective-permute-start | bytes 6291464 | tf_op jit(solution)/shard_map/ppermute | solution.py:37
  70.2 27.6 %collective-permute-start.11 = (bf16[128,4096]{1,0:T(8,128)(2,1)S(1)}, bf16[128,4096]{1,0:T(8,128)(2,1)S(1)}, u32[]{:S(2)}, u32[]{:S(2)}) collective-permute-start(bf16[128,4096]{1,0:T(8,128)(2,1)S(1)} %collective-permute-done.1.refs_3_.refs_0_), channel_id=1, source_target_pairs={{0,2},{1,3},{2,0},{3,1},{4,6},{5,7},{6,4},{7,5},{8,10},{9,11},{10,... | collective-permute-start | bytes 3145736 | tf_op jit(solution)/shard_map/ppermute | solution.py:37
  71.2 26.7 %collective-permute-start.10 = (bf16[128,4096]{1,0:T(8,128)(2,1)S(1)}, bf16[128,4096]{1,0:T(8,128)(2,1)S(1)}, u32[]{:S(2)}, u32[]{:S(2)}) collective-permute-start(bf16[128,4096]{1,0:T(8,128)(2,1)S(1)} %collective-permute-done.5.refs_0_.refs_1_), channel_id=1, source_target_pairs={{0,66},{1,67},{2,64},{3,65},{4,70},{5,71},{6,68},{7,69},{8,74},{9,... | collective-permute-start | bytes 3145736 | tf_op jit(solution)/shard_map/ppermute | solution.py:37
  78.7 19.1 %collective-permute-start.12 = (bf16[128,4096]{1,0:T(8,128)(2,1)S(1)}, bf16[128,4096]{1,0:T(8,128)(2,1)S(1)}, u32[]{:S(2)}, u32[]{:S(2)}) collective-permute-start(bf16[128,4096]{1,0:T(8,128)(2,1)S(1)} %collective-permute-done.4), channel_id=1, source_target_pairs={{0,1},{1,0},{2,3},{3,2},{4,5},{5,4},{6,7},{7,6},{8,9},{9,8},{10,11... | collective-permute-start | bytes 3145736 | tf_op jit(solution)/shard_map/ppermute | solution.py:37
  78.8 22.0 %collective-permute-start.14 = (bf16[128,4096]{1,0:T(8,128)(2,1)S(1)}, bf16[128,4096]{1,0:T(8,128)(2,1)S(1)}, u32[]{:S(2)}, u32[]{:S(2)}) collective-permute-start(bf16[128,4096]{1,0:T(8,128)(2,1)S(1)} %collective-permute-done.3.refs_6_), channel_id=1, source_target_pairs={{0,16},{1,49},{2,18},{3,51},{4,20},{5,53},{6,22},{7,55},{8,24},{9,... | collective-permute-start | bytes 3145736 | tf_op jit(solution)/shard_map/ppermute | solution.py:37
  98.0 2.0 %collective-permute-start.15 = (bf16[64,4096]{1,0:T(8,128)(2,1)S(1)}, bf16[64,4096]{1,0:T(8,128)(2,1)S(1)}, u32[]{:S(2)}, u32[]{:S(2)}) collective-permute-start(bf16[64,4096]{1,0:T(8,128)(2,1)S(1)} %get-tuple-element.99), channel_id=1, source_target_pairs={{0,1},{1,0},{2,3},{3,2},{4,5},{5,4},{6,7},{7,6},{8,9},{9,8},{10,11... | collective-permute-start | bytes 1572872 | tf_op jit(solution)/shard_map/ppermute | solution.py:37
  98.1 2.6 %collective-permute-start.16 = (bf16[64,4096]{1,0:T(8,128)(2,1)S(1)}, bf16[64,4096]{1,0:T(8,128)(2,1)S(1)}, u32[]{:S(2)}, u32[]{:S(2)}) collective-permute-start(bf16[64,4096]{1,0:T(8,128)(2,1)S(1)} %get-tuple-element.100), channel_id=1, source_target_pairs={{0,1},{1,0},{2,3},{3,2},{4,5},{5,4},{6,7},{7,6},{8,9},{9,8},{10,11... | collective-permute-start | bytes 1572872 | tf_op jit(solution)/shard_map/ppermute | solution.py:37
  100.8 6.3 %collective-permute-start.17 = (bf16[256,4096]{1,0:T(8,128)(2,1)S(1)}, bf16[256,4096]{1,0:T(8,128)(2,1)S(1)}, u32[]{:S(2)}, u32[]{:S(2)}) collective-permute-start(bf16[256,4096]{1,0:T(8,128)(2,1)S(1)} %collective-permute-done.13.refs_1_), channel_id=1, source_target_pairs={{0,1},{1,0},{2,3},{3,2},{4,5},{5,4},{6,7},{7,6},{8,9},{9,8},{10,11... | collective-permute-start | bytes 6291464 | tf_op jit(solution)/shard_map/ppermute | solution.py:37
  101.0 6.0 %collective-permute-start.18 = (bf16[128,4096]{1,0:T(8,128)(2,1)S(1)}, bf16[128,4096]{1,0:T(8,128)(2,1)S(1)}, u32[]{:S(2)}, u32[]{:S(2)}) collective-permute-start(bf16[128,4096]{1,0:T(8,128)(2,1)S(1)} %collective-permute-done.11.refs_1_), channel_id=1, source_target_pairs={{0,1},{1,0},{2,3},{3,2},{4,5},{5,4},{6,7},{7,6},{8,9},{9,8},{10,11... | collective-permute-start | bytes 3145736 | tf_op jit(solution)/shard_map/ppermute | solution.py:37
  101.4 16.0 %collective-permute-start.19 = (bf16[128,4096]{1,0:T(8,128)(2,1)S(1)}, bf16[128,4096]{1,0:T(8,128)(2,1)S(1)}, u32[]{:S(2)}, u32[]{:S(2)}) collective-permute-start(bf16[128,4096]{1,0:T(8,128)(2,1)S(1)} %collective-permute-done.11.refs_1_), channel_id=1, source_target_pairs={{0,4},{1,13},{2,6},{3,15},{4,8},{5,1},{6,10},{7,3},{8,12},{9,5},{1... | collective-permute-start | bytes 3145736 | tf_op jit(solution)/shard_map/ppermute | solution.py:37
  102.4 16.0 %collective-permute-start.22 = (bf16[128,4096]{1,0:T(8,128)(2,1)S(1)}, bf16[128,4096]{1,0:T(8,128)(2,1)S(1)}, u32[]{:S(2)}, u32[]{:S(2)}) collective-permute-start(bf16[128,4096]{1,0:T(8,128)(2,1)S(1)} %collective-permute-done.10.refs_0_.refs_4_), channel_id=1, source_target_pairs={{0,16},{1,49},{2,18},{3,51},{4,20},{5,53},{6,22},{7,55},{8,24},{9,... | collective-permute-start | bytes 3145736 | tf_op jit(solution)/shard_map/ppermute | solution.py:37
  103.5 27.0 %collective-permute-start.24 = (bf16[128,4096]{1,0:T(8,128)(2,1)S(1)}, bf16[128,4096]{1,0:T(8,128)(2,1)S(1)}, u32[]{:S(2)}, u32[]{:S(2)}) collective-permute-start(bf16[128,4096]{1,0:T(8,128)(2,1)S(1)} %collective-permute-done.14.refs_4_), channel_id=1, source_target_pairs={{0,64},{1,65},{2,66},{3,67},{4,68},{5,69},{6,70},{7,71},{8,72},{9,... | collective-permute-start | bytes 3145736 | tf_op jit(solution)/shard_map/ppermute | solution.py:37
  111.1 19.3 %collective-permute-start.23 = (bf16[128,4096]{1,0:T(8,128)(2,1)S(1)}, bf16[128,4096]{1,0:T(8,128)(2,1)S(1)}, u32[]{:S(2)}, u32[]{:S(2)}) collective-permute-start(bf16[128,4096]{1,0:T(8,128)(2,1)S(1)} %shard_map.48), channel_id=1, source_target_pairs={{0,16},{1,49},{2,18},{3,51},{4,20},{5,53},{6,22},{7,55},{8,24},{9,... | collective-permute-start | bytes 3145736 | tf_op jit(solution)/shard_map/ppermute | solution.py:37
  117.5 5.6 %collective-permute-start.20 = (bf16[64,4096]{1,0:T(8,128)(2,1)S(1)}, bf16[64,4096]{1,0:T(8,128)(2,1)S(1)}, u32[]{:S(2)}, u32[]{:S(2)}) collective-permute-start(bf16[64,4096]{1,0:T(8,128)(2,1)S(1)} %get-tuple-element.122), channel_id=1, source_target_pairs={{0,1},{1,0},{2,3},{3,2},{4,5},{5,4},{6,7},{7,6},{8,9},{9,8},{10,11... | collective-permute-start | bytes 1572872 | tf_op jit(solution)/shard_map/ppermute | solution.py:37
  117.6 5.5 %collective-permute-start.21 = (bf16[64,4096]{1,0:T(8,128)(2,1)S(1)}, bf16[64,4096]{1,0:T(8,128)(2,1)S(1)}, u32[]{:S(2)}, u32[]{:S(2)}) collective-permute-start(bf16[64,4096]{1,0:T(8,128)(2,1)S(1)} %get-tuple-element.123), channel_id=1, source_target_pairs={{0,1},{1,0},{2,3},{3,2},{4,5},{5,4},{6,7},{7,6},{8,9},{9,8},{10,11... | collective-permute-start | bytes 1572872 | tf_op jit(solution)/shard_map/ppermute | solution.py:37
  130.6 2.0 %collective-permute-start.25 = (bf16[64,4096]{1,0:T(8,128)(2,1)S(1)}, bf16[64,4096]{1,0:T(8,128)(2,1)S(1)}, u32[]{:S(2)}, u32[]{:S(2)}) collective-permute-start(bf16[64,4096]{1,0:T(8,128)(2,1)S(1)} %get-tuple-element.137), channel_id=1, source_target_pairs={{0,1},{1,0},{2,3},{3,2},{4,5},{5,4},{6,7},{7,6},{8,9},{9,8},{10,11... | collective-permute-start | bytes 1572872 | tf_op jit(solution)/shard_map/ppermute | solution.py:37
  130.7 2.6 %collective-permute-start.26 = (bf16[64,4096]{1,0:T(8,128)(2,1)S(1)}, bf16[64,4096]{1,0:T(8,128)(2,1)S(1)}, u32[]{:S(2)}, u32[]{:S(2)}) collective-permute-start(bf16[64,4096]{1,0:T(8,128)(2,1)S(1)} %get-tuple-element.138), channel_id=1, source_target_pairs={{0,1},{1,0},{2,3},{3,2},{4,5},{5,4},{6,7},{7,6},{8,9},{9,8},{10,11... | collective-permute-start | bytes 1572872 | tf_op jit(solution)/shard_map/ppermute | solution.py:37
  140.5 1.3 collective-permute-start.27
  141.8 5.5 %collective-permute-start.30 = (f32[16,128]{1,0:T(8,128)S(1)}, f32[16,128]{1,0:T(8,128)S(1)}, u32[]{:S(2)}, u32[]{:S(2)}) collective-permute-start(f32[16,128]{1,0:T(8,128)S(1)} %max.15), channel_id=1, source_target_pairs={{0,6},{1,7},{2,4},{3,5},{4,2},{5,3},{6,0},{7,1},{8,14},{9,15},{10,... | collective-permute-start | bytes 24584 | tf_op jit(solution)/shard_map/ppermute | solution.py:37
  141.8 5.5 %collective-permute-start.29 = (f32[16,128]{1,0:T(8,128)S(1)}, f32[16,128]{1,0:T(8,128)S(1)}, u32[]{:S(2)}, u32[]{:S(2)}) collective-permute-start(f32[16,128]{1,0:T(8,128)S(1)} %max.15), channel_id=1, source_target_pairs={{0,4},{1,5},{2,6},{3,7},{4,0},{5,1},{6,2},{7,3},{8,12},{9,13},{10,... | collective-permute-start | bytes 24584 | tf_op jit(solution)/shard_map/ppermute | solution.py:37
  142.7 4.6 %collective-permute-start.28 = (f32[16,128]{1,0:T(8,128)S(1)}, f32[16,128]{1,0:T(8,128)S(1)}, u32[]{:S(2)}, u32[]{:S(2)}) collective-permute-start(f32[16,128]{1,0:T(8,128)S(1)} %max.15), channel_id=1, source_target_pairs={{0,2},{1,3},{2,0},{3,1},{4,6},{5,7},{6,4},{7,5},{8,10},{9,11},{10,... | collective-permute-start | bytes 24584 | tf_op jit(solution)/shard_map/ppermute | solution.py:37
  147.3 4.9 %collective-permute-start.31 = (f32[16,128]{1,0:T(8,128)S(1)}, f32[16,128]{1,0:T(8,128)S(1)}, u32[]{:S(2)}, u32[]{:S(2)}) collective-permute-start(f32[16,128]{1,0:T(8,128)S(1)} %maximum_maximum_fusion), channel_id=1, source_target_pairs={{0,12},{1,13},{2,14},{3,15},{4,8},{5,9},{6,10},{7,11},{8,4},{9,5},... | collective-permute-start | bytes 24584 | tf_op jit(solution)/shard_map/ppermute | solution.py:37
  (1 other events, 31.4 us)

commit v4 on v3

--- a/solution.py
+++ b/solution.py
@@ -28,6 +28,8 @@
         for k, v in route.items():
             if v == "ring":
                 v = 1 if c["c"] == 0 else -1
+            elif v == "back":
+                v = -1 if c["c"] == 0 else 1
             elif v == "even":
                 v = 1 if c[k] % 2 == 0 else -1
             elif v == "odd":
@@ -350,8 +352,8 @@
 
     ring = 1 - 2 * core
     rows_at = [
-        [row_at(), row_at(dc=1), row_at(-ring), row_at(-ring, dc=1)],
-        [row_at(dy=1), row_at(dy=1, dc=1), row_at(ring, dc=1), row_at(ring)],
+        [row_at(), row_at(dc=1), row_at(-ring), row_at(ring)],
+        [row_at(dy=1), row_at(dy=1, dc=1), row_at(ring, dc=1), row_at(-ring, dc=1)],
         [row_at(2), row_at(-ring, 1, 1), row_at(2, dc=1), row_at(ring, 1)],
         [row_at(-ring, 1), row_at(ring, 1, 1), row_at(2, 1), row_at(2, 1, 1)],
     ]
@@ -395,7 +397,8 @@
 
     own_c = send(own, cross)
     x_a, z_a, pair = send(own, up_x), send(own, up_z), send(own, near)
-    x_b, z_b = send(own_c, up_x), send(own_c, up_z)
+    own, own_c = fence(own, own_c)
+    x_b, z_b = send(own, {"x": "back"}), send(own, {"z": "back"})
     pair_c = swap(pair)
     own_c, x_a, x_b, z_a, z_b, pair, *pair_c = fence(own_c, x_a, x_b, z_a, z_b, pair, *pair_c)
 
@@ -409,23 +412,21 @@
     out, best_2, rows_2, inv_2 = block_call(
         where[1], [pair, *pair_c, x_a_c, x_b_c], [cols_1], out, col_inv=[col_inv_1]
     )
-    z_a, z_b, best_2 = fence(z_a, z_b, best_2)
-    z_2, z_b_c = send(z_a, up_z), send(z_b, cross)
-    far, p_a, z_b_c, x_2 = fence(far, p_a, z_b_c, x_2)
-    far_c = swap(far)
-    (far_c,) = moved(far_c, [count])
-    x_2, p_a, far, z_2, far_c, z_b_c, best_2 = fence(x_2, p_a, far, z_2, far_c, z_b_c, best_2)
-
+    z_a, best_2 = fence(z_a, best_2)
+    z_2 = [send(v, up_z) for v in moved([z_a], [count // 2] * 2)]
+    x_2, p_a, far, best_2, *z_2 = fence(x_2, p_a, far, best_2, *z_2)
+
+    (z_2,) = moved(z_2, [count])
     f_a, f_2, p_2 = send(far, up_z), send(z_2, {"yh": 1}), send(p_a, up_x)
     x_2_c, p_a_c = fence(send(x_2, cross), send(p_a, cross))
     out, best_1, best_2, cols_2, col_inv_2 = block_call(
-        where[2], [rows_1, rows_2], [z_b_c, z_2], out, row_inv=[inv_1, inv_2], best=[best_1, best_2]
+        where[2], [rows_1, rows_2], [z_b, z_2], out, row_inv=[inv_1, inv_2], best=[best_1, best_2]
     )
     out, best_3, rows_3, inv_3 = block_call(
         where[3], [x_2, x_2_c], [cols_1, cols_2], out, col_inv=[col_inv_1, col_inv_2]
     )
-    far_c, best_3 = fence(far_c, best_3)
-    f_b = send(far_c, up_z)
+    far, best_3 = fence(far, best_3)
+    f_b = [send(v, {"z": "back"}) for v in moved([far], [3 * count // 4, count // 4])]
     p_2, best_3 = fence(p_2, best_3)
     p_2_c = swap(p_2)
     out, best_1, best_2, best_3, cols_3, col_inv_3 = block_call(
@@ -443,12 +444,10 @@
         out,
         col_inv=[col_inv_1, col_inv_2, col_inv_3],
     )
-    f_b, f_2, best_4 = fence(f_b, f_2, best_4)
-    f_b_c = swap(f_b)
     out, best, _, _ = block_call(
         where[6],
         [rows_1, rows_2, rows_3, rows_4],
-        [*f_b_c, f_2],
+        [*f_b, f_2],
         out,
         row_inv=[inv_1, inv_2, inv_3, inv_4],
         best=[best_1, best_2, best_3, best_4],

time: 153 us -> 150 us (0.980)
  waiting for transfers between devices: 60.6 us -> 44.7 us
  starting transfers between devices: 16.6 us -> 28.9 us
    ppermute x32 -> x29, waiting for transfers between devices: 60.6 us -> 44.7 us  [send(): return lax.ppermute(value, AXES, pairs)]
    ppermute x32 -> x29, starting transfers between devices: 16.6 us -> 28.9 us  [send(): return lax.ppermute(value, AXES, pairs)]
  transfers between devices with their start and end apart: 32 -> 29, of which waited for: 14 -> 11; matrix products, arithmetic and copies ran while one was open for 0% -> 0% of each run, Pallas kernels for 17% -> 18%
where the time goes in v4:
time: 150 us; the launch traced here: 149 us
  waiting for transfers between devices  44.7 us (30%)
  Pallas kernels  40.2 us (27%)
  blocking collectives  32.9 us (22%)
  starting transfers between devices  28.9 us (19%)
    ppermute x29, waiting for transfers between devices, send(): return lax.ppermute(value, AXES, pairs)  44.7 us
    all_to_all x1, blocking collectives, per_device(): lax.all_to_all(packed, AXES, split_axis=0, concat_axis=0, tiled=True)  32.9 us
    pallas_call x7, Pallas kernels, block_call(): pl.pallas_call(make_block_kernel(line, row_sizes, col_sizes, fresh_rows,...  31.4 us
    ppermute x29, starting transfers between devices, send(): return lax.ppermute(value, AXES, pairs)  28.9 us
    pallas_call x1, Pallas kernels, per_device(): pl.pallas_call(place_kernel, out_shape=jax.ShapeDtypeStruct((count, width...  3.17 us
    pallas_call x1, Pallas kernels, per_device(): pl.pallas_call(pack_kernel, out_shape=jax.ShapeDtypeStruct((count, width...  3.02 us
  transfers between devices with their start and end apart: 29, of which 11 were waited for; matrix products, arithmetic and copies ran while one was open for 0% of the time, Pallas kernels for 18%

profile of v4, /device:TPU:0, one launch (start us, length us, event | category | flops | bytes accessed | tf_op | source)
XLA Modules:
  0.0 149.4 jit_solution(7000955495995056825)
XLA Ops:
  1.6 3.0 %shard_map.41 = bf16[128,40,128]{2,1,0:T(8,128)(2,1)} custom-call(s32[1,128]{1,0:T(1,128)} %bitcast.41, bf16[128,4096]{1,0:T(8,128)(2,1)} %items_ref.1), custom_call_target="tpu_custom_call" | custom-call | tf_op jit(solution)/shard_map/pallas_call | solution.py:337
  4.7 32.9 %all_to_all.5.in_ref = bf16[128,40,128]{2,1,0:T(8,128)(2,1)} all-to-all(bf16[128,40,128]{2,1,0:T(8,128)(2,1)} %shard_map.41), channel_id=1, replica_groups=mesh['gr'=8,'gc'=16] {'gr','gc'}, dimensions={0} | all-to-all | bytes 2621440 | tf_op jit(solution)/shard_map/all_to_all | solution.py:383
  37.6 3.2 %shard_map.42.refs_1_.refs_5_ = bf16[128,4096]{1,0:T(8,128)(2,1)} custom-call(bf16[128,40,128]{2,1,0:T(8,128)(2,1)} %all_to_all.5.in_ref), custom_call_target="tpu_custom_call" | custom-call | tf_op jit(solution)/shard_map/pallas_call | solution.py:386
  41.9 1.8 %collective-permute-done.refs_2_ = bf16[128,4096]{1,0:T(8,128)(2,1)S(1)} collective-permute-done((bf16[128,4096]{1,0:T(8,128)(2,1)}, bf16[128,4096]{1,0:T(8,128)(2,1)S(1)}, u32[]{:S(2)}, u32[]{:S(2)}) %collective-permute-start) | collective-permute-done | bytes 1048608 | tf_op jit(solution)/shard_map/ppermute | solution.py:39
  43.7 0.9 collective-permute-start.4
  44.6 3.2 %collective-permute-start.2 = (bf16[128,4096]{1,0:T(8,128)(2,1)}, bf16[128,4096]{1,0:T(8,128)(2,1)S(1)}, u32[]{:S(2)}, u32[]{:S(2)}) collective-permute-start(bf16[128,4096]{1,0:T(8,128)(2,1)} %shard_map.42.refs_1_.refs_5_), channel_id=1, source_target_pairs={{0,12},{1,5},{2,14},{3,7},{4,0},{5,9},{6,2},{7,11},{8,4},{9,13},{1... | collective-permute-start | bytes 3145736 | tf_op jit(solution)/shard_map/ppermute | solution.py:39
  47.8 18.8 %collective-permute-done.5.refs_0_.refs_1_ = bf16[128,4096]{1,0:T(8,128)(2,1)S(1)} collective-permute-done((bf16[128,4096]{1,0:T(8,128)(2,1)}, bf16[128,4096]{1,0:T(8,128)(2,1)S(1)}, u32[]{:S(2)}, u32[]{:S(2)}) %collective-permute-start.5) | collective-permute-done | bytes 1048608 | tf_op jit(solution)/shard_map/ppermute | solution.py:39
  67.3 1.4 collective-permute-done.6.refs_2_.refs_1_
  68.7 0.7 collective-permute-done.7.refs_3_.refs_2_
  69.7 0.8 collective-permute-start.9
  70.6 0.9 collective-permute-start.12
  71.4 1.7 %collective-permute-start.11 = (bf16[128,4096]{1,0:T(8,128)(2,1)S(1)}, bf16[128,4096]{1,0:T(8,128)(2,1)S(1)}, u32[]{:S(2)}, u32[]{:S(2)}) collective-permute-start(bf16[128,4096]{1,0:T(8,128)(2,1)S(1)} %collective-permute-done.1.refs_3_.refs_0_), channel_id=1, source_target_pairs={{0,2},{1,3},{2,0},{3,1},{4,6},{5,7},{6,4},{7,5},{8,10},{9,11},{10,... | collective-permute-start | bytes 3145736 | tf_op jit(solution)/shard_map/ppermute | solution.py:39
  73.1 3.6 %shard_map.44 = (bf16[2048,1024]{1,0:T(8,128)(2,1)S(1)}, f32[512,128]{1,0:T(8,128)S(1)}, bf16[512,4096]{1,0:T(8,128)(2,1)S(1)}, f32[512,128]{1,0:T(8,128)S(1)}, ...) custom-call(s32[7,18]{1,0:T(8,128)S(1)} %stack.116.refs_0_, bf16[128,4096]{1,0:T(8,128)(2,1)S(1)} %copy-done, ...), custom_call_target="tpu_custom_call" | custom-call | flops 134217728 | bytes 262144 | tf_op jit(solution)/shard_map/pallas_call | solution.py:280
  76.8 2.9 %shard_map.45 = (bf16[2048,1024]{1,0:T(8,128)(2,1)S(1)}, f32[512,128]{1,0:T(8,128)S(1)}, bf16[512,4096]{1,0:T(8,128)(2,1)S(1)}, f32[512,128]{1,0:T(8,128)S(1)}) custom-call(s32[7,18]{1,0:T(8,128)S(1)} %stack.116.refs_0_, bf16[128,4096]{1,0:T(8,128)(2,1)S(1)} %collective-permute-done.5.refs_0_.refs_1_, ...), custom_call_target="tpu_custom_call", output_to_operand_aliasing={{0}: (8, {})} | custom-call | flops 134217728 | bytes 262144 | tf_op jit(solution)/shard_map/pallas_call | solution.py:280
  80.5 16.9 %collective-permute-done.12.refs_4_.refs_0_ = bf16[128,4096]{1,0:T(8,128)(2,1)S(1)} collective-permute-done((bf16[128,4096]{1,0:T(8,128)(2,1)S(1)}, bf16[128,4096]{1,0:T(8,128)(2,1)S(1)}, u32[]{:S(2)}, u32[]{:S(2)}) %collective-permute-start.12) | collective-permute-done | bytes 1048608 | tf_op jit(solution)/shard_map/ppermute | solution.py:39
  97.9 1.0 collective-permute-start.17
  99.4 2.6 %collective-permute-start.23 = (bf16[128,4096]{1,0:T(8,128)(2,1)S(1)}, bf16[128,4096]{1,0:T(8,128)(2,1)S(1)}, u32[]{:S(2)}, u32[]{:S(2)}) collective-permute-start(bf16[128,4096]{1,0:T(8,128)(2,1)S(1)} %shard_map.48.refs_4_), channel_id=1, source_target_pairs={{0,64},{1,65},{2,66},{3,67},{4,68},{5,69},{6,70},{7,71},{8,72},{9,... | collective-permute-start | bytes 3145736 | tf_op jit(solution)/shard_map/ppermute | solution.py:39
  102.0 3.6 %shard_map.49 = (bf16[2048,1024]{1,0:T(8,128)(2,1)S(1)}, f32[512,128]{1,0:T(8,128)S(1)}, f32[512,128]{1,0:T(8,128)S(1)}, bf16[256,4096]{1,0:T(8,128)(2,1)S(1)}, f32[8,256]{1,0:T(8,128)S(1)}) custom-call(s32[7,18]{1,0:T(8,128)S(1)} %stack.116.refs_0_, bf16[512,4096]{1,0:T(8,128)(2,1)S(1)} %get-tuple-element.79.refs_1_, ...), custom_call_target="tpu_custom_call", output_to_operand_aliasing={{0}: (9, {})} | custom-call | flops 268435456 | bytes 524288 | tf_op jit(solution)/shard_map/pallas_call | solution.py:280
  105.6 4.0 %shard_map.50 = (bf16[2048,1024]{1,0:T(8,128)(2,1)S(1)}, f32[512,128]{1,0:T(8,128)S(1)}, bf16[512,4096]{1,0:T(8,128)(2,1)S(1)}, f32[512,128]{1,0:T(8,128)S(1)}) custom-call(s32[7,18]{1,0:T(8,128)S(1)} %stack.116.refs_0_, bf16[256,4096]{1,0:T(8,128)(2,1)S(1)} %collective-permute-done.10.refs_1_, ...), custom_call_target="tpu_custom_call", output_to_operand_aliasing={{0}: (7, {})} | custom-call | flops 268435456 | bytes 524288 | tf_op jit(solution)/shard_map/pallas_call | solution.py:280
  109.8 3.3 %collective-permute-start.21 = (bf16[96,4096]{1,0:T(8,128)(2,1)S(1)}, bf16[96,4096]{1,0:T(8,128)(2,1)S(1)}, u32[]{:S(2)}, u32[]{:S(2)}) collective-permute-start(bf16[96,4096]{1,0:T(8,128)(2,1)S(1)} %get-tuple-element.124), channel_id=1, source_target_pairs={{0,48},{1,17},{2,50},{3,19},{4,52},{5,21},{6,54},{7,23},{8,56},{9,... | collective-permute-start | bytes 2359304 | tf_op jit(solution)/shard_map/ppermute | solution.py:39
  113.1 0.8 collective-permute-done.17.refs_0_.refs_3_
  115.0 2.1 %collective-permute-start.22 = (bf16[32,4096]{1,0:T(8,128)(2,1)S(1)}, bf16[32,4096]{1,0:T(8,128)(2,1)S(1)}, u32[]{:S(2)}, u32[]{:S(2)}) collective-permute-start(bf16[32,4096]{1,0:T(8,128)(2,1)S(1)} %get-tuple-element.125), channel_id=1, source_target_pairs={{0,48},{1,17},{2,50},{3,19},{4,52},{5,21},{6,54},{7,23},{8,56},{9,... | collective-permute-start | bytes 786440 | tf_op jit(solution)/shard_map/ppermute | solution.py:39
  117.1 4.7 %shard_map.52 = (bf16[2048,1024]{1,0:T(8,128)(2,1)S(1)}, f32[512,128]{1,0:T(8,128)S(1)}, f32[512,128]{1,0:T(8,128)S(1)}, f32[512,128]{1,0:T(8,128)S(1)}, bf16[25...) custom-call(s32[7,18]{1,0:T(8,128)S(1)} %stack.116.refs_0_, ...), custom_call_target="tpu_custom_call", output_to_operand_aliasing={{0}: (12, {})} | custom-call | flops 402653184 | bytes 786432 | tf_op jit(solution)/shard_map/pallas_call | solution.py:280
  121.9 5.3 %shard_map.53 = (bf16[2048,1024]{1,0:T(8,128)(2,1)S(1)}, f32[512,128]{1,0:T(8,128)S(1)}, bf16[512,4096]{1,0:T(8,128)(2,1)S(1)}, f32[512,128]{1,0:T(8,128)S(1)}) custom-call(s32[7,18]{1,0:T(8,128)S(1)} %stack.116.refs_0_, bf16[128,4096]{1,0:T(8,128)(2,1)S(1)} %collective-permute-done.11.refs_1_, ...), custom_call_target="tpu_custom_call", output_to_operand_aliasing={{0}: (12, {})} | custom-call | flops 402653184 | bytes 786432 | tf_op jit(solution)/shard_map/pallas_call | solution.py:280
  127.2 7.2 %shard_map.55 = (bf16[2048,1024]{1,0:T(8,128)(2,1)S(1)}, f32[16,128]{1,0:T(8,128)S(1)}, bf16[256,4096]{1,0:T(8,128)(2,1)}, f32[8,256]{1,0:T(8,128)}) custom-call(s32[7,18]{1,0:T(8,128)S(1)} %stack.116.refs_0_, bf16[512,4096]{1,0:T(8,128)(2,1)S(1)} %get-tuple-element.79.refs_1_, ...), custom_call_target="tpu_custom_call", output_to_operand_aliasing={{0}: (16, {})} | custom-call | flops 536870912 | bytes 1048576 | tf_op jit(solution)/shard_map/pallas_call | solution.py:280
  134.5 1.2 collective-permute-done.24
  135.6 0.7 collective-permute-start.27
  136.3 1.9 %collective-permute-start.26 = (f32[16,128]{1,0:T(8,128)S(1)}, f32[16,128]{1,0:T(8,128)S(1)}, u32[]{:S(2)}, u32[]{:S(2)}) collective-permute-start(f32[16,128]{1,0:T(8,128)S(1)} %max.15), channel_id=1, source_target_pairs={{0,4},{1,5},{2,6},{3,7},{4,0},{5,1},{6,2},{7,3},{8,12},{9,13},{10,... | collective-permute-start | bytes 24584 | tf_op jit(solution)/shard_map/ppermute | solution.py:39
  138.2 0.9 collective-permute-start.25
  139.1 2.0 %shard_map.56 = bf16[2048,1024]{1,0:T(8,128)(2,1)} custom-call(bf16[2048,1024]{1,0:T(8,128)(2,1)S(1)} %get-tuple-element.133.held_ref), custom_call_target="tpu_custom_call" | custom-call | bytes 8388608 | tf_op jit(solution)/shard_map/pallas_call | solution.py:314
  141.9 5.3 %collective-permute-start.28 = (f32[16,128]{1,0:T(8,128)S(1)}, f32[16,128]{1,0:T(8,128)S(1)}, u32[]{:S(2)}, u32[]{:S(2)}) collective-permute-start(f32[16,128]{1,0:T(8,128)S(1)} %maximum_maximum_fusion), channel_id=1, source_target_pairs={{0,12},{1,13},{2,14},{3,15},{4,8},{5,9},{6,10},{7,11},{8,4},{9,5},... | collective-permute-start | bytes 24584 | tf_op jit(solution)/shard_map/ppermute | solution.py:39
  147.2 1.6 %collective-permute-done.28 = f32[16,128]{1,0:T(8,128)S(1)} collective-permute-done((f32[16,128]{1,0:T(8,128)S(1)}, f32[16,128]{1,0:T(8,128)S(1)}, u32[]{:S(2)}, u32[]{:S(2)}) %collective-permute-start.28) | collective-permute-done | bytes 8224 | tf_op jit(solution)/shard_map/ppermute | solution.py:39
  (56 shorter events, 7.0 us)
Async XLA Ops:
  40.8 32.3 %copy-start = (bf16[128,4096]{1,0:T(8,128)(2,1)S(1)}, bf16[128,4096]{1,0:T(8,128)(2,1)}, u32[]{:S(2)}) copy-start(bf16[128,4096]{1,0:T(8,128)(2,1)} %shard_map.42.refs_1_.refs_5_) | copy-start | bytes 3145732
  40.8 2.9 %collective-permute-start = (bf16[128,4096]{1,0:T(8,128)(2,1)}, bf16[128,4096]{1,0:T(8,128)(2,1)S(1)}, u32[]{:S(2)}, u32[]{:S(2)}) collective-permute-start(bf16[128,4096]{1,0:T(8,128)(2,1)} %shard_map.42.refs_1_.refs_5_), channel_id=1, source_target_pairs={{0,1},{1,0},{2,3},{3,2},{4,5},{5,4},{6,7},{7,6},{8,9},{9,8},{10,11... | collective-permute-start | bytes 3145736 | tf_op jit(solution)/shard_map/ppermute | solution.py:39
  40.8 25.8 %collective-permute-start.5 = (bf16[128,4096]{1,0:T(8,128)(2,1)}, bf16[128,4096]{1,0:T(8,128)(2,1)S(1)}, u32[]{:S(2)}, u32[]{:S(2)}) collective-permute-start(bf16[128,4096]{1,0:T(8,128)(2,1)} %shard_map.42.refs_1_.refs_5_), channel_id=1, source_target_pairs={{0,2},{1,3},{2,0},{3,1},{4,6},{5,7},{6,4},{7,5},{8,10},{9,11},{10,... | collective-permute-start | bytes 3145736 | tf_op jit(solution)/shard_map/ppermute | solution.py:39
  41.3 25.9 %collective-permute-start.3 = (bf16[128,4096]{1,0:T(8,128)(2,1)}, bf16[128,4096]{1,0:T(8,128)(2,1)S(1)}, u32[]{:S(2)}, u32[]{:S(2)}) collective-permute-start(bf16[128,4096]{1,0:T(8,128)(2,1)} %shard_map.42.refs_1_.refs_5_), channel_id=1, source_target_pairs={{0,16},{1,49},{2,18},{3,51},{4,20},{5,53},{6,22},{7,55},{8,24},{9,... | collective-permute-start | bytes 3145736 | tf_op jit(solution)/shard_map/ppermute | solution.py:39
  41.3 25.9 %collective-permute-start.1 = (bf16[128,4096]{1,0:T(8,128)(2,1)}, bf16[128,4096]{1,0:T(8,128)(2,1)S(1)}, u32[]{:S(2)}, u32[]{:S(2)}) collective-permute-start(bf16[128,4096]{1,0:T(8,128)(2,1)} %shard_map.42.refs_1_.refs_5_), channel_id=1, source_target_pairs={{0,4},{1,13},{2,6},{3,15},{4,8},{5,1},{6,10},{7,3},{8,12},{9,5},{1... | collective-permute-start | bytes 3145736 | tf_op jit(solution)/shard_map/ppermute | solution.py:39
  43.7 25.8 %collective-permute-start.4 = (bf16[128,4096]{1,0:T(8,128)(2,1)}, bf16[128,4096]{1,0:T(8,128)(2,1)S(1)}, u32[]{:S(2)}, u32[]{:S(2)}) collective-permute-start(bf16[128,4096]{1,0:T(8,128)(2,1)} %shard_map.42.refs_1_.refs_5_), channel_id=1, source_target_pairs={{0,48},{1,17},{2,50},{3,19},{4,52},{5,21},{6,54},{7,23},{8,56},{9,... | collective-permute-start | bytes 3145736 | tf_op jit(solution)/shard_map/ppermute | solution.py:39
  44.6 24.9 %collective-permute-start.2 = (bf16[128,4096]{1,0:T(8,128)(2,1)}, bf16[128,4096]{1,0:T(8,128)(2,1)S(1)}, u32[]{:S(2)}, u32[]{:S(2)}) collective-permute-start(bf16[128,4096]{1,0:T(8,128)(2,1)} %shard_map.42.refs_1_.refs_5_), channel_id=1, source_target_pairs={{0,12},{1,5},{2,14},{3,7},{4,0},{5,9},{6,2},{7,11},{8,4},{9,13},{1... | collective-permute-start | bytes 3145736 | tf_op jit(solution)/shard_map/ppermute | solution.py:39
  66.7 2.0 %collective-permute-start.6 = (bf16[64,4096]{1,0:T(8,128)(2,1)S(1)}, bf16[64,4096]{1,0:T(8,128)(2,1)S(1)}, u32[]{:S(2)}, u32[]{:S(2)}) collective-permute-start(bf16[64,4096]{1,0:T(8,128)(2,1)S(1)} %get-tuple-element.73), channel_id=1, source_target_pairs={{0,1},{1,0},{2,3},{3,2},{4,5},{5,4},{6,7},{7,6},{8,9},{9,8},{10,11... | collective-permute-start | bytes 1572872 | tf_op jit(solution)/shard_map/ppermute | solution.py:39
  67.2 2.2 %collective-permute-start.7 = (bf16[64,4096]{1,0:T(8,128)(2,1)S(1)}, bf16[64,4096]{1,0:T(8,128)(2,1)S(1)}, u32[]{:S(2)}, u32[]{:S(2)}) collective-permute-start(bf16[64,4096]{1,0:T(8,128)(2,1)S(1)} %get-tuple-element.74), channel_id=1, source_target_pairs={{0,1},{1,0},{2,3},{3,2},{4,5},{5,4},{6,7},{7,6},{8,9},{9,8},{10,11... | collective-permute-start | bytes 1572872 | tf_op jit(solution)/shard_map/ppermute | solution.py:39
  69.6 27.7 %collective-permute-start.10 = (bf16[256,4096]{1,0:T(8,128)(2,1)S(1)}, bf16[256,4096]{1,0:T(8,128)(2,1)S(1)}, u32[]{:S(2)}, u32[]{:S(2)}) collective-permute-start(bf16[256,4096]{1,0:T(8,128)(2,1)S(1)} %shard_map.46), channel_id=1, source_target_pairs={{0,4},{1,13},{2,6},{3,15},{4,8},{5,1},{6,10},{7,3},{8,12},{9,5},{1... | collective-permute-start | bytes 6291464 | tf_op jit(solution)/shard_map/ppermute | solution.py:39
  69.7 7.1 %collective-permute-start.9 = (bf16[128,4096]{1,0:T(8,128)(2,1)S(1)}, bf16[128,4096]{1,0:T(8,128)(2,1)S(1)}, u32[]{:S(2)}, u32[]{:S(2)}) collective-permute-start(bf16[128,4096]{1,0:T(8,128)(2,1)S(1)} %collective-permute-done.2.refs_4_), channel_id=1, source_target_pairs={{0,1},{1,0},{2,3},{3,2},{4,5},{5,4},{6,7},{7,6},{8,9},{9,8},{10,11... | collective-permute-start | bytes 3145736 | tf_op jit(solution)/shard_map/ppermute | solution.py:39
  70.5 6.2 %collective-permute-start.8 = (bf16[128,4096]{1,0:T(8,128)(2,1)S(1)}, bf16[128,4096]{1,0:T(8,128)(2,1)S(1)}, u32[]{:S(2)}, u32[]{:S(2)}) collective-permute-start(bf16[128,4096]{1,0:T(8,128)(2,1)S(1)} %collective-permute-done.1.refs_3_.refs_0_), channel_id=1, source_target_pairs={{0,1},{1,0},{2,3},{3,2},{4,5},{5,4},{6,7},{7,6},{8,9},{9,8},{10,11... | collective-permute-start | bytes 3145736 | tf_op jit(solution)/shard_map/ppermute | solution.py:39
  70.6 26.8 %collective-permute-start.12 = (bf16[128,4096]{1,0:T(8,128)(2,1)S(1)}, bf16[128,4096]{1,0:T(8,128)(2,1)S(1)}, u32[]{:S(2)}, u32[]{:S(2)}) collective-permute-start(bf16[128,4096]{1,0:T(8,128)(2,1)S(1)} %collective-permute-done.5.refs_0_.refs_1_), channel_id=1, source_target_pairs={{0,66},{1,67},{2,64},{3,65},{4,70},{5,71},{6,68},{7,69},{8,74},{9,... | collective-permute-start | bytes 3145736 | tf_op jit(solution)/shard_map/ppermute | solution.py:39
  71.4 25.9 %collective-permute-start.11 = (bf16[128,4096]{1,0:T(8,128)(2,1)S(1)}, bf16[128,4096]{1,0:T(8,128)(2,1)S(1)}, u32[]{:S(2)}, u32[]{:S(2)}) collective-permute-start(bf16[128,4096]{1,0:T(8,128)(2,1)S(1)} %collective-permute-done.1.refs_3_.refs_0_), channel_id=1, source_target_pairs={{0,2},{1,3},{2,0},{3,1},{4,6},{5,7},{6,4},{7,5},{8,10},{9,11},{10,... | collective-permute-start | bytes 3145736 | tf_op jit(solution)/shard_map/ppermute | solution.py:39
  79.8 17.5 %collective-permute-start.13 = (bf16[64,4096]{1,0:T(8,128)(2,1)S(1)}, bf16[64,4096]{1,0:T(8,128)(2,1)S(1)}, u32[]{:S(2)}, u32[]{:S(2)}) collective-permute-start(bf16[64,4096]{1,0:T(8,128)(2,1)S(1)} %get-tuple-element.90), channel_id=1, source_target_pairs={{0,16},{1,49},{2,18},{3,51},{4,20},{5,53},{6,22},{7,55},{8,24},{9,... | collective-permute-start | bytes 1572872 | tf_op jit(solution)/shard_map/ppermute | solution.py:39
  79.9 17.4 %collective-permute-start.14 = (bf16[64,4096]{1,0:T(8,128)(2,1)S(1)}, bf16[64,4096]{1,0:T(8,128)(2,1)S(1)}, u32[]{:S(2)}, u32[]{:S(2)}) collective-permute-start(bf16[64,4096]{1,0:T(8,128)(2,1)S(1)} %get-tuple-element.91), channel_id=1, source_target_pairs={{0,16},{1,49},{2,18},{3,51},{4,20},{5,53},{6,22},{7,55},{8,24},{9,... | collective-permute-start | bytes 1572872 | tf_op jit(solution)/shard_map/ppermute | solution.py:39
  97.4 8.3 %collective-permute-start.15 = (bf16[256,4096]{1,0:T(8,128)(2,1)S(1)}, bf16[256,4096]{1,0:T(8,128)(2,1)S(1)}, u32[]{:S(2)}, u32[]{:S(2)}) collective-permute-start(bf16[256,4096]{1,0:T(8,128)(2,1)S(1)} %collective-permute-done.10.refs_1_), channel_id=1, source_target_pairs={{0,1},{1,0},{2,3},{3,2},{4,5},{5,4},{6,7},{7,6},{8,9},{9,8},{10,11... | collective-permute-start | bytes 6291464 | tf_op jit(solution)/shard_map/ppermute | solution.py:39
  97.5 8.2 %collective-permute-start.16 = (bf16[128,4096]{1,0:T(8,128)(2,1)S(1)}, bf16[128,4096]{1,0:T(8,128)(2,1)S(1)}, u32[]{:S(2)}, u32[]{:S(2)}) collective-permute-start(bf16[128,4096]{1,0:T(8,128)(2,1)S(1)} %collective-permute-done.11.refs_1_), channel_id=1, source_target_pairs={{0,1},{1,0},{2,3},{3,2},{4,5},{5,4},{6,7},{7,6},{8,9},{9,8},{10,11... | collective-permute-start | bytes 3145736 | tf_op jit(solution)/shard_map/ppermute | solution.py:39
  97.9 16.0 %collective-permute-start.17 = (bf16[128,4096]{1,0:T(8,128)(2,1)S(1)}, bf16[128,4096]{1,0:T(8,128)(2,1)S(1)}, u32[]{:S(2)}, u32[]{:S(2)}) collective-permute-start(bf16[128,4096]{1,0:T(8,128)(2,1)S(1)} %collective-permute-done.11.refs_1_), channel_id=1, source_target_pairs={{0,4},{1,13},{2,6},{3,15},{4,8},{5,1},{6,10},{7,3},{8,12},{9,5},{1... | collective-permute-start | bytes 3145736 | tf_op jit(solution)/shard_map/ppermute | solution.py:39
  99.0 16.0 %collective-permute-start.20 = (bf16[128,4096]{1,0:T(8,128)(2,1)S(1)}, bf16[128,4096]{1,0:T(8,128)(2,1)S(1)}, u32[]{:S(2)}, u32[]{:S(2)}) collective-permute-start(bf16[128,4096]{1,0:T(8,128)(2,1)S(1)} %collective-permute-done.12.refs_4_.refs_0_), channel_id=1, source_target_pairs={{0,16},{1,49},{2,18},{3,51},{4,20},{5,53},{6,22},{7,55},{8,24},{9,... | collective-permute-start | bytes 3145736 | tf_op jit(solution)/shard_map/ppermute | solution.py:39
  99.4 27.8 %collective-permute-start.23 = (bf16[128,4096]{1,0:T(8,128)(2,1)S(1)}, bf16[128,4096]{1,0:T(8,128)(2,1)S(1)}, u32[]{:S(2)}, u32[]{:S(2)}) collective-permute-start(bf16[128,4096]{1,0:T(8,128)(2,1)S(1)} %shard_map.48.refs_4_), channel_id=1, source_target_pairs={{0,64},{1,65},{2,66},{3,67},{4,68},{5,69},{6,70},{7,71},{8,72},{9,... | collective-permute-start | bytes 3145736 | tf_op jit(solution)/shard_map/ppermute | solution.py:39
  109.8 17.4 %collective-permute-start.21 = (bf16[96,4096]{1,0:T(8,128)(2,1)S(1)}, bf16[96,4096]{1,0:T(8,128)(2,1)S(1)}, u32[]{:S(2)}, u32[]{:S(2)}) collective-permute-start(bf16[96,4096]{1,0:T(8,128)(2,1)S(1)} %get-tuple-element.124), channel_id=1, source_target_pairs={{0,48},{1,17},{2,50},{3,19},{4,52},{5,21},{6,54},{7,23},{8,56},{9,... | collective-permute-start | bytes 2359304 | tf_op jit(solution)/shard_map/ppermute | solution.py:39
  114.1 7.8 %collective-permute-start.18 = (bf16[64,4096]{1,0:T(8,128)(2,1)S(1)}, bf16[64,4096]{1,0:T(8,128)(2,1)S(1)}, u32[]{:S(2)}, u32[]{:S(2)}) collective-permute-start(bf16[64,4096]{1,0:T(8,128)(2,1)S(1)} %get-tuple-element.112), channel_id=1, source_target_pairs={{0,1},{1,0},{2,3},{3,2},{4,5},{5,4},{6,7},{7,6},{8,9},{9,8},{10,11... | collective-permute-start | bytes 1572872 | tf_op jit(solution)/shard_map/ppermute | solution.py:39
  114.2 7.7 %collective-permute-start.19 = (bf16[64,4096]{1,0:T(8,128)(2,1)S(1)}, bf16[64,4096]{1,0:T(8,128)(2,1)S(1)}, u32[]{:S(2)}, u32[]{:S(2)}) collective-permute-start(bf16[64,4096]{1,0:T(8,128)(2,1)S(1)} %get-tuple-element.113), channel_id=1, source_target_pairs={{0,1},{1,0},{2,3},{3,2},{4,5},{5,4},{6,7},{7,6},{8,9},{9,8},{10,11... | collective-permute-start | bytes 1572872 | tf_op jit(solution)/shard_map/ppermute | solution.py:39
  115.0 12.2 %collective-permute-start.22 = (bf16[32,4096]{1,0:T(8,128)(2,1)S(1)}, bf16[32,4096]{1,0:T(8,128)(2,1)S(1)}, u32[]{:S(2)}, u32[]{:S(2)}) collective-permute-start(bf16[32,4096]{1,0:T(8,128)(2,1)S(1)} %get-tuple-element.125), channel_id=1, source_target_pairs={{0,48},{1,17},{2,50},{3,19},{4,52},{5,21},{6,54},{7,23},{8,56},{9,... | collective-permute-start | bytes 786440 | tf_op jit(solution)/shard_map/ppermute | solution.py:39
  134.4 1.3 collective-permute-start.24
  135.6 5.5 %collective-permute-start.27 = (f32[16,128]{1,0:T(8,128)S(1)}, f32[16,128]{1,0:T(8,128)S(1)}, u32[]{:S(2)}, u32[]{:S(2)}) collective-permute-start(f32[16,128]{1,0:T(8,128)S(1)} %max.15), channel_id=1, source_target_pairs={{0,6},{1,7},{2,4},{3,5},{4,2},{5,3},{6,0},{7,1},{8,14},{9,15},{10,... | collective-permute-start | bytes 24584 | tf_op jit(solution)/shard_map/ppermute | solution.py:39
  136.3 4.9 %collective-permute-start.26 = (f32[16,128]{1,0:T(8,128)S(1)}, f32[16,128]{1,0:T(8,128)S(1)}, u32[]{:S(2)}, u32[]{:S(2)}) collective-permute-start(f32[16,128]{1,0:T(8,128)S(1)} %max.15), channel_id=1, source_target_pairs={{0,4},{1,5},{2,6},{3,7},{4,0},{5,1},{6,2},{7,3},{8,12},{9,13},{10,... | collective-permute-start | bytes 24584 | tf_op jit(solution)/shard_map/ppermute | solution.py:39
  138.2 3.7 %collective-permute-start.25 = (f32[16,128]{1,0:T(8,128)S(1)}, f32[16,128]{1,0:T(8,128)S(1)}, u32[]{:S(2)}, u32[]{:S(2)}) collective-permute-start(f32[16,128]{1,0:T(8,128)S(1)} %max.15), channel_id=1, source_target_pairs={{0,2},{1,3},{2,0},{3,1},{4,6},{5,7},{6,4},{7,5},{8,10},{9,11},{10,... | collective-permute-start | bytes 24584 | tf_op jit(solution)/shard_map/ppermute | solution.py:39
  141.9 6.9 %collective-permute-start.28 = (f32[16,128]{1,0:T(8,128)S(1)}, f32[16,128]{1,0:T(8,128)S(1)}, u32[]{:S(2)}, u32[]{:S(2)}) collective-permute-start(f32[16,128]{1,0:T(8,128)S(1)} %maximum_maximum_fusion), channel_id=1, source_target_pairs={{0,12},{1,13},{2,14},{3,15},{4,8},{5,9},{6,10},{7,11},{8,4},{9,5},... | collective-permute-start | bytes 24584 | tf_op jit(solution)/shard_map/ppermute | solution.py:39

commit v5 on v4

--- a/solution.py
+++ b/solution.py
@@ -426,7 +426,7 @@
         where[3], [x_2, x_2_c], [cols_1, cols_2], out, col_inv=[col_inv_1, col_inv_2]
     )
     far, best_3 = fence(far, best_3)
-    f_b = [send(v, {"z": "back"}) for v in moved([far], [3 * count // 4, count // 4])]
+    f_b = [send(far, {"z": "back"})]
     p_2, best_3 = fence(p_2, best_3)
     p_2_c = swap(p_2)
     out, best_1, best_2, best_3, cols_3, col_inv_3 = block_call(

time: 150 us -> 149 us (level)
  starting transfers between devices: 28.9 us -> 27.3 us
    ppermute x29 -> x28, starting transfers between devices: 28.9 us -> 27.3 us  [send(): return lax.ppermute(value, AXES, pairs)]
    ppermute x29 -> x28, waiting for transfers between devices: 44.7 us -> 45.1 us  [send(): return lax.ppermute(value, AXES, pairs)]
  transfers between devices with their start and end apart: 29 -> 28, of which waited for: 11 -> 12; matrix products, arithmetic and copies ran while one was open for 0% -> 0% of each run, Pallas kernels for 18% -> 18%
where the time goes in v5:
time: 149 us; the launch traced here: 148 us
  waiting for transfers between devices  45.1 us (30%)
  Pallas kernels  40.1 us (27%)
  blocking collectives  32.9 us (22%)
  starting transfers between devices  27.3 us (18%)
    ppermute x28, waiting for transfers between devices, send(): return lax.ppermute(value, AXES, pairs)  45.1 us
    all_to_all x1, blocking collectives, per_device(): lax.all_to_all(packed, AXES, split_axis=0, concat_axis=0, tiled=True)  32.9 us
    pallas_call x7, Pallas kernels, block_call(): pl.pallas_call(make_block_kernel(line, row_sizes, col_sizes, fresh_rows,...  31.3 us
    ppermute x28, starting transfers between devices, send(): return lax.ppermute(value, AXES, pairs)  27.3 us
    pallas_call x1, Pallas kernels, per_device(): pl.pallas_call(place_kernel, out_shape=jax.ShapeDtypeStruct((count, width...  3.17 us
    pallas_call x1, Pallas kernels, per_device(): pl.pallas_call(pack_kernel, out_shape=jax.ShapeDtypeStruct((count, width...  3.02 us
  transfers between devices with their start and end apart: 28, of which 12 were waited for; matrix products, arithmetic and copies ran while one was open for 0% of the time, Pallas kernels for 18%

profile of v5, /device:TPU:0, one launch (start us, length us, event | category | flops | bytes accessed | tf_op | source)
XLA Modules:
  0.0 148.0 jit_solution(2716003707815852914)
XLA Ops:
  1.6 3.0 %shard_map.41 = bf16[128,40,128]{2,1,0:T(8,128)(2,1)} custom-call(s32[1,128]{1,0:T(1,128)} %bitcast.41, bf16[128,4096]{1,0:T(8,128)(2,1)} %items_ref.1), custom_call_target="tpu_custom_call" | custom-call | tf_op jit(solution)/shard_map/pallas_call | solution.py:337
  4.7 32.9 %all_to_all.5.in_ref = bf16[128,40,128]{2,1,0:T(8,128)(2,1)} all-to-all(bf16[128,40,128]{2,1,0:T(8,128)(2,1)} %shard_map.41), channel_id=1, replica_groups=mesh['gr'=8,'gc'=16] {'gr','gc'}, dimensions={0} | all-to-all | bytes 2621440 | tf_op jit(solution)/shard_map/all_to_all | solution.py:383
  37.6 3.2 %shard_map.42.refs_1_.refs_5_ = bf16[128,4096]{1,0:T(8,128)(2,1)} custom-call(bf16[128,40,128]{2,1,0:T(8,128)(2,1)} %all_to_all.5.in_ref), custom_call_target="tpu_custom_call" | custom-call | tf_op jit(solution)/shard_map/pallas_call | solution.py:386
  41.9 1.8 %collective-permute-done.refs_2_ = bf16[128,4096]{1,0:T(8,128)(2,1)S(1)} collective-permute-done((bf16[128,4096]{1,0:T(8,128)(2,1)}, bf16[128,4096]{1,0:T(8,128)(2,1)S(1)}, u32[]{:S(2)}, u32[]{:S(2)}) %collective-permute-start) | collective-permute-done | bytes 1048608 | tf_op jit(solution)/shard_map/ppermute | solution.py:39
  43.7 0.9 collective-permute-start.4
  44.6 3.2 %collective-permute-start.2 = (bf16[128,4096]{1,0:T(8,128)(2,1)}, bf16[128,4096]{1,0:T(8,128)(2,1)S(1)}, u32[]{:S(2)}, u32[]{:S(2)}) collective-permute-start(bf16[128,4096]{1,0:T(8,128)(2,1)} %shard_map.42.refs_1_.refs_5_), channel_id=1, source_target_pairs={{0,12},{1,5},{2,14},{3,7},{4,0},{5,9},{6,2},{7,11},{8,4},{9,13},{1... | collective-permute-start | bytes 3145736 | tf_op jit(solution)/shard_map/ppermute | solution.py:39
  47.8 18.8 %collective-permute-done.5.refs_0_.refs_1_ = bf16[128,4096]{1,0:T(8,128)(2,1)S(1)} collective-permute-done((bf16[128,4096]{1,0:T(8,128)(2,1)}, bf16[128,4096]{1,0:T(8,128)(2,1)S(1)}, u32[]{:S(2)}, u32[]{:S(2)}) %collective-permute-start.5) | collective-permute-done | bytes 1048608 | tf_op jit(solution)/shard_map/ppermute | solution.py:39
  67.3 1.4 collective-permute-done.6.refs_2_.refs_1_
  69.7 0.8 collective-permute-start.9
  70.6 0.9 collective-permute-start.12
  71.4 1.7 %collective-permute-start.11 = (bf16[128,4096]{1,0:T(8,128)(2,1)S(1)}, bf16[128,4096]{1,0:T(8,128)(2,1)S(1)}, u32[]{:S(2)}, u32[]{:S(2)}) collective-permute-start(bf16[128,4096]{1,0:T(8,128)(2,1)S(1)} %collective-permute-done.1.refs_3_.refs_0_), channel_id=1, source_target_pairs={{0,2},{1,3},{2,0},{3,1},{4,6},{5,7},{6,4},{7,5},{8,10},{9,11},{10,... | collective-permute-start | bytes 3145736 | tf_op jit(solution)/shard_map/ppermute | solution.py:39
  73.1 3.6 %shard_map.44 = (bf16[2048,1024]{1,0:T(8,128)(2,1)S(1)}, f32[512,128]{1,0:T(8,128)S(1)}, bf16[512,4096]{1,0:T(8,128)(2,1)S(1)}, f32[512,128]{1,0:T(8,128)S(1)}, ...) custom-call(s32[7,18]{1,0:T(8,128)S(1)} %stack.116.refs_0_, bf16[128,4096]{1,0:T(8,128)(2,1)S(1)} %copy-done, ...), custom_call_target="tpu_custom_call" | custom-call | flops 134217728 | bytes 262144 | tf_op jit(solution)/shard_map/pallas_call | solution.py:280
  76.8 2.9 %shard_map.45 = (bf16[2048,1024]{1,0:T(8,128)(2,1)S(1)}, f32[512,128]{1,0:T(8,128)S(1)}, bf16[512,4096]{1,0:T(8,128)(2,1)S(1)}, f32[512,128]{1,0:T(8,128)S(1)}) custom-call(s32[7,18]{1,0:T(8,128)S(1)} %stack.116.refs_0_, bf16[128,4096]{1,0:T(8,128)(2,1)S(1)} %collective-permute-done.5.refs_0_.refs_1_, ...), custom_call_target="tpu_custom_call", output_to_operand_aliasing={{0}: (8, {})} | custom-call | flops 134217728 | bytes 262144 | tf_op jit(solution)/shard_map/pallas_call | solution.py:280
  80.5 16.9 %collective-permute-done.12.refs_4_ = bf16[128,4096]{1,0:T(8,128)(2,1)S(1)} collective-permute-done((bf16[128,4096]{1,0:T(8,128)(2,1)S(1)}, bf16[128,4096]{1,0:T(8,128)(2,1)S(1)}, u32[]{:S(2)}, u32[]{:S(2)}) %collective-permute-start.12) | collective-permute-done | bytes 1048608 | tf_op jit(solution)/shard_map/ppermute | solution.py:39
  97.9 1.0 collective-permute-start.17
  99.4 2.6 %collective-permute-start.22 = (bf16[128,4096]{1,0:T(8,128)(2,1)S(1)}, bf16[128,4096]{1,0:T(8,128)(2,1)S(1)}, u32[]{:S(2)}, u32[]{:S(2)}) collective-permute-start(bf16[128,4096]{1,0:T(8,128)(2,1)S(1)} %shard_map.48.refs_4_), channel_id=1, source_target_pairs={{0,64},{1,65},{2,66},{3,67},{4,68},{5,69},{6,70},{7,71},{8,72},{9,... | collective-permute-start | bytes 3145736 | tf_op jit(solution)/shard_map/ppermute | solution.py:39
  102.0 3.6 %shard_map.49 = (bf16[2048,1024]{1,0:T(8,128)(2,1)S(1)}, f32[512,128]{1,0:T(8,128)S(1)}, f32[512,128]{1,0:T(8,128)S(1)}, bf16[256,4096]{1,0:T(8,128)(2,1)S(1)}, f32[8,256]{1,0:T(8,128)S(1)}) custom-call(s32[7,18]{1,0:T(8,128)S(1)} %stack.116.refs_0_, bf16[512,4096]{1,0:T(8,128)(2,1)S(1)} %get-tuple-element.77.refs_1_, ...), custom_call_target="tpu_custom_call", output_to_operand_aliasing={{0}: (9, {})} | custom-call | flops 268435456 | bytes 524288 | tf_op jit(solution)/shard_map/pallas_call | solution.py:280
  105.6 4.0 %shard_map.50 = (bf16[2048,1024]{1,0:T(8,128)(2,1)S(1)}, f32[512,128]{1,0:T(8,128)S(1)}, bf16[512,4096]{1,0:T(8,128)(2,1)S(1)}, f32[512,128]{1,0:T(8,128)S(1)}) custom-call(s32[7,18]{1,0:T(8,128)S(1)} %stack.116.refs_0_, bf16[256,4096]{1,0:T(8,128)(2,1)S(1)} %collective-permute-done.10.refs_1_, ...), custom_call_target="tpu_custom_call", output_to_operand_aliasing={{0}: (7, {})} | custom-call | flops 268435456 | bytes 524288 | tf_op jit(solution)/shard_map/pallas_call | solution.py:280
  109.7 3.3 %collective-permute-start.21 = (bf16[128,4096]{1,0:T(8,128)(2,1)S(1)}, bf16[128,4096]{1,0:T(8,128)(2,1)S(1)}, u32[]{:S(2)}, u32[]{:S(2)}) collective-permute-start(bf16[128,4096]{1,0:T(8,128)(2,1)S(1)} %collective-permute-done.12.refs_4_), channel_id=1, source_target_pairs={{0,48},{1,17},{2,50},{3,19},{4,52},{5,21},{6,54},{7,23},{8,56},{9,... | collective-permute-start | bytes 3145736 | tf_op jit(solution)/shard_map/ppermute | solution.py:39
  113.0 1.0 collective-permute-done.17.refs_0_.refs_3_
  115.0 4.7 %shard_map.52 = (bf16[2048,1024]{1,0:T(8,128)(2,1)S(1)}, f32[512,128]{1,0:T(8,128)S(1)}, f32[512,128]{1,0:T(8,128)S(1)}, f32[512,128]{1,0:T(8,128)S(1)}, bf16[25...) custom-call(s32[7,18]{1,0:T(8,128)S(1)} %stack.116.refs_0_, ...), custom_call_target="tpu_custom_call", output_to_operand_aliasing={{0}: (12, {})} | custom-call | flops 402653184 | bytes 786432 | tf_op jit(solution)/shard_map/pallas_call | solution.py:280
  119.7 5.3 %shard_map.53 = (bf16[2048,1024]{1,0:T(8,128)(2,1)S(1)}, f32[512,128]{1,0:T(8,128)S(1)}, bf16[512,4096]{1,0:T(8,128)(2,1)S(1)}, f32[512,128]{1,0:T(8,128)S(1)}) custom-call(s32[7,18]{1,0:T(8,128)S(1)} %stack.116.refs_0_, bf16[128,4096]{1,0:T(8,128)(2,1)S(1)} %collective-permute-done.11.refs_1_, ...), custom_call_target="tpu_custom_call", output_to_operand_aliasing={{0}: (12, {})} | custom-call | flops 402653184 | bytes 786432 | tf_op jit(solution)/shard_map/pallas_call | solution.py:280
  125.0 1.0 collective-permute-done.22.refs_6_
  126.0 7.2 %shard_map.54 = (bf16[2048,1024]{1,0:T(8,128)(2,1)S(1)}, f32[16,128]{1,0:T(8,128)S(1)}, bf16[256,4096]{1,0:T(8,128)(2,1)}, f32[8,256]{1,0:T(8,128)}) custom-call(s32[7,18]{1,0:T(8,128)S(1)} %stack.116.refs_0_, bf16[512,4096]{1,0:T(8,128)(2,1)S(1)} %get-tuple-element.77.refs_1_, ...), custom_call_target="tpu_custom_call", output_to_operand_aliasing={{0}: (15, {})} | custom-call | flops 536870912 | bytes 1048576 | tf_op jit(solution)/shard_map/pallas_call | solution.py:280
  133.2 0.9 collective-permute-start.23
  134.1 0.8 collective-permute-done.23
  134.9 0.9 collective-permute-start.26
  135.9 1.3 collective-permute-start.25
  137.2 1.2 collective-permute-start.24
  138.4 2.0 %shard_map.55 = bf16[2048,1024]{1,0:T(8,128)(2,1)} custom-call(bf16[2048,1024]{1,0:T(8,128)(2,1)S(1)} %get-tuple-element.129.held_ref), custom_call_target="tpu_custom_call" | custom-call | bytes 8388608 | tf_op jit(solution)/shard_map/pallas_call | solution.py:314
  140.8 5.0 %collective-permute-start.27 = (f32[16,128]{1,0:T(8,128)S(1)}, f32[16,128]{1,0:T(8,128)S(1)}, u32[]{:S(2)}, u32[]{:S(2)}) collective-permute-start(f32[16,128]{1,0:T(8,128)S(1)} %maximum_maximum_fusion), channel_id=1, source_target_pairs={{0,12},{1,13},{2,14},{3,15},{4,8},{5,9},{6,10},{7,11},{8,4},{9,5},... | collective-permute-start | bytes 24584 | tf_op jit(solution)/shard_map/ppermute | solution.py:39
  145.8 1.6 %collective-permute-done.27 = f32[16,128]{1,0:T(8,128)S(1)} collective-permute-done((f32[16,128]{1,0:T(8,128)S(1)}, f32[16,128]{1,0:T(8,128)S(1)}, u32[]{:S(2)}, u32[]{:S(2)}) %collective-permute-start.27) | collective-permute-done | bytes 8224 | tf_op jit(solution)/shard_map/ppermute | solution.py:39
  (53 shorter events, 7.2 us)
Async XLA Ops:
  40.8 32.3 %copy-start = (bf16[128,4096]{1,0:T(8,128)(2,1)S(1)}, bf16[128,4096]{1,0:T(8,128)(2,1)}, u32[]{:S(2)}) copy-start(bf16[128,4096]{1,0:T(8,128)(2,1)} %shard_map.42.refs_1_.refs_5_) | copy-start | bytes 3145732
  40.8 2.9 %collective-permute-start = (bf16[128,4096]{1,0:T(8,128)(2,1)}, bf16[128,4096]{1,0:T(8,128)(2,1)S(1)}, u32[]{:S(2)}, u32[]{:S(2)}) collective-permute-start(bf16[128,4096]{1,0:T(8,128)(2,1)} %shard_map.42.refs_1_.refs_5_), channel_id=1, source_target_pairs={{0,1},{1,0},{2,3},{3,2},{4,5},{5,4},{6,7},{7,6},{8,9},{9,8},{10,11... | collective-permute-start | bytes 3145736 | tf_op jit(solution)/shard_map/ppermute | solution.py:39
  40.8 25.8 %collective-permute-start.5 = (bf16[128,4096]{1,0:T(8,128)(2,1)}, bf16[128,4096]{1,0:T(8,128)(2,1)S(1)}, u32[]{:S(2)}, u32[]{:S(2)}) collective-permute-start(bf16[128,4096]{1,0:T(8,128)(2,1)} %shard_map.42.refs_1_.refs_5_), channel_id=1, source_target_pairs={{0,2},{1,3},{2,0},{3,1},{4,6},{5,7},{6,4},{7,5},{8,10},{9,11},{10,... | collective-permute-start | bytes 3145736 | tf_op jit(solution)/shard_map/ppermute | solution.py:39
  41.3 25.9 %collective-permute-start.3 = (bf16[128,4096]{1,0:T(8,128)(2,1)}, bf16[128,4096]{1,0:T(8,128)(2,1)S(1)}, u32[]{:S(2)}, u32[]{:S(2)}) collective-permute-start(bf16[128,4096]{1,0:T(8,128)(2,1)} %shard_map.42.refs_1_.refs_5_), channel_id=1, source_target_pairs={{0,16},{1,49},{2,18},{3,51},{4,20},{5,53},{6,22},{7,55},{8,24},{9,... | collective-permute-start | bytes 3145736 | tf_op jit(solution)/shard_map/ppermute | solution.py:39
  41.3 25.9 %collective-permute-start.1 = (bf16[128,4096]{1,0:T(8,128)(2,1)}, bf16[128,4096]{1,0:T(8,128)(2,1)S(1)}, u32[]{:S(2)}, u32[]{:S(2)}) collective-permute-start(bf16[128,4096]{1,0:T(8,128)(2,1)} %shard_map.42.refs_1_.refs_5_), channel_id=1, source_target_pairs={{0,4},{1,13},{2,6},{3,15},{4,8},{5,1},{6,10},{7,3},{8,12},{9,5},{1... | collective-permute-start | bytes 3145736 | tf_op jit(solution)/shard_map/ppermute | solution.py:39
  43.7 25.8 %collective-permute-start.4 = (bf16[128,4096]{1,0:T(8,128)(2,1)}, bf16[128,4096]{1,0:T(8,128)(2,1)S(1)}, u32[]{:S(2)}, u32[]{:S(2)}) collective-permute-start(bf16[128,4096]{1,0:T(8,128)(2,1)} %shard_map.42.refs_1_.refs_5_), channel_id=1, source_target_pairs={{0,48},{1,17},{2,50},{3,19},{4,52},{5,21},{6,54},{7,23},{8,56},{9,... | collective-permute-start | bytes 3145736 | tf_op jit(solution)/shard_map/ppermute | solution.py:39
  44.6 24.9 %collective-permute-start.2 = (bf16[128,4096]{1,0:T(8,128)(2,1)}, bf16[128,4096]{1,0:T(8,128)(2,1)S(1)}, u32[]{:S(2)}, u32[]{:S(2)}) collective-permute-start(bf16[128,4096]{1,0:T(8,128)(2,1)} %shard_map.42.refs_1_.refs_5_), channel_id=1, source_target_pairs={{0,12},{1,5},{2,14},{3,7},{4,0},{5,9},{6,2},{7,11},{8,4},{9,13},{1... | collective-permute-start | bytes 3145736 | tf_op jit(solution)/shard_map/ppermute | solution.py:39
  66.7 2.0 %collective-permute-start.6 = (bf16[64,4096]{1,0:T(8,128)(2,1)S(1)}, bf16[64,4096]{1,0:T(8,128)(2,1)S(1)}, u32[]{:S(2)}, u32[]{:S(2)}) collective-permute-start(bf16[64,4096]{1,0:T(8,128)(2,1)S(1)} %get-tuple-element.71), channel_id=1, source_target_pairs={{0,1},{1,0},{2,3},{3,2},{4,5},{5,4},{6,7},{7,6},{8,9},{9,8},{10,11... | collective-permute-start | bytes 1572872 | tf_op jit(solution)/shard_map/ppermute | solution.py:39
  67.2 2.2 %collective-permute-start.7 = (bf16[64,4096]{1,0:T(8,128)(2,1)S(1)}, bf16[64,4096]{1,0:T(8,128)(2,1)S(1)}, u32[]{:S(2)}, u32[]{:S(2)}) collective-permute-start(bf16[64,4096]{1,0:T(8,128)(2,1)S(1)} %get-tuple-element.72), channel_id=1, source_target_pairs={{0,1},{1,0},{2,3},{3,2},{4,5},{5,4},{6,7},{7,6},{8,9},{9,8},{10,11... | collective-permute-start | bytes 1572872 | tf_op jit(solution)/shard_map/ppermute | solution.py:39
  69.6 27.7 %collective-permute-start.10 = (bf16[256,4096]{1,0:T(8,128)(2,1)S(1)}, bf16[256,4096]{1,0:T(8,128)(2,1)S(1)}, u32[]{:S(2)}, u32[]{:S(2)}) collective-permute-start(bf16[256,4096]{1,0:T(8,128)(2,1)S(1)} %shard_map.46), channel_id=1, source_target_pairs={{0,4},{1,13},{2,6},{3,15},{4,8},{5,1},{6,10},{7,3},{8,12},{9,5},{1... | collective-permute-start | bytes 6291464 | tf_op jit(solution)/shard_map/ppermute | solution.py:39
  69.7 7.1 %collective-permute-start.9 = (bf16[128,4096]{1,0:T(8,128)(2,1)S(1)}, bf16[128,4096]{1,0:T(8,128)(2,1)S(1)}, u32[]{:S(2)}, u32[]{:S(2)}) collective-permute-start(bf16[128,4096]{1,0:T(8,128)(2,1)S(1)} %collective-permute-done.2.refs_4_), channel_id=1, source_target_pairs={{0,1},{1,0},{2,3},{3,2},{4,5},{5,4},{6,7},{7,6},{8,9},{9,8},{10,11... | collective-permute-start | bytes 3145736 | tf_op jit(solution)/shard_map/ppermute | solution.py:39
  70.5 6.2 %collective-permute-start.8 = (bf16[128,4096]{1,0:T(8,128)(2,1)S(1)}, bf16[128,4096]{1,0:T(8,128)(2,1)S(1)}, u32[]{:S(2)}, u32[]{:S(2)}) collective-permute-start(bf16[128,4096]{1,0:T(8,128)(2,1)S(1)} %collective-permute-done.1.refs_3_.refs_0_), channel_id=1, source_target_pairs={{0,1},{1,0},{2,3},{3,2},{4,5},{5,4},{6,7},{7,6},{8,9},{9,8},{10,11... | collective-permute-start | bytes 3145736 | tf_op jit(solution)/shard_map/ppermute | solution.py:39
  70.6 26.8 %collective-permute-start.12 = (bf16[128,4096]{1,0:T(8,128)(2,1)S(1)}, bf16[128,4096]{1,0:T(8,128)(2,1)S(1)}, u32[]{:S(2)}, u32[]{:S(2)}) collective-permute-start(bf16[128,4096]{1,0:T(8,128)(2,1)S(1)} %collective-permute-done.5.refs_0_.refs_1_), channel_id=1, source_target_pairs={{0,66},{1,67},{2,64},{3,65},{4,70},{5,71},{6,68},{7,69},{8,74},{9,... | collective-permute-start | bytes 3145736 | tf_op jit(solution)/shard_map/ppermute | solution.py:39
  71.4 25.9 %collective-permute-start.11 = (bf16[128,4096]{1,0:T(8,128)(2,1)S(1)}, bf16[128,4096]{1,0:T(8,128)(2,1)S(1)}, u32[]{:S(2)}, u32[]{:S(2)}) collective-permute-start(bf16[128,4096]{1,0:T(8,128)(2,1)S(1)} %collective-permute-done.1.refs_3_.refs_0_), channel_id=1, source_target_pairs={{0,2},{1,3},{2,0},{3,1},{4,6},{5,7},{6,4},{7,5},{8,10},{9,11},{10,... | collective-permute-start | bytes 3145736 | tf_op jit(solution)/shard_map/ppermute | solution.py:39
  79.8 17.5 %collective-permute-start.13 = (bf16[64,4096]{1,0:T(8,128)(2,1)S(1)}, bf16[64,4096]{1,0:T(8,128)(2,1)S(1)}, u32[]{:S(2)}, u32[]{:S(2)}) collective-permute-start(bf16[64,4096]{1,0:T(8,128)(2,1)S(1)} %get-tuple-element.88), channel_id=1, source_target_pairs={{0,16},{1,49},{2,18},{3,51},{4,20},{5,53},{6,22},{7,55},{8,24},{9,... | collective-permute-start | bytes 1572872 | tf_op jit(solution)/shard_map/ppermute | solution.py:39
  79.9 17.4 %collective-permute-start.14 = (bf16[64,4096]{1,0:T(8,128)(2,1)S(1)}, bf16[64,4096]{1,0:T(8,128)(2,1)S(1)}, u32[]{:S(2)}, u32[]{:S(2)}) collective-permute-start(bf16[64,4096]{1,0:T(8,128)(2,1)S(1)} %get-tuple-element.89), channel_id=1, source_target_pairs={{0,16},{1,49},{2,18},{3,51},{4,20},{5,53},{6,22},{7,55},{8,24},{9,... | collective-permute-start | bytes 1572872 | tf_op jit(solution)/shard_map/ppermute | solution.py:39
  97.4 8.3 %collective-permute-start.15 = (bf16[256,4096]{1,0:T(8,128)(2,1)S(1)}, bf16[256,4096]{1,0:T(8,128)(2,1)S(1)}, u32[]{:S(2)}, u32[]{:S(2)}) collective-permute-start(bf16[256,4096]{1,0:T(8,128)(2,1)S(1)} %collective-permute-done.10.refs_1_), channel_id=1, source_target_pairs={{0,1},{1,0},{2,3},{3,2},{4,5},{5,4},{6,7},{7,6},{8,9},{9,8},{10,11... | collective-permute-start | bytes 6291464 | tf_op jit(solution)/shard_map/ppermute | solution.py:39
  97.5 8.2 %collective-permute-start.16 = (bf16[128,4096]{1,0:T(8,128)(2,1)S(1)}, bf16[128,4096]{1,0:T(8,128)(2,1)S(1)}, u32[]{:S(2)}, u32[]{:S(2)}) collective-permute-start(bf16[128,4096]{1,0:T(8,128)(2,1)S(1)} %collective-permute-done.11.refs_1_), channel_id=1, source_target_pairs={{0,1},{1,0},{2,3},{3,2},{4,5},{5,4},{6,7},{7,6},{8,9},{9,8},{10,11... | collective-permute-start | bytes 3145736 | tf_op jit(solution)/shard_map/ppermute | solution.py:39
  97.9 16.0 %collective-permute-start.17 = (bf16[128,4096]{1,0:T(8,128)(2,1)S(1)}, bf16[128,4096]{1,0:T(8,128)(2,1)S(1)}, u32[]{:S(2)}, u32[]{:S(2)}) collective-permute-start(bf16[128,4096]{1,0:T(8,128)(2,1)S(1)} %collective-permute-done.11.refs_1_), channel_id=1, source_target_pairs={{0,4},{1,13},{2,6},{3,15},{4,8},{5,1},{6,10},{7,3},{8,12},{9,5},{1... | collective-permute-start | bytes 3145736 | tf_op jit(solution)/shard_map/ppermute | solution.py:39
  99.0 16.0 %collective-permute-start.20 = (bf16[128,4096]{1,0:T(8,128)(2,1)S(1)}, bf16[128,4096]{1,0:T(8,128)(2,1)S(1)}, u32[]{:S(2)}, u32[]{:S(2)}) collective-permute-start(bf16[128,4096]{1,0:T(8,128)(2,1)S(1)} %collective-permute-done.12.refs_4_), channel_id=1, source_target_pairs={{0,16},{1,49},{2,18},{3,51},{4,20},{5,53},{6,22},{7,55},{8,24},{9,... | collective-permute-start | bytes 3145736 | tf_op jit(solution)/shard_map/ppermute | solution.py:39
  99.4 26.6 %collective-permute-start.22 = (bf16[128,4096]{1,0:T(8,128)(2,1)S(1)}, bf16[128,4096]{1,0:T(8,128)(2,1)S(1)}, u32[]{:S(2)}, u32[]{:S(2)}) collective-permute-start(bf16[128,4096]{1,0:T(8,128)(2,1)S(1)} %shard_map.48.refs_4_), channel_id=1, source_target_pairs={{0,64},{1,65},{2,66},{3,67},{4,68},{5,69},{6,70},{7,71},{8,72},{9,... | collective-permute-start | bytes 3145736 | tf_op jit(solution)/shard_map/ppermute | solution.py:39
  109.7 16.3 %collective-permute-start.21 = (bf16[128,4096]{1,0:T(8,128)(2,1)S(1)}, bf16[128,4096]{1,0:T(8,128)(2,1)S(1)}, u32[]{:S(2)}, u32[]{:S(2)}) collective-permute-start(bf16[128,4096]{1,0:T(8,128)(2,1)S(1)} %collective-permute-done.12.refs_4_), channel_id=1, source_target_pairs={{0,48},{1,17},{2,50},{3,19},{4,52},{5,21},{6,54},{7,23},{8,56},{9,... | collective-permute-start | bytes 3145736 | tf_op jit(solution)/shard_map/ppermute | solution.py:39
  114.1 5.6 %collective-permute-start.18 = (bf16[64,4096]{1,0:T(8,128)(2,1)S(1)}, bf16[64,4096]{1,0:T(8,128)(2,1)S(1)}, u32[]{:S(2)}, u32[]{:S(2)}) collective-permute-start(bf16[64,4096]{1,0:T(8,128)(2,1)S(1)} %get-tuple-element.110), channel_id=1, source_target_pairs={{0,1},{1,0},{2,3},{3,2},{4,5},{5,4},{6,7},{7,6},{8,9},{9,8},{10,11... | collective-permute-start | bytes 1572872 | tf_op jit(solution)/shard_map/ppermute | solution.py:39
  114.2 5.6 %collective-permute-start.19 = (bf16[64,4096]{1,0:T(8,128)(2,1)S(1)}, bf16[64,4096]{1,0:T(8,128)(2,1)S(1)}, u32[]{:S(2)}, u32[]{:S(2)}) collective-permute-start(bf16[64,4096]{1,0:T(8,128)(2,1)S(1)} %get-tuple-element.111), channel_id=1, source_target_pairs={{0,1},{1,0},{2,3},{3,2},{4,5},{5,4},{6,7},{7,6},{8,9},{9,8},{10,11... | collective-permute-start | bytes 1572872 | tf_op jit(solution)/shard_map/ppermute | solution.py:39
  133.2 1.7 %collective-permute-start.23 = (f32[16,128]{1,0:T(8,128)S(1)}, f32[16,128]{1,0:T(8,128)S(1)}, u32[]{:S(2)}, u32[]{:S(2)}) collective-permute-start(f32[16,128]{1,0:T(8,128)S(1)} %get-tuple-element.128), channel_id=1, source_target_pairs={{0,1},{1,0},{2,3},{3,2},{4,5},{5,4},{6,7},{7,6},{8,9},{9,8},{10,11... | collective-permute-start | bytes 24584 | tf_op jit(solution)/shard_map/ppermute | solution.py:39
  134.9 5.5 %collective-permute-start.26 = (f32[16,128]{1,0:T(8,128)S(1)}, f32[16,128]{1,0:T(8,128)S(1)}, u32[]{:S(2)}, u32[]{:S(2)}) collective-permute-start(f32[16,128]{1,0:T(8,128)S(1)} %max.15), channel_id=1, source_target_pairs={{0,6},{1,7},{2,4},{3,5},{4,2},{5,3},{6,0},{7,1},{8,14},{9,15},{10,... | collective-permute-start | bytes 24584 | tf_op jit(solution)/shard_map/ppermute | solution.py:39
  135.9 4.6 %collective-permute-start.25 = (f32[16,128]{1,0:T(8,128)S(1)}, f32[16,128]{1,0:T(8,128)S(1)}, u32[]{:S(2)}, u32[]{:S(2)}) collective-permute-start(f32[16,128]{1,0:T(8,128)S(1)} %max.15), channel_id=1, source_target_pairs={{0,4},{1,5},{2,6},{3,7},{4,0},{5,1},{6,2},{7,3},{8,12},{9,13},{10,... | collective-permute-start | bytes 24584 | tf_op jit(solution)/shard_map/ppermute | solution.py:39
  137.2 3.7 %collective-permute-start.24 = (f32[16,128]{1,0:T(8,128)S(1)}, f32[16,128]{1,0:T(8,128)S(1)}, u32[]{:S(2)}, u32[]{:S(2)}) collective-permute-start(f32[16,128]{1,0:T(8,128)S(1)} %max.15), channel_id=1, source_target_pairs={{0,2},{1,3},{2,0},{3,1},{4,6},{5,7},{6,4},{7,5},{8,10},{9,11},{10,... | collective-permute-start | bytes 24584 | tf_op jit(solution)/shard_map/ppermute | solution.py:39
  140.8 6.6 %collective-permute-start.27 = (f32[16,128]{1,0:T(8,128)S(1)}, f32[16,128]{1,0:T(8,128)S(1)}, u32[]{:S(2)}, u32[]{:S(2)}) collective-permute-start(f32[16,128]{1,0:T(8,128)S(1)} %maximum_maximum_fusion), channel_id=1, source_target_pairs={{0,12},{1,13},{2,14},{3,15},{4,8},{5,9},{6,10},{7,11},{8,4},{9,5},... | collective-permute-start | bytes 24584 | tf_op jit(solution)/shard_map/ppermute | solution.py:39

commit v6 on v5

--- a/solution.py
+++ b/solution.py
@@ -1,5 +1,6 @@
 import jax
 import jax.numpy as jnp
+import numpy as np
 from jax import lax
 from jax.experimental import pallas as pl
 from jax.experimental.pallas import tpu as pltpu
@@ -344,42 +345,44 @@
     yh, z = gr // 4, gr % 4
     x, yl, core = gc // 4, (gc // 2) % 2, gc % 2
 
-    def row_at(dx=0, dy=0, dc=0):
-        return ((x + dx + 4) % 4) * 4 + ((yl + dy) % 2) * 2 + (core + dc) % 2
-
-    def col_at(dy=0, dz=0):
-        return ((yh + dy) % 2) * 4 + (z + dz + 4) % 4
-
     ring = 1 - 2 * core
     rows_at = [
-        [row_at(), row_at(dc=1), row_at(-ring), row_at(ring)],
-        [row_at(dy=1), row_at(dy=1, dc=1), row_at(ring, dc=1), row_at(-ring, dc=1)],
-        [row_at(2), row_at(-ring, 1, 1), row_at(2, dc=1), row_at(ring, 1)],
-        [row_at(-ring, 1), row_at(ring, 1, 1), row_at(2, 1), row_at(2, 1, 1)],
+        [(0, 0, 0, 0), (0, 0, 0, 1), (-1, 0, 0, 0), (1, 0, 0, 0)],
+        [(0, 0, 1, 0), (0, 0, 1, 1), (1, 0, 0, 1), (-1, 0, 0, 1)],
+        [(0, 2, 0, 0), (-1, 0, 1, 1), (0, 2, 0, 1), (1, 0, 1, 0)],
+        [(-1, 0, 1, 0), (1, 0, 1, 1), (0, 2, 1, 0), (0, 2, 1, 1)],
     ]
     cols_at = [
-        [col_at(), col_at(dz=-ring)],
-        [col_at(dz=ring), col_at(dz=2)],
-        [col_at(1), col_at(1, -ring)],
-        [col_at(1, ring), col_at(1, 2)],
+        [(0, 0, 0), (-1, 0, 0)],
+        [(1, 0, 0), (0, 2, 0)],
+        [(0, 0, 1), (-1, 0, 1)],
+        [(1, 0, 1), (0, 2, 1)],
     ]
-
-    def places(rows, cols):
-        flat_list = sum([rows_at[r] for r in rows], []) + sum([cols_at[c] for c in cols], [])
-        return flat_list
-
-    lists = [
-        places([0], [0]),
-        places([1], [0]),
-        places([0, 1], [1]),
-        places([2], [0, 1]),
-        places([0, 1, 2], [2]),
-        places([3], [0, 1, 2]),
-        places([0, 1, 2, 3], [3]),
+    calls = [
+        ([0], [0]),
+        ([1], [0]),
+        ([0, 1], [1]),
+        ([2], [0, 1]),
+        ([0, 1, 2], [2]),
+        ([3], [0, 1, 2]),
+        ([0, 1, 2, 3], [3]),
     ]
-    table = jnp.stack([jnp.stack(p + [p[0]] * (18 - len(p))) for p in lists]).astype(jnp.int32)
+    codes = np.zeros((len(calls), 18), np.int32)
+    for n, (rows, cols) in enumerate(calls):
+        entries = [(0, *w) for r in rows for w in rows_at[r]]
+        entries += [(1, *w, 0) for c in cols for w in cols_at[c]]
+        for m, (kind, turn, step, over_y, over_c) in enumerate(entries):
+            codes[n, m] = kind * 64 + (turn + 1) * 16 + step * 4 + over_y * 2 + over_c
+    code = jnp.asarray(codes)
+    turn = (code // 16 % 4 - 1) * ring + code // 4 % 4 + 4
+    over_y, over_c = code // 2 % 2, code % 2
+    table = jnp.where(
+        code >= 64,
+        ((yh + over_y) % 2) * 4 + (z + turn) % 4,
+        ((x + turn) % 4) * 4 + ((yl + over_y) % 2) * 2 + (core + over_c) % 2,
+    ).astype(jnp.int32)
     packed, table = fence(packed, table)
-    where = [(table, n) for n in range(len(lists))]
+    where = [(table, n) for n in range(len(calls))]
     arrived = lax.all_to_all(
         packed, AXES, split_axis=0, concat_axis=0, tiled=True
     )

time: 149 us -> 148 us (level)
  no operation moved by 1% of the time
where the time goes in v6:
time: 148 us
  waiting for transfers between devices  44.8 us (30%)
  Pallas kernels  40.1 us (27%)
  blocking collectives  32.9 us (22%)
  starting transfers between devices  27.5 us (19%)
    ppermute x28, waiting for transfers between devices, send(): return lax.ppermute(value, AXES, pairs)  44.8 us
    all_to_all x1, blocking collectives, per_device(): lax.all_to_all(packed, AXES, split_axis=0, concat_axis=0, tiled=True)  32.9 us
    pallas_call x7, Pallas kernels, block_call(): pl.pallas_call(make_block_kernel(line, row_sizes, col_sizes, fresh_rows,...  31.3 us
    ppermute x28, starting transfers between devices, send(): return lax.ppermute(value, AXES, pairs)  27.5 us
    pallas_call x1, Pallas kernels, per_device(): pl.pallas_call(place_kernel, out_shape=jax.ShapeDtypeStruct((count, width...  3.17 us
    pallas_call x1, Pallas kernels, per_device(): pl.pallas_call(pack_kernel, out_shape=jax.ShapeDtypeStruct((count, width...  3.02 us
  transfers between devices with their start and end apart: 28, of which 12 were waited for; matrix products, arithmetic and copies ran while one was open for 0% of the time, Pallas kernels for 18%

profile of v6, /device:TPU:0, one launch (start us, length us, event | category | flops | bytes accessed | tf_op | source)
XLA Modules:
  0.0 147.7 jit_solution(10697677492833691326)
XLA Ops:
  0.7 3.0 %shard_map.50 = bf16[128,40,128]{2,1,0:T(8,128)(2,1)} custom-call(s32[1,128]{1,0:T(1,128)} %bitcast.3, bf16[128,4096]{1,0:T(8,128)(2,1)} %items_ref.1), custom_call_target="tpu_custom_call" | custom-call | tf_op jit(solution)/shard_map/pallas_call | solution.py:338
  3.7 0.8 fusion.2.refs_0_
  4.5 32.9 %all_to_all.5.in_ref = bf16[128,40,128]{2,1,0:T(8,128)(2,1)} all-to-all(bf16[128,40,128]{2,1,0:T(8,128)(2,1)} %shard_map.50), channel_id=1, replica_groups=mesh['gr'=8,'gc'=16] {'gr','gc'}, dimensions={0} | all-to-all | bytes 2621440 | tf_op jit(solution)/shard_map/all_to_all | solution.py:386
  37.4 3.2 %shard_map.51.refs_1_.refs_5_ = bf16[128,4096]{1,0:T(8,128)(2,1)} custom-call(bf16[128,40,128]{2,1,0:T(8,128)(2,1)} %all_to_all.5.in_ref), custom_call_target="tpu_custom_call" | custom-call | tf_op jit(solution)/shard_map/pallas_call | solution.py:389
  41.7 1.8 %collective-permute-done.refs_2_ = bf16[128,4096]{1,0:T(8,128)(2,1)S(1)} collective-permute-done((bf16[128,4096]{1,0:T(8,128)(2,1)}, bf16[128,4096]{1,0:T(8,128)(2,1)S(1)}, u32[]{:S(2)}, u32[]{:S(2)}) %collective-permute-start) | collective-permute-done | bytes 1048608 | tf_op jit(solution)/shard_map/ppermute | solution.py:40
  43.5 0.9 collective-permute-start.4
  44.4 3.2 %collective-permute-start.2 = (bf16[128,4096]{1,0:T(8,128)(2,1)}, bf16[128,4096]{1,0:T(8,128)(2,1)S(1)}, u32[]{:S(2)}, u32[]{:S(2)}) collective-permute-start(bf16[128,4096]{1,0:T(8,128)(2,1)} %shard_map.51.refs_1_.refs_5_), channel_id=1, source_target_pairs={{0,12},{1,5},{2,14},{3,7},{4,0},{5,9},{6,2},{7,11},{8,4},{9,13},{1... | collective-permute-start | bytes 3145736 | tf_op jit(solution)/shard_map/ppermute | solution.py:40
  47.6 18.8 %collective-permute-done.5.refs_0_.refs_1_ = bf16[128,4096]{1,0:T(8,128)(2,1)S(1)} collective-permute-done((bf16[128,4096]{1,0:T(8,128)(2,1)}, bf16[128,4096]{1,0:T(8,128)(2,1)S(1)}, u32[]{:S(2)}, u32[]{:S(2)}) %collective-permute-start.5) | collective-permute-done | bytes 1048608 | tf_op jit(solution)/shard_map/ppermute | solution.py:40
  67.1 1.4 collective-permute-done.6.refs_2_.refs_1_
  69.5 0.9 collective-permute-start.9
  70.4 0.8 collective-permute-start.12
  71.2 1.7 %collective-permute-start.11 = (bf16[128,4096]{1,0:T(8,128)(2,1)S(1)}, bf16[128,4096]{1,0:T(8,128)(2,1)S(1)}, u32[]{:S(2)}, u32[]{:S(2)}) collective-permute-start(bf16[128,4096]{1,0:T(8,128)(2,1)S(1)} %collective-permute-done.1.refs_3_.refs_0_), channel_id=1, source_target_pairs={{0,2},{1,3},{2,0},{3,1},{4,6},{5,7},{6,4},{7,5},{8,10},{9,11},{10,... | collective-permute-start | bytes 3145736 | tf_op jit(solution)/shard_map/ppermute | solution.py:40
  72.9 3.6 %shard_map.53 = (bf16[2048,1024]{1,0:T(8,128)(2,1)S(1)}, f32[512,128]{1,0:T(8,128)S(1)}, bf16[512,4096]{1,0:T(8,128)(2,1)S(1)}, f32[512,128]{1,0:T(8,128)S(1)}, ...) custom-call(s32[7,18]{1,0:T(8,128)S(1)} %fusion.2.refs_0_, bf16[128,4096]{1,0:T(8,128)(2,1)S(1)} %copy-done, ...), custom_call_target="tpu_custom_call" | custom-call | flops 134217728 | bytes 262144 | tf_op jit(solution)/shard_map/pallas_call | solution.py:281
  76.6 2.9 %shard_map.54 = (bf16[2048,1024]{1,0:T(8,128)(2,1)S(1)}, f32[512,128]{1,0:T(8,128)S(1)}, bf16[512,4096]{1,0:T(8,128)(2,1)S(1)}, f32[512,128]{1,0:T(8,128)S(1)}) custom-call(s32[7,18]{1,0:T(8,128)S(1)} %fusion.2.refs_0_, bf16[128,4096]{1,0:T(8,128)(2,1)S(1)} %collective-permute-done.5.refs_0_.refs_1_, ...), custom_call_target="tpu_custom_call", output_to_operand_aliasing={{0}: (8, {})} | custom-call | flops 134217728 | bytes 262144 | tf_op jit(solution)/shard_map/pallas_call | solution.py:281
  80.3 16.9 %collective-permute-done.12.refs_4_ = bf16[128,4096]{1,0:T(8,128)(2,1)S(1)} collective-permute-done((bf16[128,4096]{1,0:T(8,128)(2,1)S(1)}, bf16[128,4096]{1,0:T(8,128)(2,1)S(1)}, u32[]{:S(2)}, u32[]{:S(2)}) %collective-permute-start.12) | collective-permute-done | bytes 1048608 | tf_op jit(solution)/shard_map/ppermute | solution.py:40
  97.8 1.0 collective-permute-start.17
  99.2 2.6 %collective-permute-start.22 = (bf16[128,4096]{1,0:T(8,128)(2,1)S(1)}, bf16[128,4096]{1,0:T(8,128)(2,1)S(1)}, u32[]{:S(2)}, u32[]{:S(2)}) collective-permute-start(bf16[128,4096]{1,0:T(8,128)(2,1)S(1)} %shard_map.57.refs_4_), channel_id=1, source_target_pairs={{0,64},{1,65},{2,66},{3,67},{4,68},{5,69},{6,70},{7,71},{8,72},{9,... | collective-permute-start | bytes 3145736 | tf_op jit(solution)/shard_map/ppermute | solution.py:40
  101.8 3.6 %shard_map.58 = (bf16[2048,1024]{1,0:T(8,128)(2,1)S(1)}, f32[512,128]{1,0:T(8,128)S(1)}, f32[512,128]{1,0:T(8,128)S(1)}, bf16[256,4096]{1,0:T(8,128)(2,1)S(1)}, f32[8,256]{1,0:T(8,128)S(1)}) custom-call(s32[7,18]{1,0:T(8,128)S(1)} %fusion.2.refs_0_, bf16[512,4096]{1,0:T(8,128)(2,1)S(1)} %get-tuple-element.77.refs_1_, ...), custom_call_target="tpu_custom_call", output_to_operand_aliasing={{0}: (9, {})} | custom-call | flops 268435456 | bytes 524288 | tf_op jit(solution)/shard_map/pallas_call | solution.py:281
  105.4 4.0 %shard_map.59 = (bf16[2048,1024]{1,0:T(8,128)(2,1)S(1)}, f32[512,128]{1,0:T(8,128)S(1)}, bf16[512,4096]{1,0:T(8,128)(2,1)S(1)}, f32[512,128]{1,0:T(8,128)S(1)}) custom-call(s32[7,18]{1,0:T(8,128)S(1)} %fusion.2.refs_0_, bf16[256,4096]{1,0:T(8,128)(2,1)S(1)} %collective-permute-done.10.refs_1_, ...), custom_call_target="tpu_custom_call", output_to_operand_aliasing={{0}: (7, {})} | custom-call | flops 268435456 | bytes 524288 | tf_op jit(solution)/shard_map/pallas_call | solution.py:281
  109.5 3.3 %collective-permute-start.21 = (bf16[128,4096]{1,0:T(8,128)(2,1)S(1)}, bf16[128,4096]{1,0:T(8,128)(2,1)S(1)}, u32[]{:S(2)}, u32[]{:S(2)}) collective-permute-start(bf16[128,4096]{1,0:T(8,128)(2,1)S(1)} %collective-permute-done.12.refs_4_), channel_id=1, source_target_pairs={{0,48},{1,17},{2,50},{3,19},{4,52},{5,21},{6,54},{7,23},{8,56},{9,... | collective-permute-start | bytes 3145736 | tf_op jit(solution)/shard_map/ppermute | solution.py:40
  112.8 1.0 collective-permute-done.17.refs_0_.refs_3_
  114.8 4.7 %shard_map.61 = (bf16[2048,1024]{1,0:T(8,128)(2,1)S(1)}, f32[512,128]{1,0:T(8,128)S(1)}, f32[512,128]{1,0:T(8,128)S(1)}, f32[512,128]{1,0:T(8,128)S(1)}, bf16[25...) custom-call(s32[7,18]{1,0:T(8,128)S(1)} %fusion.2.refs_0_, ...), custom_call_target="tpu_custom_call", output_to_operand_aliasing={{0}: (12, {})} | custom-call | flops 402653184 | bytes 786432 | tf_op jit(solution)/shard_map/pallas_call | solution.py:281
  119.5 5.3 %shard_map.62 = (bf16[2048,1024]{1,0:T(8,128)(2,1)S(1)}, f32[512,128]{1,0:T(8,128)S(1)}, bf16[512,4096]{1,0:T(8,128)(2,1)S(1)}, f32[512,128]{1,0:T(8,128)S(1)}) custom-call(s32[7,18]{1,0:T(8,128)S(1)} %fusion.2.refs_0_, bf16[128,4096]{1,0:T(8,128)(2,1)S(1)} %collective-permute-done.11.refs_1_, ...), custom_call_target="tpu_custom_call", output_to_operand_aliasing={{0}: (12, {})} | custom-call | flops 402653184 | bytes 786432 | tf_op jit(solution)/shard_map/pallas_call | solution.py:281
  124.8 0.8 collective-permute-done.22.refs_6_
  125.6 7.2 %shard_map.63 = (bf16[2048,1024]{1,0:T(8,128)(2,1)S(1)}, f32[16,128]{1,0:T(8,128)S(1)}, bf16[256,4096]{1,0:T(8,128)(2,1)}, f32[8,256]{1,0:T(8,128)}) custom-call(s32[7,18]{1,0:T(8,128)S(1)} %fusion.2.refs_0_, bf16[512,4096]{1,0:T(8,128)(2,1)S(1)} %get-tuple-element.77.refs_1_, ...), custom_call_target="tpu_custom_call", output_to_operand_aliasing={{0}: (15, {})} | custom-call | flops 536870912 | bytes 1048576 | tf_op jit(solution)/shard_map/pallas_call | solution.py:281
  132.8 1.2 collective-permute-start.23
  134.0 0.8 collective-permute-done.23
  135.5 1.5 collective-permute-start.25
  137.0 1.4 collective-permute-start.24
  138.3 2.0 %shard_map.64 = bf16[2048,1024]{1,0:T(8,128)(2,1)} custom-call(bf16[2048,1024]{1,0:T(8,128)(2,1)S(1)} %get-tuple-element.129.held_ref), custom_call_target="tpu_custom_call" | custom-call | bytes 8388608 | tf_op jit(solution)/shard_map/pallas_call | solution.py:315
  140.6 4.8 %collective-permute-start.27 = (f32[16,128]{1,0:T(8,128)S(1)}, f32[16,128]{1,0:T(8,128)S(1)}, u32[]{:S(2)}, u32[]{:S(2)}) collective-permute-start(f32[16,128]{1,0:T(8,128)S(1)} %maximum_maximum_fusion), channel_id=1, source_target_pairs={{0,12},{1,13},{2,14},{3,15},{4,8},{5,9},{6,10},{7,11},{8,4},{9,5},... | collective-permute-start | bytes 24584 | tf_op jit(solution)/shard_map/ppermute | solution.py:40
  145.4 1.6 %collective-permute-done.27 = f32[16,128]{1,0:T(8,128)S(1)} collective-permute-done((f32[16,128]{1,0:T(8,128)S(1)}, f32[16,128]{1,0:T(8,128)S(1)}, u32[]{:S(2)}, u32[]{:S(2)}) %collective-permute-start.27) | collective-permute-done | bytes 8224 | tf_op jit(solution)/shard_map/ppermute | solution.py:40
  (46 shorter events, 7.0 us)
Async XLA Ops:
  40.6 32.3 %copy-start = (bf16[128,4096]{1,0:T(8,128)(2,1)S(1)}, bf16[128,4096]{1,0:T(8,128)(2,1)}, u32[]{:S(2)}) copy-start(bf16[128,4096]{1,0:T(8,128)(2,1)} %shard_map.51.refs_1_.refs_5_) | copy-start | bytes 3145732
  40.6 2.9 %collective-permute-start = (bf16[128,4096]{1,0:T(8,128)(2,1)}, bf16[128,4096]{1,0:T(8,128)(2,1)S(1)}, u32[]{:S(2)}, u32[]{:S(2)}) collective-permute-start(bf16[128,4096]{1,0:T(8,128)(2,1)} %shard_map.51.refs_1_.refs_5_), channel_id=1, source_target_pairs={{0,1},{1,0},{2,3},{3,2},{4,5},{5,4},{6,7},{7,6},{8,9},{9,8},{10,11... | collective-permute-start | bytes 3145736 | tf_op jit(solution)/shard_map/ppermute | solution.py:40
  40.6 25.8 %collective-permute-start.5 = (bf16[128,4096]{1,0:T(8,128)(2,1)}, bf16[128,4096]{1,0:T(8,128)(2,1)S(1)}, u32[]{:S(2)}, u32[]{:S(2)}) collective-permute-start(bf16[128,4096]{1,0:T(8,128)(2,1)} %shard_map.51.refs_1_.refs_5_), channel_id=1, source_target_pairs={{0,2},{1,3},{2,0},{3,1},{4,6},{5,7},{6,4},{7,5},{8,10},{9,11},{10,... | collective-permute-start | bytes 3145736 | tf_op jit(solution)/shard_map/ppermute | solution.py:40
  41.1 25.9 %collective-permute-start.3 = (bf16[128,4096]{1,0:T(8,128)(2,1)}, bf16[128,4096]{1,0:T(8,128)(2,1)S(1)}, u32[]{:S(2)}, u32[]{:S(2)}) collective-permute-start(bf16[128,4096]{1,0:T(8,128)(2,1)} %shard_map.51.refs_1_.refs_5_), channel_id=1, source_target_pairs={{0,16},{1,49},{2,18},{3,51},{4,20},{5,53},{6,22},{7,55},{8,24},{9,... | collective-permute-start | bytes 3145736 | tf_op jit(solution)/shard_map/ppermute | solution.py:40
  41.1 25.9 %collective-permute-start.1 = (bf16[128,4096]{1,0:T(8,128)(2,1)}, bf16[128,4096]{1,0:T(8,128)(2,1)S(1)}, u32[]{:S(2)}, u32[]{:S(2)}) collective-permute-start(bf16[128,4096]{1,0:T(8,128)(2,1)} %shard_map.51.refs_1_.refs_5_), channel_id=1, source_target_pairs={{0,4},{1,13},{2,6},{3,15},{4,8},{5,1},{6,10},{7,3},{8,12},{9,5},{1... | collective-permute-start | bytes 3145736 | tf_op jit(solution)/shard_map/ppermute | solution.py:40
  43.5 25.8 %collective-permute-start.4 = (bf16[128,4096]{1,0:T(8,128)(2,1)}, bf16[128,4096]{1,0:T(8,128)(2,1)S(1)}, u32[]{:S(2)}, u32[]{:S(2)}) collective-permute-start(bf16[128,4096]{1,0:T(8,128)(2,1)} %shard_map.51.refs_1_.refs_5_), channel_id=1, source_target_pairs={{0,48},{1,17},{2,50},{3,19},{4,52},{5,21},{6,54},{7,23},{8,56},{9,... | collective-permute-start | bytes 3145736 | tf_op jit(solution)/shard_map/ppermute | solution.py:40
  44.4 24.8 %collective-permute-start.2 = (bf16[128,4096]{1,0:T(8,128)(2,1)}, bf16[128,4096]{1,0:T(8,128)(2,1)S(1)}, u32[]{:S(2)}, u32[]{:S(2)}) collective-permute-start(bf16[128,4096]{1,0:T(8,128)(2,1)} %shard_map.51.refs_1_.refs_5_), channel_id=1, source_target_pairs={{0,12},{1,5},{2,14},{3,7},{4,0},{5,9},{6,2},{7,11},{8,4},{9,13},{1... | collective-permute-start | bytes 3145736 | tf_op jit(solution)/shard_map/ppermute | solution.py:40
  66.5 2.0 %collective-permute-start.6 = (bf16[64,4096]{1,0:T(8,128)(2,1)S(1)}, bf16[64,4096]{1,0:T(8,128)(2,1)S(1)}, u32[]{:S(2)}, u32[]{:S(2)}) collective-permute-start(bf16[64,4096]{1,0:T(8,128)(2,1)S(1)} %get-tuple-element.71), channel_id=1, source_target_pairs={{0,1},{1,0},{2,3},{3,2},{4,5},{5,4},{6,7},{7,6},{8,9},{9,8},{10,11... | collective-permute-start | bytes 1572872 | tf_op jit(solution)/shard_map/ppermute | solution.py:40
  67.0 2.2 %collective-permute-start.7 = (bf16[64,4096]{1,0:T(8,128)(2,1)S(1)}, bf16[64,4096]{1,0:T(8,128)(2,1)S(1)}, u32[]{:S(2)}, u32[]{:S(2)}) collective-permute-start(bf16[64,4096]{1,0:T(8,128)(2,1)S(1)} %get-tuple-element.72), channel_id=1, source_target_pairs={{0,1},{1,0},{2,3},{3,2},{4,5},{5,4},{6,7},{7,6},{8,9},{9,8},{10,11... | collective-permute-start | bytes 1572872 | tf_op jit(solution)/shard_map/ppermute | solution.py:40
  69.4 27.7 %collective-permute-start.10 = (bf16[256,4096]{1,0:T(8,128)(2,1)S(1)}, bf16[256,4096]{1,0:T(8,128)(2,1)S(1)}, u32[]{:S(2)}, u32[]{:S(2)}) collective-permute-start(bf16[256,4096]{1,0:T(8,128)(2,1)S(1)} %shard_map.55), channel_id=1, source_target_pairs={{0,4},{1,13},{2,6},{3,15},{4,8},{5,1},{6,10},{7,3},{8,12},{9,5},{1... | collective-permute-start | bytes 6291464 | tf_op jit(solution)/shard_map/ppermute | solution.py:40
  69.5 7.1 %collective-permute-start.9 = (bf16[128,4096]{1,0:T(8,128)(2,1)S(1)}, bf16[128,4096]{1,0:T(8,128)(2,1)S(1)}, u32[]{:S(2)}, u32[]{:S(2)}) collective-permute-start(bf16[128,4096]{1,0:T(8,128)(2,1)S(1)} %collective-permute-done.2.refs_4_), channel_id=1, source_target_pairs={{0,1},{1,0},{2,3},{3,2},{4,5},{5,4},{6,7},{7,6},{8,9},{9,8},{10,11... | collective-permute-start | bytes 3145736 | tf_op jit(solution)/shard_map/ppermute | solution.py:40
  70.4 6.2 %collective-permute-start.8 = (bf16[128,4096]{1,0:T(8,128)(2,1)S(1)}, bf16[128,4096]{1,0:T(8,128)(2,1)S(1)}, u32[]{:S(2)}, u32[]{:S(2)}) collective-permute-start(bf16[128,4096]{1,0:T(8,128)(2,1)S(1)} %collective-permute-done.1.refs_3_.refs_0_), channel_id=1, source_target_pairs={{0,1},{1,0},{2,3},{3,2},{4,5},{5,4},{6,7},{7,6},{8,9},{9,8},{10,11... | collective-permute-start | bytes 3145736 | tf_op jit(solution)/shard_map/ppermute | solution.py:40
  70.4 26.8 %collective-permute-start.12 = (bf16[128,4096]{1,0:T(8,128)(2,1)S(1)}, bf16[128,4096]{1,0:T(8,128)(2,1)S(1)}, u32[]{:S(2)}, u32[]{:S(2)}) collective-permute-start(bf16[128,4096]{1,0:T(8,128)(2,1)S(1)} %collective-permute-done.5.refs_0_.refs_1_), channel_id=1, source_target_pairs={{0,66},{1,67},{2,64},{3,65},{4,70},{5,71},{6,68},{7,69},{8,74},{9,... | collective-permute-start | bytes 3145736 | tf_op jit(solution)/shard_map/ppermute | solution.py:40
  71.2 25.9 %collective-permute-start.11 = (bf16[128,4096]{1,0:T(8,128)(2,1)S(1)}, bf16[128,4096]{1,0:T(8,128)(2,1)S(1)}, u32[]{:S(2)}, u32[]{:S(2)}) collective-permute-start(bf16[128,4096]{1,0:T(8,128)(2,1)S(1)} %collective-permute-done.1.refs_3_.refs_0_), channel_id=1, source_target_pairs={{0,2},{1,3},{2,0},{3,1},{4,6},{5,7},{6,4},{7,5},{8,10},{9,11},{10,... | collective-permute-start | bytes 3145736 | tf_op jit(solution)/shard_map/ppermute | solution.py:40
  79.6 17.5 %collective-permute-start.13 = (bf16[64,4096]{1,0:T(8,128)(2,1)S(1)}, bf16[64,4096]{1,0:T(8,128)(2,1)S(1)}, u32[]{:S(2)}, u32[]{:S(2)}) collective-permute-start(bf16[64,4096]{1,0:T(8,128)(2,1)S(1)} %get-tuple-element.88), channel_id=1, source_target_pairs={{0,16},{1,49},{2,18},{3,51},{4,20},{5,53},{6,22},{7,55},{8,24},{9,... | collective-permute-start | bytes 1572872 | tf_op jit(solution)/shard_map/ppermute | solution.py:40
  79.7 17.4 %collective-permute-start.14 = (bf16[64,4096]{1,0:T(8,128)(2,1)S(1)}, bf16[64,4096]{1,0:T(8,128)(2,1)S(1)}, u32[]{:S(2)}, u32[]{:S(2)}) collective-permute-start(bf16[64,4096]{1,0:T(8,128)(2,1)S(1)} %get-tuple-element.89), channel_id=1, source_target_pairs={{0,16},{1,49},{2,18},{3,51},{4,20},{5,53},{6,22},{7,55},{8,24},{9,... | collective-permute-start | bytes 1572872 | tf_op jit(solution)/shard_map/ppermute | solution.py:40
  97.2 8.3 %collective-permute-start.15 = (bf16[256,4096]{1,0:T(8,128)(2,1)S(1)}, bf16[256,4096]{1,0:T(8,128)(2,1)S(1)}, u32[]{:S(2)}, u32[]{:S(2)}) collective-permute-start(bf16[256,4096]{1,0:T(8,128)(2,1)S(1)} %collective-permute-done.10.refs_1_), channel_id=1, source_target_pairs={{0,1},{1,0},{2,3},{3,2},{4,5},{5,4},{6,7},{7,6},{8,9},{9,8},{10,11... | collective-permute-start | bytes 6291464 | tf_op jit(solution)/shard_map/ppermute | solution.py:40
  97.3 8.1 %collective-permute-start.16 = (bf16[128,4096]{1,0:T(8,128)(2,1)S(1)}, bf16[128,4096]{1,0:T(8,128)(2,1)S(1)}, u32[]{:S(2)}, u32[]{:S(2)}) collective-permute-start(bf16[128,4096]{1,0:T(8,128)(2,1)S(1)} %collective-permute-done.11.refs_1_), channel_id=1, source_target_pairs={{0,1},{1,0},{2,3},{3,2},{4,5},{5,4},{6,7},{7,6},{8,9},{9,8},{10,11... | collective-permute-start | bytes 3145736 | tf_op jit(solution)/shard_map/ppermute | solution.py:40
  97.8 16.0 %collective-permute-start.17 = (bf16[128,4096]{1,0:T(8,128)(2,1)S(1)}, bf16[128,4096]{1,0:T(8,128)(2,1)S(1)}, u32[]{:S(2)}, u32[]{:S(2)}) collective-permute-start(bf16[128,4096]{1,0:T(8,128)(2,1)S(1)} %collective-permute-done.11.refs_1_), channel_id=1, source_target_pairs={{0,4},{1,13},{2,6},{3,15},{4,8},{5,1},{6,10},{7,3},{8,12},{9,5},{1... | collective-permute-start | bytes 3145736 | tf_op jit(solution)/shard_map/ppermute | solution.py:40
  98.8 16.0 %collective-permute-start.20 = (bf16[128,4096]{1,0:T(8,128)(2,1)S(1)}, bf16[128,4096]{1,0:T(8,128)(2,1)S(1)}, u32[]{:S(2)}, u32[]{:S(2)}) collective-permute-start(bf16[128,4096]{1,0:T(8,128)(2,1)S(1)} %collective-permute-done.12.refs_4_), channel_id=1, source_target_pairs={{0,16},{1,49},{2,18},{3,51},{4,20},{5,53},{6,22},{7,55},{8,24},{9,... | collective-permute-start | bytes 3145736 | tf_op jit(solution)/shard_map/ppermute | solution.py:40
  99.2 26.4 %collective-permute-start.22 = (bf16[128,4096]{1,0:T(8,128)(2,1)S(1)}, bf16[128,4096]{1,0:T(8,128)(2,1)S(1)}, u32[]{:S(2)}, u32[]{:S(2)}) collective-permute-start(bf16[128,4096]{1,0:T(8,128)(2,1)S(1)} %shard_map.57.refs_4_), channel_id=1, source_target_pairs={{0,64},{1,65},{2,66},{3,67},{4,68},{5,69},{6,70},{7,71},{8,72},{9,... | collective-permute-start | bytes 3145736 | tf_op jit(solution)/shard_map/ppermute | solution.py:40
  109.5 16.1 %collective-permute-start.21 = (bf16[128,4096]{1,0:T(8,128)(2,1)S(1)}, bf16[128,4096]{1,0:T(8,128)(2,1)S(1)}, u32[]{:S(2)}, u32[]{:S(2)}) collective-permute-start(bf16[128,4096]{1,0:T(8,128)(2,1)S(1)} %collective-permute-done.12.refs_4_), channel_id=1, source_target_pairs={{0,48},{1,17},{2,50},{3,19},{4,52},{5,21},{6,54},{7,23},{8,56},{9,... | collective-permute-start | bytes 3145736 | tf_op jit(solution)/shard_map/ppermute | solution.py:40
  113.9 5.6 %collective-permute-start.18 = (bf16[64,4096]{1,0:T(8,128)(2,1)S(1)}, bf16[64,4096]{1,0:T(8,128)(2,1)S(1)}, u32[]{:S(2)}, u32[]{:S(2)}) collective-permute-start(bf16[64,4096]{1,0:T(8,128)(2,1)S(1)} %get-tuple-element.110), channel_id=1, source_target_pairs={{0,1},{1,0},{2,3},{3,2},{4,5},{5,4},{6,7},{7,6},{8,9},{9,8},{10,11... | collective-permute-start | bytes 1572872 | tf_op jit(solution)/shard_map/ppermute | solution.py:40
  114.0 5.6 %collective-permute-start.19 = (bf16[64,4096]{1,0:T(8,128)(2,1)S(1)}, bf16[64,4096]{1,0:T(8,128)(2,1)S(1)}, u32[]{:S(2)}, u32[]{:S(2)}) collective-permute-start(bf16[64,4096]{1,0:T(8,128)(2,1)S(1)} %get-tuple-element.111), channel_id=1, source_target_pairs={{0,1},{1,0},{2,3},{3,2},{4,5},{5,4},{6,7},{7,6},{8,9},{9,8},{10,11... | collective-permute-start | bytes 1572872 | tf_op jit(solution)/shard_map/ppermute | solution.py:40
  132.8 2.0 %collective-permute-start.23 = (f32[16,128]{1,0:T(8,128)S(1)}, f32[16,128]{1,0:T(8,128)S(1)}, u32[]{:S(2)}, u32[]{:S(2)}) collective-permute-start(f32[16,128]{1,0:T(8,128)S(1)} %get-tuple-element.128), channel_id=1, source_target_pairs={{0,1},{1,0},{2,3},{3,2},{4,5},{5,4},{6,7},{7,6},{8,9},{9,8},{10,11... | collective-permute-start | bytes 24584 | tf_op jit(solution)/shard_map/ppermute | solution.py:40
  134.8 5.5 %collective-permute-start.26 = (f32[16,128]{1,0:T(8,128)S(1)}, f32[16,128]{1,0:T(8,128)S(1)}, u32[]{:S(2)}, u32[]{:S(2)}) collective-permute-start(f32[16,128]{1,0:T(8,128)S(1)} %max.15), channel_id=1, source_target_pairs={{0,6},{1,7},{2,4},{3,5},{4,2},{5,3},{6,0},{7,1},{8,14},{9,15},{10,... | collective-permute-start | bytes 24584 | tf_op jit(solution)/shard_map/ppermute | solution.py:40
  135.5 4.9 %collective-permute-start.25 = (f32[16,128]{1,0:T(8,128)S(1)}, f32[16,128]{1,0:T(8,128)S(1)}, u32[]{:S(2)}, u32[]{:S(2)}) collective-permute-start(f32[16,128]{1,0:T(8,128)S(1)} %max.15), channel_id=1, source_target_pairs={{0,4},{1,5},{2,6},{3,7},{4,0},{5,1},{6,2},{7,3},{8,12},{9,13},{10,... | collective-permute-start | bytes 24584 | tf_op jit(solution)/shard_map/ppermute | solution.py:40
  137.0 3.7 %collective-permute-start.24 = (f32[16,128]{1,0:T(8,128)S(1)}, f32[16,128]{1,0:T(8,128)S(1)}, u32[]{:S(2)}, u32[]{:S(2)}) collective-permute-start(f32[16,128]{1,0:T(8,128)S(1)} %max.15), channel_id=1, source_target_pairs={{0,2},{1,3},{2,0},{3,1},{4,6},{5,7},{6,4},{7,5},{8,10},{9,11},{10,... | collective-permute-start | bytes 24584 | tf_op jit(solution)/shard_map/ppermute | solution.py:40
  140.6 6.4 %collective-permute-start.27 = (f32[16,128]{1,0:T(8,128)S(1)}, f32[16,128]{1,0:T(8,128)S(1)}, u32[]{:S(2)}, u32[]{:S(2)}) collective-permute-start(f32[16,128]{1,0:T(8,128)S(1)} %maximum_maximum_fusion), channel_id=1, source_target_pairs={{0,12},{1,13},{2,14},{3,15},{4,8},{5,9},{6,10},{7,11},{8,4},{9,5},... | collective-permute-start | bytes 24584 | tf_op jit(solution)/shard_map/ppermute | solution.py:40
